TPU v7x, 128 devices: a whole 4x4x4 slice. The times are simulated.
128 devices in a mesh: ctx: 16 (over x, z_hi, core), head: 8 (over z_lo, y).
Axes of the slice: x: 4, y: 4, z: 4 (z_hi: 2, z_lo: 2; z = z_hi * 2 + z_lo), core: 2. Of those that a mesh axis runs over, the one named last changes fastest.
Arguments:
- prefill_query: bfloat16 [4096, 8192], P('ctx', 'head'), may hold values from -96 to 96
- prefill_key: bfloat16 [4096, 1024], P('ctx', 'head'), may hold values from -4 to 4
- prefill_value: bfloat16 [4096, 1024], P('ctx', 'head'), may hold values from -5 to 5
- tree_mask: int32 [64, 64], replicated, may hold values from 0 to 1, as said below
- pages: int32 [256, 8], replicated, may hold values from 0 to 63, as said below
- cache_len: int32 [256], replicated, may hold values from 256 to 512, as said below
- dec_in: bfloat16 [4, 256, 8192], P(None, None, 'ctx'), may hold values from -4 to 4
- norm_gain: bfloat16 [8192], P('ctx'), may hold values from 0.25 to 1.75
- w_query: bfloat16 [8192, 8192], P('ctx', 'head'), may hold values from -1 to 1
- w_keyval: bfloat16 [8192, 2, 1024], P('ctx', None, 'head'), may hold values from -0.0625 to 0.0625
- w_out: bfloat16 [8192, 8192], P('head', 'ctx'), may hold values from -0.125 to 0.125
Outputs:
- prefill_out: bfloat16 [4096, 8192], P('ctx', 'head')
- dec_out: bfloat16 [4, 256, 8192], P(None, None, 'ctx')
Inputs may be any that keep to these rules, and one draw needn't show every extreme that they name: `tree_mask`: entry [a, b] is 1 exactly when node b is node a or an ancestor of a in the prompt tree, where every node but node 0 has one earlier node as parent. Page k holds prompt positions k * 64 to (k + 1) * 64 - 1; each row names 8 distinct pages; the 128 entries of each aligned block of 16 rows name exactly 2 distinct pages among pages k * 4 to (k + 1) * 4 - 1, for every k, each such page named equally often. `cache_len`: some row reads all 512 cached positions.
All inputs are finite; a program needn't handle non-finite values.
Results may differ from a plain program's by a relative error of at most 0.034.
Values may be sent and summed in bfloat16 or wider, within the bound.
A program may use at most 64 MiB of HBM per device.

v0:
```python
import jax
import jax.numpy as jnp
from jax import lax
from jax.sharding import PartitionSpec as P

D = 8192
HD = 128
PAGE = 64
P_SIZE = 8
STEPS = 4


def per_device(
    prefill_query,
    prefill_key,
    prefill_value,
    tree_mask,
    pages,
    cache_len,
    dec_in,
    norm_gain,
    w_query,
    w_keyval,
    w_out,
):
    tok, qcols = prefill_query.shape
    kvcols = prefill_key.shape[1]
    kv_here = kvcols // HD
    heads_here = qcols // HD
    group = heads_here // kv_here
    nctx = lax.axis_size("ctx")
    my_ctx = lax.axis_index("ctx")
    per_dev = tok // PAGE
    scale = HD ** (-0.5)
    width = 2 * kvcols
    paired = jnp.stack([prefill_key, prefill_value], axis=1).reshape(tok, width)
    queries = prefill_query.reshape(tok, kv_here, group, HD)
    qpos = my_ctx * tok + jnp.arange(tok, dtype=jnp.int32)
    qnode = my_ctx * per_dev
    start_state = (
        jnp.full((kv_here, group, tok), -1e30, jnp.float32),
        jnp.zeros((kv_here, group, tok), jnp.float32),
        jnp.zeros((kv_here, group, tok, HD), jnp.float32),
    )
    fold_piece = lax.all_gather(paired, "ctx", axis=0, tiled=True)
    rows = fold_piece.shape[0]
    block = min(rows, 512)
    count = rows // block
    nodes_blk = block // PAGE

    def one_block(index, state):
        kstart = index * block
        section = lax.dynamic_slice_in_dim(fold_piece, index * block, block, 0).reshape(
            block, 2, kv_here, HD
        )
        marks = lax.dynamic_slice(tree_mask, (qnode, kstart // PAGE), (per_dev, nodes_blk))
        peak, total, summed = state
        scores = (
            jnp.einsum("tkgd,skd->kgts", queries, section[:, 0], preferred_element_type=jnp.float32)
            * scale
        )
        wide = jnp.broadcast_to(marks[:, None, :, None], (per_dev, PAGE, nodes_blk, PAGE)).reshape(
            tok, block
        )
        kpos = kstart + jnp.arange(block, dtype=jnp.int32)
        allowed = (wide > 0) & (qpos[:, None] >= kpos[None, :])
        scores = jnp.where(allowed, scores, -1e30)
        new_peak = jnp.maximum(peak, jnp.max(scores, axis=-1))
        weights = jnp.where(allowed, jnp.exp(scores - new_peak[..., None]), 0.0)
        factor = jnp.exp(peak - new_peak)
        total = total * factor + jnp.sum(weights, axis=-1)
        rounded = weights.astype(jnp.bfloat16)
        summed = summed * factor[..., None] + jnp.einsum(
            "kgts,skd->kgtd", rounded, section[:, 1], preferred_element_type=jnp.float32
        )
        return (new_peak, total, summed)

    state = lax.fori_loop(0, count, one_block, (start_state[0], start_state[1], start_state[2]))
    total = state[1]
    summed = state[2]
    prefill_out = (
        (summed / total[..., None]).transpose(2, 0, 1, 3).reshape(tok, qcols).astype(jnp.bfloat16)
    )
    rows_all = dec_in.shape[1]
    grp_rows = rows_all // nctx
    all_pages = per_dev * nctx
    own_pages = lax.dynamic_slice_in_dim(pages, my_ctx * grp_rows, grp_rows, 0)
    whole = lax.all_gather(paired, "ctx", axis=0, tiled=True)
    cache = whole.reshape(all_pages, PAGE * width)[own_pages]
    cache = cache.reshape(grp_rows, P_SIZE * PAGE, 2, kv_here, HD)
    cache_keys = cache[:, :, 0]
    cache_values = cache[:, :, 1]
    own_len = lax.dynamic_slice_in_dim(cache_len, my_ctx * grp_rows, grp_rows, 0)
    live = jnp.arange(P_SIZE * PAGE, dtype=jnp.int32)[None, :] < own_len[:, None]
    gain = norm_gain.astype(jnp.float32)
    w_joined = jnp.concatenate([w_query, w_keyval.reshape(w_keyval.shape[0], width)], axis=1)
    new_keys = jnp.zeros((grp_rows, STEPS, kv_here, HD), jnp.bfloat16)
    new_values = jnp.zeros((grp_rows, STEPS, kv_here, HD), jnp.bfloat16)
    outputs = []
    for step in range(STEPS):
        hidden = dec_in[step].astype(jnp.float32)
        partial_sq = jnp.sum(hidden * hidden, axis=1)
        scaled = (hidden * gain).astype(jnp.bfloat16)
        all_sq = lax.psum(partial_sq, "ctx")
        own_sq = lax.dynamic_slice_in_dim(all_sq, my_ctx * grp_rows, grp_rows, 0)
        projected = lax.psum_scatter(
            jnp.dot(scaled, w_joined, preferred_element_type=jnp.float32).astype(jnp.bfloat16),
            "ctx",
            scatter_dimension=0,
            tiled=True,
        ).astype(jnp.float32)
        inverse = lax.rsqrt(own_sq / D + 1e-05)
        projected = projected * inverse[:, None]
        query_now = projected[:, :qcols].astype(jnp.bfloat16).reshape(grp_rows, kv_here, group, HD)
        keyval_now = projected[:, qcols:].astype(jnp.bfloat16).reshape(grp_rows, 2, kv_here, HD)
        new_keys = new_keys.at[:, step].set(keyval_now[:, 0])
        new_values = new_values.at[:, step].set(keyval_now[:, 1])
        score_cache = (
            jnp.einsum("rkgd,rskd->rkgs", query_now, cache_keys, preferred_element_type=jnp.float32)
            * scale
        )
        score_cache = jnp.where(live[:, None, None, :], score_cache, -1e30)
        score_new = (
            jnp.einsum("rkgd,rskd->rkgs", query_now, new_keys, preferred_element_type=jnp.float32)
            * scale
        )
        score_new = jnp.where((jnp.arange(STEPS) <= step)[None, None, None, :], score_new, -1e30)
        scores = jnp.concatenate([score_cache, score_new], axis=-1)
        top = jnp.max(scores, axis=-1, keepdims=True)
        weights = jnp.exp(scores - top)
        total_now = jnp.sum(weights, axis=-1, keepdims=True)
        rounded = weights.astype(jnp.bfloat16)
        mixed = jnp.einsum(
            "rkgs,rskd->rkgd",
            rounded[..., : P_SIZE * PAGE],
            cache_values,
            preferred_element_type=jnp.float32,
        )
        mixed = mixed + jnp.einsum(
            "rkgs,rskd->rkgd",
            rounded[..., P_SIZE * PAGE :],
            new_values,
            preferred_element_type=jnp.float32,
        )
        head_out = (mixed / total_now).reshape(grp_rows, qcols).astype(jnp.bfloat16)
        spread = jnp.dot(
            lax.all_gather(head_out, "ctx", axis=0, tiled=True),
            w_out,
            preferred_element_type=jnp.float32,
        )
        added = lax.psum(spread.astype(jnp.bfloat16), "head").astype(jnp.float32)
        outputs.append((hidden + added).astype(jnp.bfloat16))
    return (prefill_out, jnp.stack(outputs))


def solution(mesh):
    return jax.shard_map(
        per_device,
        mesh=mesh,
        in_specs=(
            P("ctx", "head"),
            P("ctx", "head"),
            P("ctx", "head"),
            P(),
            P(),
            P(),
            P(None, None, "ctx"),
            P("ctx"),
            P("ctx", "head"),
            P("ctx", None, "head"),
            P("head", "ctx"),
        ),
        out_specs=(P("ctx", "head"), P(None, None, "ctx")),
        check_vma=False,
    )
```

profile of v0, /device:TPU:0, one launch (start us, length us, event | category | flops | bytes accessed | tf_op | source)
XLA Modules:
  0.0 570.9 jit_solution(2314054572967214845)
XLA Ops:
  17.4 38.8 %all-reduce.2 = (f32[256]{0:T(256)S(1)}, f32[256]{0:T(256)S(1)}, f32[256]{0:T(256)S(1)}, f32[256]{0:T(256)S(1)}) all-reduce(f32[256]{0:T(256)S(1)} %get-tuple-element.389, f32[256]{0:T(256)S(1)} %get-tuple-element.387, f32[256]{0:T(256)S(1)} %get-tuple-element.388, ...), channel_id=1, replica_groups=mesh['ctx'=16,'head'=8] {'ctx'}, use_global_device_ids=true, to_apply=%region_27.28 | all-reduce | flops 1024 | bytes 8192 | tf_op jit(solution)/shard_map/psum | solution.py:104
  56.6 23.3 %reduce-scatter.7.cloned.1.call-done = bf16[16,1280]{1,0:T(8,128)(2,1)} async-done(((bf16[256,1280]{1,0:T(8,128)(2,1)}), bf16[16,1280]{1,0:T(8,128)(2,1)}) %reduce-scatter.7.cloned.1.call-update) | async-done | bytes 40976 | tf_op jit(solution)/shard_map/reduce_scatter | solution.py:106
  80.8 68.0 %reduce-scatter.5.cloned.1.call-done = bf16[16,1280]{1,0:T(8,128)(2,1)} async-done(((bf16[256,1280]{1,0:T(8,128)(2,1)}), bf16[16,1280]{1,0:T(8,128)(2,1)}) %reduce-scatter.5.cloned.1.call-update) | async-done | bytes 40976 | tf_op jit(solution)/shard_map/reduce_scatter | solution.py:106
  149.7 67.6 %reduce-scatter.9.cloned.1.call-done = bf16[16,1280]{1,0:T(8,128)(2,1)} async-done(((bf16[256,1280]{1,0:T(8,128)(2,1)}), bf16[16,1280]{1,0:T(8,128)(2,1)}) %reduce-scatter.9.cloned.1.call-update) | async-done | bytes 40976 | tf_op jit(solution)/shard_map/reduce_scatter | solution.py:106
  218.2 67.9 %reduce-scatter.11.cloned.1.call-done = bf16[16,1280]{1,0:T(8,128)(2,1)} async-done(((bf16[256,1280]{1,0:T(8,128)(2,1)}), bf16[16,1280]{1,0:T(8,128)(2,1)}) %reduce-scatter.11.cloned.1.call-update) | async-done | bytes 40976 | tf_op jit(solution)/shard_map/reduce_scatter | solution.py:106
  292.9 44.1 %all-gather.2.cloned.1.call-done = bf16[4096,256]{0,1:T(8,128)(2,1)} async-done(((bf16[256,256]{0,1:T(8,128)(2,1)}), bf16[4096,256]{0,1:T(8,128)(2,1)}) %all-gather.2.cloned.1.call-update) | async-done | bytes 2097168 | tf_op jit(solution)/shard_map/all_gather | solution.py:45
  336.9 4.1 copy.63
  341.0 2.9 reshape.906
  343.9 5.1 gather_fusion
  349.0 7.7 %reshape.907 = bf16[16,512,2,1,128]{4,2,1,0,3:T(2,128)(2,1)} reshape(bf16[128,16384]{1,0:T(8,128)(2,1)} %gather_fusion) | data formatting | bytes 8388608 | tf_op jit(solution)/shard_map/reshape | solution.py:90
  356.7 8.9 %fusion.88 = (bf16[16,512,1,1,128]{4,2,1,0,3:T(2,128)(2,1)S(1)}, bf16[16,512,1,1,128]{4,2,1,0,3:T(2,128)(2,1)S(1)}) fusion(bf16[16,512,2,1,128]{4,2,1,0,3:T(2,128)(2,1)} %reshape.907), kind=kLoop, calls=%fused_computation.176 | loop fusion | bytes 8388608 | tf_op jit(solution)/shard_map/slice | solution.py:91
  376.6 22.6 %all_gather.20 = bf16[256,1024]{1,0:T(8,128)(2,1)S(1)} all-gather(bf16[16,1024]{1,0:T(8,128)(2,1)S(1)} %bitcast.284), channel_id=1, replica_groups=mesh['ctx'=16,'head'=8] {'ctx'}, dimensions={0}, use_global_device_ids=true | all-gather | bytes 557056 | tf_op jit(solution)/shard_map/all_gather | solution.py:147
  400.0 21.9 %all_gather.19 = bf16[256,1024]{1,0:T(8,128)(2,1)S(1)} all-gather(bf16[16,1024]{1,0:T(8,128)(2,1)S(1)} %bitcast.285), channel_id=1, replica_groups=mesh['ctx'=16,'head'=8] {'ctx'}, dimensions={0}, use_global_device_ids=true | all-gather | bytes 557056 | tf_op jit(solution)/shard_map/all_gather | solution.py:147
  424.2 22.3 %all_gather.18 = bf16[256,1024]{1,0:T(8,128)(2,1)S(1)} all-gather(bf16[16,1024]{1,0:T(8,128)(2,1)S(1)} %bitcast.286), channel_id=1, replica_groups=mesh['ctx'=16,'head'=8] {'ctx'}, dimensions={0}, use_global_device_ids=true | all-gather | bytes 557056 | tf_op jit(solution)/shard_map/all_gather | solution.py:147
  448.5 22.1 %all_gather.17 = bf16[256,1024]{1,0:T(8,128)(2,1)S(1)} all-gather(bf16[16,1024]{1,0:T(8,128)(2,1)S(1)} %bitcast.287), channel_id=1, replica_groups=mesh['ctx'=16,'head'=8] {'ctx'}, dimensions={0}, use_global_device_ids=true | all-gather | bytes 557056 | tf_op jit(solution)/shard_map/all_gather | solution.py:147
  471.8 88.0 %while.28 = (s32[]{:T(128)}, f32[1,8,256]{2,1,0:T(8,128)S(1)}, f32[1,8,256]{2,1,0:T(8,128)S(1)}, f32[1,8,256,128]{3,2,1,0:T(8,128)S(1)}, s32[64,64]{1,0:T(8,128)...) while((s32[]{:T(128)}, f32[1,8,256]{2,1,0:T(8,128)S(1)}, ...), condition=%wide.region_3.4_spmd.clone, body=%wide.region_0.3_spmd.clone.sunk | while | flops 551564096 | bytes 33954936 | solution.py:78
  474.6 2.8 fusion.138
  477.4 3.4 fusion.140
  485.7 2.8 fusion.138
  488.5 3.3 fusion.140
  496.7 2.8 fusion.138
  499.4 3.4 fusion.140
  507.7 2.8 fusion.138
  510.5 3.3 fusion.140
  518.7 2.8 fusion.138
  521.4 3.3 fusion.140
  529.7 2.8 fusion.138
  532.5 3.4 fusion.140
  540.7 2.8 fusion.138
  543.5 3.3 fusion.140
  551.7 2.8 fusion.138
  554.4 3.3 fusion.140
  (283 shorter events, 79.1 us)
Async XLA Ops:
  7.2 414.8 %copy-start = (bf16[1024,512]{1,0:T(8,128)(2,1)S(1)}, bf16[1024,512]{1,0:T(8,128)(2,1)}, u32[]{:S(2)}) copy-start(bf16[1024,512]{1,0:T(8,128)(2,1)} %param.39) | copy-start | bytes 3145732
  7.2 1.7 copy-start.3
  7.2 72.7 %reduce-scatter.7.cloned.1.call-start = ((), (), s32[]{:S(2)}) async-start(), calls=%async_computation.6 | async-start | bytes 696320 | tf_op jit(solution)/shard_map/reduce_scatter | solution.py:106
  10.3 138.5 %reduce-scatter.5.cloned.1.call-start = ((), (), s32[]{:S(2)}) async-start(), calls=%async_computation.5 | async-start | bytes 696320 | tf_op jit(solution)/shard_map/reduce_scatter | solution.py:106
  11.7 205.6 %reduce-scatter.9.cloned.1.call-start = ((), (), s32[]{:S(2)}) async-start(), calls=%async_computation.7 | async-start | bytes 696320 | tf_op jit(solution)/shard_map/reduce_scatter | solution.py:106
  13.1 1.5 copy-start.13
  13.1 1.5 copy-start.14
  13.2 272.9 %reduce-scatter.11.cloned.1.call-start = ((), (), s32[]{:S(2)}) async-start(), calls=%async_computation.8 | async-start | bytes 696320 | tf_op jit(solution)/shard_map/reduce_scatter | solution.py:106
  14.6 2.6 copy-start.24
  14.6 41.7 %copy-start.26 = (s32[256]{0:T(256)S(1)}, s32[256]{0:T(256)}, u32[]{:S(2)}) copy-start(s32[256]{0:T(256)} %param.34) | copy-start | bytes 3076
  14.6 322.3 %all-gather.2.cloned.1.call-start = ((), (), s32[]{:S(2)}) async-start(), calls=%async_computation.4 | async-start | bytes 2228224 | tf_op jit(solution)/shard_map/all_gather | solution.py:45
  15.5 546.0 %all-reduce.6.cloned.1.call-start = ((), (), s32[]{:S(2)}) async-start(), calls=%async_computation.9 | async-start | bytes 2097152 | tf_op jit(solution)/shard_map/psum | solution.py:151
  287.8 3.5 copy-start.22
  369.5 2.2 copy-start.20
  369.5 2.2 copy-start.11
  370.7 2.2 copy-start.6
  370.7 2.2 copy-start.23
  371.7 3.8 copy-start.16
  371.9 1.8 copy-start.7
  400.0 24.2 %copy-start.15 = (bf16[16,8,128]{2,1,0:T(8,128)(2,1)S(1)}, bf16[16,8,128]{2,1,0:T(8,128)(2,1)}, u32[]{:S(2)}) copy-start(bf16[16,8,128]{2,1,0:T(8,128)(2,1)} %fusion.34) | copy-start | bytes 98308
  446.6 1.8 copy-start.18
  448.3 23.5 %copy-start.2 = (bf16[256,1,8,128]{3,0,2,1:T(8,128)(2,1)S(1)}, bf16[256,1,8,128]{3,0,2,1:T(8,128)(2,1)}, u32[]{:S(2)}) copy-start(bf16[256,1,8,128]{3,0,2,1:T(8,128)(2,1)} %copy.61) | copy-start | bytes 1572868
  448.3 23.5 %copy-start.5 = (f32[1,8,256,128]{3,2,1,0:T(8,128)S(1)}, f32[1,8,256,128]{3,2,1,0:T(8,128)}, u32[]{:S(2)}) copy-start(f32[1,8,256,128]{3,2,1,0:T(8,128)} %custom-call.2) | copy-start | bytes 3145732
  477.4 3.6 copy-start.1
  488.5 3.5 copy-start.1
  499.4 3.5 copy-start.1
  510.5 3.5 copy-start.1
  521.4 3.5 copy-start.1
  532.4 3.5 copy-start.1
  543.5 3.5 copy-start.1
  554.4 3.5 copy-start.1
  559.9 1.6 copy-start.4
  (8 other events, 10.7 us)
Sparse Core Ops, SparseCore 0:
  11.8 68.1 reduce-scatter.6
  84.1 64.6 reduce-scatter.4
  152.6 64.6 reduce-scatter.8
  221.4 64.6 reduce-scatter.10
  288.2 48.6 all-gather.1
  471.9 75.7 all-reduce.5
where the time goes:
time: 574 us; the launch traced here: 571 us
  waiting for transfers between devices  271 us (47%)
  blocking collectives  128 us (22%)
  matrix products  61.6 us (11%)
  local copies, waits for them, and re-layouts  57.8 us (10%)
  other arithmetic  37 us (6%)
  between operations  14.6 us (3%)
    reduce_scatter x4, waiting for transfers between devices, per_device(): lax.psum_scatter(jnp.dot(scaled, w_joined, preferred_element_type=jnp.flo...  227 us
    all_gather x4, blocking collectives, per_device(): lax.all_gather(head_out, 'ctx', axis=0, tiled=True)  89 us
    all_gather x1, waiting for transfers between devices, per_device(): fold_piece = lax.all_gather(paired, 'ctx', axis=0, tiled=True)  44.1 us
    psum x1, blocking collectives, per_device(): all_sq = lax.psum(partial_sq, 'ctx')  38.8 us
    reduce_sum x8, other arithmetic, one_block(): total = total * factor + jnp.sum(weights, axis=-1)  26.8 us
    dot_general x8, matrix products, one_block(): jnp.einsum('tkgd,skd->kgts', queries, section[:, 0], preferred_element_ty...  22.1 us
    dot_general x8, matrix products, one_block(): jnp.einsum('kgts,skd->kgtd', rounded, section[:, 1], preferred_element_ty...  15.9 us
  transfers between devices with their start and end apart: 6, of which 5 were waited for; matrix products, arithmetic and copies ran while one was open for 18% of the time, Pallas kernels for 0%

commit v1 on v0

v1 whole, which is shorter than its diff:
```python
import jax
import jax.numpy as jnp
from jax import lax
from jax.experimental import pallas as pl
from jax.experimental.pallas import tpu as pltpu
from jax.sharding import PartitionSpec as P

D = 8192
HD = 128
PAGE = 64
STEPS = 4
SCALE = HD ** (-0.5)
NEG = -1e30
F32 = jnp.float32
BF16 = jnp.bfloat16
MESH = pl.DeviceIdType.MESH

NCH = 2
TS = STEPS // NCH
RB = 16 * TS

KV0 = 0
SQ0 = 17
PART0 = 33
M_CORE, M_X, M_Z, M_HO, M_Y, M_ZL, M_FO = 0, 1, 7, 8, 25, 31, 32
PART_MSGS = 41
NMSG = PART0 + NCH * PART_MSGS


def rdot(a, b):
    return lax.dot_general(a, b, (((1,), (1,)), ((), ())), preferred_element_type=F32)


def mdot(a, b):
    return lax.dot_general(a, b, (((1,), (0,)), ((), ())), preferred_element_type=F32)


def layer_kernel(
    q_ref, key_ref, val_ref, mask_ref, pages_ref, clen_ref, x_ref, gain_ref, wq_ref, wkv_ref,
    wo_ref,
    pout, out,
    kv, qb, xb, wb, wkvb, wkvf, wob, xs, sqs, sqr, gs, gr, g, prelay, pleft, pright, zs, zr, rf,
    pr, nk, nv, bias, marks, sb, lsum, acc, psb, plsum, pacc, ho, o, of, orelay, oleft, oright,
    ozs, ozr, lsem, ssem, rsem,
):
    c = lax.axis_index("ctx")
    h = lax.axis_index("head")
    core = lax.rem(c, 2)
    zh = lax.rem(c // 2, 2)
    x = c // 4
    y = lax.rem(h, 4)
    zl = h // 4

    def cidx(xi, zi, ci):
        return xi * 4 + zi * 2 + ci

    def hidx(yi, zi):
        return zi * 4 + yi

    xr, xl, xo = lax.rem(x + 1, 4), lax.rem(x + 3, 4), lax.rem(x + 2, 4)
    yr, yl, yo = lax.rem(y + 1, 4), lax.rem(y + 3, 4), lax.rem(y + 2, 4)
    d_xr = (cidx(xr, zh, core), h)
    d_xl = (cidx(xl, zh, core), h)
    d_z = (cidx(x, 1 - zh, core), h)
    d_c = (cidx(x, zh, 1 - core), h)
    d_yr = (c, hidx(yr, zl))
    d_yl = (c, hidx(yl, zl))
    d_zl = (c, hidx(y, 1 - zl))

    def msg(i, src, dst, dev):
        return pltpu.make_async_remote_copy(
            src_ref=src, dst_ref=dst, send_sem=ssem.at[i], recv_sem=rsem.at[i],
            device_id=dev, device_id_type=MESH,
        )

    loads = [
        pltpu.make_async_copy(key_ref, kv.at[0, c], lsem.at[0]),
        pltpu.make_async_copy(val_ref, kv.at[1, c], lsem.at[1]),
        pltpu.make_async_copy(x_ref, xb, lsem.at[2]),
        pltpu.make_async_copy(wkv_ref, wkvb, lsem.at[3]),
    ]
    for j in range(4):
        loads.append(
            pltpu.make_async_copy(wq_ref.at[:, pl.ds(256 * j, 256)], wb.at[j], lsem.at[4 + j])
        )
    for j in range(2):
        loads.append(
            pltpu.make_async_copy(wo_ref.at[:, pl.ds(256 * j, 256)], wob.at[j], lsem.at[8 + j])
        )
    loads.append(pltpu.make_async_copy(q_ref, qb, lsem.at[10]))
    for copy in loads:
        copy.start()

    barrier = pltpu.get_barrier_semaphore()

    def greet(d, carry):
        pl.semaphore_signal(
            barrier, inc=1, device_id=(lax.rem(c + d, 16), h), device_id_type=MESH
        )
        return carry

    lax.fori_loop(1, 16, greet, 0)
    for dev in (d_yr, d_yl, d_zl):
        pl.semaphore_signal(barrier, inc=1, device_id=dev, device_id_type=MESH)
    pl.semaphore_wait(barrier, 18)

    sent = []

    def send(i, src, dst, dev):
        m = msg(i, src, dst, dev)
        m.start()
        sent.append(m)
        return m

    class Gather:
        def __init__(self, base, blk, half, p, q, right, left, far_p, d_r, d_l, d_q, share):
            self.base, self.blk, self.half, self.p, self.q = base, blk, half, p, q
            self.right, self.left, self.far_p = right, left, far_p
            self.d_r, self.d_l, self.d_q, self.share = d_r, d_l, d_q, share
            self.m = {}

        def put(self, k, ref, dev):
            self.m[k] = send(self.base + k, ref, ref, dev)

        def to_core(self, k, p_, q_):
            if self.share:
                ref = self.blk(p_, q_)
                self.m[9 + k] = send(self.base + 9 + k, ref, ref, d_c)

        def start(self):
            own = self.blk(self.p, self.q)
            self.put(0, own, self.d_q)
            self.put(1, own, self.d_r)
            self.put(2, own, self.d_l)
            self.to_core(0, self.p, self.q)

        def near(self):
            q2 = 1 - self.q
            self.m[0].wait_recv()
            other = self.blk(self.p, q2)
            self.put(3, other, self.d_r)
            self.put(4, other, self.d_l)
            self.to_core(1, self.p, q2)
            self.m[1].wait_recv()
            self.put(5, self.half(self.left, self.q, 0), self.d_r)
            self.to_core(2, self.left, self.q)
            self.m[2].wait_recv()
            self.put(6, self.half(self.right, self.q, 1), self.d_l)
            self.to_core(3, self.right, self.q)

        def far(self):
            q2 = 1 - self.q
            self.m[3].wait_recv()
            self.put(7, self.half(self.left, q2, 0), self.d_r)
            self.to_core(4, self.left, q2)
            self.m[4].wait_recv()
            self.put(8, self.half(self.right, q2, 1), self.d_l)
            self.to_core(5, self.right, q2)

        def last(self):
            q2 = 1 - self.q
            self.m[5].wait_recv()
            self.m[6].wait_recv()
            self.to_core(6, self.far_p, self.q)
            self.m[7].wait_recv()
            self.m[8].wait_recv()
            self.to_core(7, self.far_p, q2)

        def finish(self):
            if self.share:
                for k in range(8):
                    self.m[9 + k].wait_recv()

    kvg = Gather(
        KV0, lambda a, b: kv.at[:, cidx(a, b, core)], lambda a, b, k: kv.at[k, cidx(a, b, core)],
        x, zh, xr, xl, xo, d_xr, d_xl, d_z, True,
    )
    loads[0].wait()
    loads[1].wait()
    kvg.start()

    loads[2].wait()
    row_id = lax.broadcasted_iota(jnp.int32, (64, 128), 0)
    lane_id = lax.broadcasted_iota(jnp.int32, (64, 128), 1)
    eye = row_id == lane_id
    gain4 = gain_ref[...].astype(F32)
    gain = jnp.concatenate([gain4[i : i + 1] for i in range(4)], axis=1)

    def prepare(d, carry):
        raw = xb[:, d].astype(F32).reshape(64, 512)
        scaled = (raw * gain).astype(BF16).reshape(NCH, RB, 512)
        for k in range(NCH):
            xs[k, lax.rem(d, 2), d // 2] = scaled[k]
        part = jnp.sum(raw * raw, axis=1, keepdims=True)
        flat = jnp.sum(jnp.where(eye, part, 0.0), axis=0, keepdims=True)
        sqs[d] = jnp.broadcast_to(flat, (8, 128))
        return carry

    lax.fori_loop(0, 16, prepare, 0)

    def sq_msg(d):
        to = lax.rem(c + d, 16)
        return msg(SQ0 + d, sqs.at[to], sqr.at[c], (to, h))

    loads[3].wait()
    wkvf[...] = wkvb[...].astype(F32)
    wb[4, :, 0:128] = wkvf[pl.ds(0, 512, stride=2), :].astype(BF16)
    wb[4, :, 128:256] = wkvf[pl.ds(1, 512, stride=2), :].astype(BF16)
    for k in range(4, 8):
        loads[k].wait()

    first = pl.ds(0, 5)
    second = pl.ds(5, 5)

    class Part:
        pass

    parts = []
    for k in range(NCH):
        p = Part()
        p.k = k
        p.base = PART0 + k * PART_MSGS
        p.px, p.oy = {}, {}
        p.hog = Gather(
            p.base + M_HO, lambda a, b, k=k: ho.at[k, cidx(a, b, core)],
            lambda a, b, f, k=k: ho.at[k, cidx(a, b, core), f],
            x, zh, xr, xl, xo, d_xr, d_xl, d_z, True,
        )
        steps = pl.ds(k * TS, TS)
        p.fog = Gather(
            p.base + M_FO, lambda a, b, s=steps: out.at[s, 2 * a + b],
            lambda a, b, f, s=steps: out.at[s, 2 * a + b, pl.ds(16 * f, 16)],
            y, zl, yr, yl, yo, d_yr, d_yl, d_zl, False,
        )
        parts.append(p)

    def other_rows(p):
        k = p.k

        def body(j, carry):
            res = mdot(xs[k, 1 - core].reshape(8 * RB, 512), wb[j]).astype(BF16)
            gs[k, 2 * j] = res[:, :128].reshape(4, 2, RB, 128)
            gs[k, 2 * j + 1] = res[:, 128:].reshape(4, 2, RB, 128)
            return carry

        lax.fori_loop(0, 5, body, 0)
        p.core = send(p.base + M_CORE, gs.at[k], gr.at[k], d_c)

    def own_rows(p):
        k, px = p.k, p.px
        p.core.wait_recv()

        def body(j, carry):
            res = mdot(xs[k, core].reshape(8 * RB, 512), wb[j])
            for i in range(2):
                both = res[:, 128 * i : 128 * i + 128].reshape(4, 2, RB, 128) + gr[
                    k, 2 * j + i
                ].astype(F32)
                g[k, 2 * j + i] = both.astype(BF16)
            return carry

        lax.fori_loop(0, 3, body, 0)
        px[0] = send(p.base + M_X + 0, g.at[k, first, xo], prelay.at[k, 0], d_xr)
        px[3] = send(p.base + M_X + 3, g.at[k, first, xl], pright.at[k, 0], d_xl)
        lax.fori_loop(3, 5, body, 0)
        px[2] = send(p.base + M_X + 2, g.at[k, second, xo], prelay.at[k, 1], d_xl)
        px[1] = send(p.base + M_X + 1, g.at[k, second, xr], pleft.at[k, 1], d_xr)

    def x_relay(p):
        k, px = p.k, p.px
        px[0].wait_recv()
        g[k, first, xr] = (g[k, first, xr].astype(F32) + prelay[k, 0].astype(F32)).astype(BF16)
        px[4] = send(p.base + M_X + 4, g.at[k, first, xr], pleft.at[k, 0], d_xr)
        px[2].wait_recv()
        g[k, second, xl] = (g[k, second, xl].astype(F32) + prelay[k, 1].astype(F32)).astype(BF16)
        px[5] = send(p.base + M_X + 5, g.at[k, second, xl], pright.at[k, 1], d_xl)

    def x_sum(p):
        k, px = p.k, p.px
        for i in (1, 3, 4, 5):
            px[i].wait_recv()

        def three(half, s, z):
            return (
                g[k, 5 * half + s, x, z].astype(F32)
                + pleft[k, half, s, z].astype(F32)
                + pright[k, half, s, z].astype(F32)
            )

        def gone(s, carry):
            for half in range(2):
                zs[k, 5 * half + s] = three(half, s, 1 - zh).astype(BF16)
            return carry

        lax.fori_loop(0, 5, gone, 0)
        p.zp = send(p.base + M_Z, zs.at[k], zr.at[k], d_z)

        def kept(s, carry):
            for half in range(2):
                rf[k, 5 * half + s] = three(half, s, zh)
            return carry

        lax.fori_loop(0, 5, kept, 0)

    def attend(p, inverse):
        k = p.k
        nrow = 8 * RB
        nnew = (k + 1) * RB
        inv = inverse[k * RB : (k + 1) * RB]
        p.zp.wait_recv()

        def projected(s, carry):
            pr[k, s] = ((rf[k, s] + zr[k, s].astype(F32)) * inv).astype(BF16)
            return carry

        lax.fori_loop(0, 10, projected, 0)
        nk[k * RB : (k + 1) * RB] = pr[k, 8]
        nv[k * RB : (k + 1) * RB] = pr[k, 9]

        def queries():
            return pr[k, 0:8].reshape(nrow, HD)

        i_id = lax.broadcasted_iota(jnp.int32, (nrow, nnew), 0)
        j_id = lax.broadcasted_iota(jnp.int32, (nrow, nnew), 1)
        seen = (lax.rem(i_id, 16) == lax.rem(j_id, 16)) & (
            j_id // 16 <= k * TS + lax.rem(i_id // 16, TS)
        )
        s_new = jnp.where(seen, rdot(queries(), nk[0:nnew]) * SCALE, NEG)
        lsum[...] = jnp.full((nrow, 128), NEG, F32)

        def score(b, carry):
            s = rdot(queries(), kv[0, b]) * SCALE
            s = (s.reshape(nrow // 16, 16, 256) + bias[b][None]).reshape(nrow, 256)
            sb[b] = s
            lsum[...] = jnp.maximum(lsum[...], jnp.maximum(s[:, :128], s[:, 128:]))
            return carry

        lax.fori_loop(0, 16, score, 0)
        top = jnp.maximum(
            jnp.max(lsum[...], axis=1, keepdims=True), jnp.max(s_new, axis=1, keepdims=True)
        )
        w_new = jnp.exp(s_new - top)
        new_total = jnp.sum(w_new, axis=1, keepdims=True)
        acc[...] = mdot(w_new.astype(BF16), nv[0:nnew])
        lsum[...] = jnp.zeros((nrow, 128), F32)

        def mix(b, carry):
            w = jnp.exp(sb[b] - top)
            lsum[...] += w[:, :128] + w[:, 128:]
            acc[...] += mdot(w.astype(BF16), kv[1, b])
            return carry

        lax.fori_loop(0, 16, mix, 0)
        total = jnp.sum(lsum[...], axis=1, keepdims=True) + new_total
        head_out = (acc[...] / total).astype(BF16)
        for s in range(8):
            ho[k, c, s // 4, :, (s % 4) * HD : (s % 4 + 1) * HD] = head_out[s * RB : (s + 1) * RB]
        p.hog.start()

    def out_rows(p):
        k, oy = p.k, p.oy
        p.hog.finish()
        lhs = [ho[k, :, f].reshape(16 * RB, 512) for f in range(2)]
        for n in range(2):
            res = mdot(lhs[0], wob[n, 0:512]) + mdot(lhs[1], wob[n, 512:1024])
            o[k, :, :, :, n * 256 : (n + 1) * 256] = res.astype(BF16).reshape(4, 2, 2 * RB, 256)
        oy[0] = send(p.base + M_Y + 0, o.at[k, yo, 0], orelay.at[k, 0], d_yr)
        oy[2] = send(p.base + M_Y + 2, o.at[k, yo, 1], orelay.at[k, 1], d_yl)
        oy[1] = send(p.base + M_Y + 1, o.at[k, yr, 1], oleft.at[k, 1], d_yr)
        oy[3] = send(p.base + M_Y + 3, o.at[k, yl, 0], oright.at[k, 0], d_yl)

    def y_relay(p):
        k, oy = p.k, p.oy
        oy[0].wait_recv()
        o[k, yr, 0] = (o[k, yr, 0].astype(F32) + orelay[k, 0].astype(F32)).astype(BF16)
        oy[4] = send(p.base + M_Y + 4, o.at[k, yr, 0], oleft.at[k, 0], d_yr)
        oy[2].wait_recv()
        o[k, yl, 1] = (o[k, yl, 1].astype(F32) + orelay[k, 1].astype(F32)).astype(BF16)
        oy[5] = send(p.base + M_Y + 5, o.at[k, yl, 1], oright.at[k, 1], d_yl)

    def y_sum(p):
        k, oy = p.k, p.oy
        for i in (1, 3, 4, 5):
            oy[i].wait_recv()

        def three(z):
            return (
                o[k, y, z].astype(F32) + oleft[k, z].astype(F32) + oright[k, z].astype(F32)
            )

        ozs[k] = three(1 - zl).astype(BF16)
        p.oz = send(p.base + M_ZL, ozs.at[k], ozr.at[k], d_zl)
        of[k] = three(zl)

    def add_input(p):
        k = p.k
        p.oz.wait_recv()
        steps = pl.ds(k * TS, TS)
        mine = 2 * y + zl
        for i in range(2):
            rows = pl.ds(i * RB, RB)
            full = (of[k, rows] + ozr[k, rows].astype(F32)).reshape(TS, 16, 512)
            hidden = xb[steps, cidx(y, zl, i)].astype(F32)
            out[steps, mine, pl.ds(16 * i, 16), :] = (hidden + full).astype(BF16)
        p.fog.start()

    def prefill_head(s):
        lanes = slice(s * HD, (s + 1) * HD)

        def score_block(b):
            t = rdot(qb[:, lanes], kv[0, b])
            rows = [
                t[64 * n : 64 * n + 64] * SCALE + marks[b, pl.ds(4 * c + n, 1), :]
                for n in range(4)
            ]
            return jnp.concatenate(rows, axis=0)

        q_id = lax.broadcasted_iota(jnp.int32, (256, 256), 0)
        k_id = lax.broadcasted_iota(jnp.int32, (256, 256), 1)
        own = jnp.where(q_id >= k_id, score_block(c), NEG)
        plsum[...] = jnp.maximum(own[:, :128], own[:, 128:])

        def score(b, carry):
            t = score_block(b)
            psb[b] = t
            plsum[...] = jnp.maximum(plsum[...], jnp.maximum(t[:, :128], t[:, 128:]))
            return carry

        lax.fori_loop(0, c, score, 0)
        psb[c] = own
        top = jnp.max(plsum[...], axis=1, keepdims=True)
        plsum[...] = jnp.zeros((256, 128), F32)
        pacc[...] = jnp.zeros((256, HD), F32)

        def mix(b, carry):
            w = jnp.exp(psb[b] - top)
            plsum[...] += w[:, :128] + w[:, 128:]
            pacc[...] += mdot(w.astype(BF16), kv[1, b])
            return carry

        lax.fori_loop(0, c + 1, mix, 0)
        total = jnp.sum(plsum[...], axis=1, keepdims=True)
        pout[:, lanes] = (pacc[...] / total).astype(BF16)

    todo = list(range(8))

    def fill(count=1):
        for _ in range(count):
            if todo:
                prefill_head(todo.pop(0))

    pa, pb = parts
    other_rows(pa)
    other_rows(pb)

    def sq_send(d, carry):
        sq_msg(d).start()
        return carry

    lax.fori_loop(1, 16, sq_send, 0)
    own_rows(pa)
    own_rows(pb)
    kvg.near()
    x_relay(pa)

    pick = (
        lax.broadcasted_iota(jnp.int32, (16, 256), 1)
        == lax.broadcasted_iota(jnp.int32, (16, 256), 0) + 16 * c
    )
    own_pages = rdot(pick.astype(BF16), pages_ref[...].astype(BF16)).astype(jnp.int32)
    r_id = lax.broadcasted_iota(jnp.int32, (16, 256), 0)
    s_id = lax.broadcasted_iota(jnp.int32, (16, 256), 1)
    lens = jnp.zeros((16, 256), jnp.int32)
    for r in range(16):
        lens = jnp.where(r_id == r, clen_ref[c * 16 + r], lens)
    in_page = lax.rem(s_id, PAGE)
    node_marks = mask_ref[...].astype(BF16)
    node_id = lax.broadcasted_iota(jnp.int32, (64, 256), 0)
    node_of = lax.broadcasted_iota(jnp.int32, (64, 256), 1) // PAGE

    def masks(b, carry):
        page = b * 4 + s_id // PAGE
        live = jnp.zeros((16, 256), F32)
        for slot in range(8):
            hit = (own_pages[:, slot : slot + 1] == page) & (in_page + slot * PAGE < lens)
            live = jnp.where(hit, 1.0, live)
        bias[b] = jnp.where(live > 0.0, 0.0, NEG)
        spread = mdot(node_marks, (node_id == node_of + 4 * b).astype(BF16))
        marks[b] = jnp.where(spread > 0.5, 0.0, NEG)
        return carry

    lax.fori_loop(0, 16, masks, 0)

    def sq_wait(d, carry):
        sq_msg(d).wait_recv()
        return carry

    lax.fori_loop(1, 16, sq_wait, 0)
    sqr[c] = sqs[c]
    flat = jnp.sum(sqr[...], axis=0)[0:1, :]
    row_sq = jnp.sum(jnp.where(eye, flat, 0.0), axis=1, keepdims=True)
    inverse = lax.rsqrt(row_sq / D + 1e-05)

    kvg.far()
    x_relay(pb)
    x_sum(pa)
    kvg.last()
    x_sum(pb)
    kvg.finish()
    attend(pa, inverse)
    attend(pb, inverse)
    loads[10].wait()
    fill()
    pa.hog.near()
    fill()
    pb.hog.near()
    pa.hog.far()
    fill()
    pa.hog.last()
    pb.hog.far()
    loads[8].wait()
    loads[9].wait()
    out_rows(pa)
    pb.hog.last()
    fill()
    out_rows(pb)
    y_relay(pa)
    fill()
    y_relay(pb)
    y_sum(pa)
    fill()
    y_sum(pb)
    add_input(pa)
    fill()
    add_input(pb)
    pa.fog.near()
    fill()
    pb.fog.near()
    pa.fog.far()
    pb.fog.far()
    pa.fog.last()
    pb.fog.last()

    for m in sent:
        m.wait_send()

    def sq_done(d, carry):
        sq_msg(d).wait_send()
        return carry

    lax.fori_loop(1, 16, sq_done, 0)


def layer_call(*args):
    hbm = pl.BlockSpec(memory_space=pl.ANY)
    vmem = pl.BlockSpec(memory_space=pltpu.VMEM)
    smem = pl.BlockSpec(memory_space=pltpu.SMEM)
    return pl.pallas_call(
        layer_kernel,
        out_shape=(
            jax.ShapeDtypeStruct((256, 1024), BF16),
            jax.ShapeDtypeStruct((4, 8, 32, 512), BF16),
        ),
        in_specs=[hbm, hbm, hbm, vmem, vmem, smem, hbm, vmem, hbm, hbm, hbm],
        out_specs=(vmem, vmem),
        scratch_shapes=[
            pltpu.VMEM((2, 16, 256, HD), BF16),
            pltpu.VMEM((256, 1024), BF16),
            pltpu.VMEM((4, 16, 16, 512), BF16),
            pltpu.VMEM((5, 512, 256), BF16),
            pltpu.VMEM((1024, 128), BF16),
            pltpu.VMEM((1024, 128), F32),
            pltpu.VMEM((2, 1024, 256), BF16),
            pltpu.VMEM((NCH, 2, 8, RB, 512), BF16),
            pltpu.VMEM((16, 8, 128), F32),
            pltpu.VMEM((16, 8, 128), F32),
            pltpu.VMEM((NCH, 10, 4, 2, RB, 128), BF16),
            pltpu.VMEM((NCH, 10, 4, 2, RB, 128), BF16),
            pltpu.VMEM((NCH, 10, 4, 2, RB, 128), BF16),
            pltpu.VMEM((NCH, 2, 5, 2, RB, 128), BF16),
            pltpu.VMEM((NCH, 2, 5, 2, RB, 128), BF16),
            pltpu.VMEM((NCH, 2, 5, 2, RB, 128), BF16),
            pltpu.VMEM((NCH, 10, RB, 128), BF16),
            pltpu.VMEM((NCH, 10, RB, 128), BF16),
            pltpu.VMEM((NCH, 10, RB, 128), F32),
            pltpu.VMEM((NCH, 10, RB, 128), BF16),
            pltpu.VMEM((64, 128), BF16),
            pltpu.VMEM((64, 128), BF16),
            pltpu.VMEM((16, 16, 256), F32),
            pltpu.VMEM((16, 64, 256), F32),
            pltpu.VMEM((16, 8 * RB, 256), F32),
            pltpu.VMEM((8 * RB, 128), F32),
            pltpu.VMEM((8 * RB, 128), F32),
            pltpu.VMEM((16, 256, 256), F32),
            pltpu.VMEM((256, 128), F32),
            pltpu.VMEM((256, 128), F32),
            pltpu.VMEM((NCH, 16, 2, RB, 512), BF16),
            pltpu.VMEM((NCH, 4, 2, 2 * RB, 512), BF16),
            pltpu.VMEM((NCH, 2 * RB, 512), F32),
            pltpu.VMEM((NCH, 2, 2 * RB, 512), BF16),
            pltpu.VMEM((NCH, 2, 2 * RB, 512), BF16),
            pltpu.VMEM((NCH, 2, 2 * RB, 512), BF16),
            pltpu.VMEM((NCH, 2 * RB, 512), BF16),
            pltpu.VMEM((NCH, 2 * RB, 512), BF16),
            pltpu.SemaphoreType.DMA((11,)),
            pltpu.SemaphoreType.DMA((NMSG,)),
            pltpu.SemaphoreType.DMA((NMSG,)),
        ],
        compiler_params=pltpu.CompilerParams(
            collective_id=0, has_side_effects=True, vmem_limit_bytes=56 * 1024 * 1024
        ),
        name="layer",
    )(*args)


def per_device(
    prefill_query, prefill_key, prefill_value, tree_mask, pages, cache_len,
    dec_in, norm_gain, w_query, w_keyval, w_out,
):
    prefill_out, dec_out = layer_call(
        prefill_query, prefill_key, prefill_value, tree_mask, pages.T, cache_len,
        dec_in.reshape(4, 16, 16, 512), norm_gain.reshape(4, 128), w_query,
        w_keyval.reshape(1024, 128), w_out,
    )
    return prefill_out, dec_out.reshape(4, 256, 512)


def solution(mesh):
    return jax.shard_map(
        per_device,
        mesh=mesh,
        in_specs=(
            P("ctx", "head"), P("ctx", "head"), P("ctx", "head"), P(), P(), P(),
            P(None, None, "ctx"), P("ctx"), P("ctx", "head"), P("ctx", None, "head"),
            P("head", "ctx"),
        ),
        out_specs=(P("ctx", "head"), P(None, None, "ctx")),
        check_vma=False,
    )
```

time: 574 us -> 110 us (0.19)
  the two profiles are of different devices: /device:TPU:0 before, /device:TPU:71 now
where the time goes in v1:
time: 110 us
  Pallas kernels  107 us (97%)
  local copies, waits for them, and re-layouts  2.93 us (3%)
    pallas_call x1, Pallas kernels, layer_call(): pl.pallas_call(layer_kernel, out_shape=(jax.ShapeDtypeStruct((256, 1024),...  107 us
    unnamed x4, local copies, waits for them, and re-layouts  2.93 us

profile of v1, /device:TPU:71, one launch (start us, length us, event | category | flops | bytes accessed | tf_op | source)
XLA Modules:
  0.0 110.1 jit_solution(5665983094023765746)
XLA Ops:
  0.6 106.6 %layer.1 = (bf16[256,1024]{1,0:T(8,128)(2,1)}, bf16[4,8,32,512]{3,2,1,0:T(8,128)(2,1)}) custom-call(bf16[256,1024]{1,0:T(8,128)(2,1)} %q_ref.1, bf16[256,128]{1,0:T(8,128)(2,1)} %key_ref.1, bf16[256,128]{1,0:T(8,128)(2,1)} %val_ref.1, s32[64,64]{1,0:T(8,128)} %mask_ref.1, s32[8,256]{1,0:T(8,128)} %bitcast.8, s32[256]{0:T(256)} %clen_ref.1, ...), custom_call_target="tpu_custom_call" | custom-call | tf_op jit(solution)/shard_map/layer/pallas_call | solution.py:558
  107.2 0.0 copy-start
  107.2 2.0 %copy.15 = bf16[256,1024]{1,0:T(8,128)(2,1)} copy(bf16[256,1024]{1,0:T(8,128)(2,1)} %get-tuple-element.8) | data formatting | bytes 1048576
  109.2 0.0 copy-done
  109.2 1.0 copy.16
Async XLA Ops:
  107.2 2.0 %copy-start = (bf16[4,8,32,512]{3,2,1,0:T(8,128)(2,1)S(1)}, bf16[4,8,32,512]{3,2,1,0:T(8,128)(2,1)}, u32[]{:S(2)}) copy-start(bf16[4,8,32,512]{3,2,1,0:T(8,128)(2,1)} %get-tuple-element.5) | copy-start | bytes 3145732

commit v2 on v1

v2 whole, which is shorter than its diff:
```python
import jax
import jax.numpy as jnp
from jax import lax
from jax.experimental import pallas as pl
from jax.experimental.pallas import tpu as pltpu
from jax.sharding import PartitionSpec as P

D = 8192
HD = 128
PAGE = 64
STEPS = 4
SCALE = HD ** (-0.5)
NEG = -1e30
F32 = jnp.float32
BF16 = jnp.bfloat16
MESH = pl.DeviceIdType.MESH

NCH = 2
TS = STEPS // NCH
RB = 16 * TS

KV0 = 0
SQ0 = 17
PART0 = 33
M_CORE, M_X, M_Z, M_HO, M_Y, M_ZL, M_FO = 0, 1, 7, 8, 25, 31, 32
PART_MSGS = 36
NMSG = PART0 + NCH * PART_MSGS


ORDER = (
    "p0.other", "p1.other", "kv.r1", "kv.r2", "p0.own", "all.sq", "kv.r5", "kv.r0", "p0.xr0",
    "p0.xr2", "p1.own", "all.mask", "kv.r3", "kv.r4", "p1.xr0", "p1.xr2", "p0.xsum", "all.list",
    "kv.r7", "p1.xsum", "kv.fin", "all.take", "p0.att", "p1.att", "p0.h0", "p0.h1", "p0.h2",
    "p1.h1", "p1.h2", "p0.h3", "p0.h4", "p1.h0", "p0.h5", "p1.h5", "p0.h7", "p1.h3", "p1.h4",
    "p0.out", "p1.h7", "p0.yr0", "p0.yr2", "p1.out", "p0.ysum", "p1.yr0", "p1.yr2", "p0.add",
    "p1.ysum", "p1.add", "p0.f1", "p0.f2", "p1.f1", "p1.f2", "p0.f5", "p1.f5",
)


def rdot(a, b):
    return lax.dot_general(a, b, (((1,), (1,)), ((), ())), preferred_element_type=F32)


def mdot(a, b):
    return lax.dot_general(a, b, (((1,), (0,)), ((), ())), preferred_element_type=F32)


def layer_kernel(
    key_ref, val_ref, mask_ref, pages_ref, clen_ref, x_ref, gain_ref, wq_ref, wkv_ref, wo_ref,
    kv_out, picks, out,
    kv, xb, wb, wkvb, wkvf, wob, xs, sqs, sqr, gs, gr, g, prelay, pleft, pright, zs, zr, rf,
    pr, nk, nv, bias, chosen, pool, sb, ho, o, orelay, oleft, oright, ozs, ozr,
    lsem, ssem, rsem,
):
    c = lax.axis_index("ctx")
    h = lax.axis_index("head")
    core = lax.rem(c, 2)
    zh = lax.rem(c // 2, 2)
    x = c // 4
    y = lax.rem(h, 4)
    zl = h // 4

    def cidx(xi, zi, ci):
        return xi * 4 + zi * 2 + ci

    def hidx(yi, zi):
        return zi * 4 + yi

    xr, xl, xo = lax.rem(x + 1, 4), lax.rem(x + 3, 4), lax.rem(x + 2, 4)
    yr, yl, yo = lax.rem(y + 1, 4), lax.rem(y + 3, 4), lax.rem(y + 2, 4)
    d_xr = (cidx(xr, zh, core), h)
    d_xl = (cidx(xl, zh, core), h)
    d_z = (cidx(x, 1 - zh, core), h)
    d_c = (cidx(x, zh, 1 - core), h)
    d_yr = (c, hidx(yr, zl))
    d_yl = (c, hidx(yl, zl))
    d_zl = (c, hidx(y, 1 - zl))

    def msg(i, src, dst, dev):
        return pltpu.make_async_remote_copy(
            src_ref=src, dst_ref=dst, send_sem=ssem.at[i], recv_sem=rsem.at[i],
            device_id=dev, device_id_type=MESH,
        )

    loads = [
        pltpu.make_async_copy(key_ref, kv.at[0, c], lsem.at[0]),
        pltpu.make_async_copy(val_ref, kv.at[1, c], lsem.at[1]),
        pltpu.make_async_copy(x_ref, xb, lsem.at[2]),
        pltpu.make_async_copy(wkv_ref, wkvb, lsem.at[3]),
    ]
    for j in range(4):
        loads.append(
            pltpu.make_async_copy(wq_ref.at[:, pl.ds(256 * j, 256)], wb.at[j], lsem.at[4 + j])
        )
    for j in range(2):
        loads.append(
            pltpu.make_async_copy(wo_ref.at[:, pl.ds(256 * j, 256)], wob.at[j], lsem.at[8 + j])
        )
    for copy in loads:
        copy.start()

    barrier = pltpu.get_barrier_semaphore()

    def greet(d, carry):
        pl.semaphore_signal(
            barrier, inc=1, device_id=(lax.rem(c + d, 16), h), device_id_type=MESH
        )
        return carry

    lax.fori_loop(1, 16, greet, 0)
    for dev in (d_yr, d_yl, d_zl):
        pl.semaphore_signal(barrier, inc=1, device_id=dev, device_id_type=MESH)
    pl.semaphore_wait(barrier, 18)

    sent = []

    def send(i, src, dst, dev):
        m = msg(i, src, dst, dev)
        m.start()
        sent.append(m)
        return m

    class Gather:
        def __init__(self, base, blk, half):
            self.base, self.blk, self.half = base, blk, half
            self.m = {}

        def put(self, k, ref, dev):
            self.m[k] = send(self.base + k, ref, ref, dev)

        def share(self, k, xi, zi):
            ref = self.blk(xi, zi)
            self.m[9 + k] = send(self.base + 9 + k, ref, ref, d_c)

        def start(self):
            own = self.blk(x, zh)
            self.put(0, own, d_z)
            self.put(1, own, d_xr)
            self.put(2, own, d_xl)
            self.share(0, x, zh)

        def take(self, k):
            z2 = 1 - zh
            self.m[k].wait_recv()
            if k == 0:
                other = self.blk(x, z2)
                self.put(3, other, d_xr)
                self.put(4, other, d_xl)
                self.share(1, x, z2)
            elif k == 1:
                self.put(5, self.half(xl, zh, 0), d_xr)
                self.share(2, xl, zh)
            elif k == 2:
                self.put(6, self.half(xr, zh, 1), d_xl)
                self.share(3, xr, zh)
            elif k == 3:
                self.put(7, self.half(xl, z2, 0), d_xr)
                self.share(4, xl, z2)
            elif k == 4:
                self.put(8, self.half(xr, z2, 1), d_xl)
                self.share(5, xr, z2)
            elif k == 5:
                self.m[6].wait_recv()
                self.share(6, xo, zh)
            else:
                self.m[8].wait_recv()
                self.share(7, xo, z2)

        def finish(self):
            for k in range(8):
                self.m[9 + k].wait_recv()

    kvg = Gather(
        KV0, lambda a, b: kv.at[:, cidx(a, b, core)], lambda a, b, k: kv.at[k, cidx(a, b, core)]
    )
    loads[0].wait()
    loads[1].wait()
    kvg.start()

    loads[2].wait()
    row_id = lax.broadcasted_iota(jnp.int32, (64, 128), 0)
    lane_id = lax.broadcasted_iota(jnp.int32, (64, 128), 1)
    eye = row_id == lane_id
    gain4 = gain_ref[...].astype(F32)
    gain = jnp.concatenate([gain4[i : i + 1] for i in range(4)], axis=1)

    def scale_rows(p, side):
        steps = pl.ds(p.k * TS, TS)

        def body(i, carry):
            raw = xb[steps, 2 * i + side].astype(F32).reshape(RB, 512)
            xs[p.k, side, i] = (raw * gain).astype(BF16)
            return carry

        lax.fori_loop(0, 8, body, 0, unroll=True)

    def squares(d, carry):
        raw = xb[:, d].astype(F32).reshape(64, 512)
        part = jnp.sum(raw * raw, axis=1, keepdims=True)
        flat = jnp.sum(jnp.where(eye, part, 0.0), axis=0, keepdims=True)
        sqs[d] = jnp.broadcast_to(flat, (8, 128))
        return carry

    def sq_msg(d):
        to = lax.rem(c + d, 16)
        return msg(SQ0 + d, sqs.at[to], sqr.at[c], (to, h))

    first = pl.ds(0, 5)
    second = pl.ds(5, 5)

    class Part:
        pass

    parts = []
    for k in range(NCH):
        p = Part()
        p.k = k
        p.base = PART0 + k * PART_MSGS
        p.px, p.oy = {}, {}
        p.hog = Gather(
            p.base + M_HO, lambda a, b, k=k: ho.at[k, cidx(a, b, core)],
            lambda a, b, f, k=k: ho.at[k, cidx(a, b, core), f],
        )
        parts.append(p)

    def other_rows(p):
        k = p.k

        rows = xs[k, 1 - core].reshape(8 * RB, 512)
        for j in range(5):
            res = mdot(rows, wb[j]).astype(BF16)
            gs[k, 2 * j] = res[:, :128].reshape(4, 2, RB, 128)
            gs[k, 2 * j + 1] = res[:, 128:].reshape(4, 2, RB, 128)
        p.core = send(p.base + M_CORE, gs.at[k], gr.at[k], d_c)

    def own_rows(p):
        k, px = p.k, p.px
        p.core.wait_recv()
        rows = xs[k, core].reshape(8 * RB, 512)

        def body(j):
            res = mdot(rows, wb[j])
            for i in range(2):
                both = res[:, 128 * i : 128 * i + 128].reshape(4, 2, RB, 128) + gr[
                    k, 2 * j + i
                ].astype(F32)
                g[k, 2 * j + i] = both.astype(BF16)

        for j in range(3):
            body(j)
        px[0] = send(p.base + M_X + 0, g.at[k, first, xo], prelay.at[k, 0], d_xr)
        px[3] = send(p.base + M_X + 3, g.at[k, first, xl], pright.at[k, 0], d_xl)
        for j in range(3, 5):
            body(j)
        px[2] = send(p.base + M_X + 2, g.at[k, second, xo], prelay.at[k, 1], d_xl)
        px[1] = send(p.base + M_X + 1, g.at[k, second, xr], pleft.at[k, 1], d_xr)

    def x_relay(p, half):
        k, px = p.k, p.px
        which, to, dev, into = ((first, xr, d_xr, pleft), (second, xl, d_xl, pright))[half]
        px[2 * half].wait_recv()
        g[k, which, to] = (g[k, which, to].astype(F32) + prelay[k, half].astype(F32)).astype(BF16)
        px[4 + half] = send(p.base + M_X + 4 + half, g.at[k, which, to], into.at[k, half], dev)

    def x_sum(p):
        k, px = p.k, p.px
        for i in (1, 3, 4, 5):
            px[i].wait_recv()

        def three(half, s, z):
            return (
                g[k, 5 * half + s, x, z].astype(F32)
                + pleft[k, half, s, z].astype(F32)
                + pright[k, half, s, z].astype(F32)
            )

        for s in range(10):
            zs[k, s] = three(s // 5, s % 5, 1 - zh).astype(BF16)
        p.zp = send(p.base + M_Z, zs.at[k], zr.at[k], d_z)

        for s in range(10):
            rf[k, s] = three(s // 5, s % 5, zh)

    def attend(p, inverse):
        k = p.k
        nrow = 8 * RB
        nnew = (k + 1) * RB
        inv = inverse[k * RB : (k + 1) * RB]
        p.zp.wait_recv()

        for s in range(10):
            pr[k, s] = ((rf[k, s] + zr[k, s].astype(F32)) * inv).astype(BF16)
        nk[k * RB : (k + 1) * RB] = pr[k, 8]
        nv[k * RB : (k + 1) * RB] = pr[k, 9]

        q = pr[k, 0:8].reshape(nrow, HD)
        i_id = lax.broadcasted_iota(jnp.int32, (nrow, nnew), 0)
        j_id = lax.broadcasted_iota(jnp.int32, (nrow, nnew), 1)
        seen = (lax.rem(i_id, 16) == lax.rem(j_id, 16)) & (
            j_id // 16 <= k * TS + lax.rem(i_id // 16, TS)
        )
        s_new = jnp.where(seen, rdot(q, nk[0:nnew]) * SCALE, NEG)
        peak = None
        for b in range(8):
            s = rdot(q, pool[0, 256 * b : 256 * b + 256]) * SCALE
            s = (s.reshape(nrow // 16, 16, 256) + bias[b][None]).reshape(nrow, 256)
            sb[b] = s
            here = jnp.maximum(s[:, :128], s[:, 128:])
            peak = here if peak is None else jnp.maximum(peak, here)
        top = jnp.maximum(
            jnp.max(peak, axis=1, keepdims=True), jnp.max(s_new, axis=1, keepdims=True)
        )
        w_new = jnp.exp(s_new - top)
        mixed = mdot(w_new.astype(BF16), nv[0:nnew])
        part = None
        for b in range(8):
            w = jnp.exp(sb[b] - top)
            here = w[:, :128] + w[:, 128:]
            part = here if part is None else part + here
            mixed = mixed + mdot(w.astype(BF16), pool[1, 256 * b : 256 * b + 256])
        total = jnp.sum(part, axis=1, keepdims=True) + jnp.sum(w_new, axis=1, keepdims=True)
        head_out = (mixed / total).astype(BF16)
        for s in range(8):
            ho[k, c, s // 4, :, (s % 4) * HD : (s % 4 + 1) * HD] = head_out[s * RB : (s + 1) * RB]
        p.hog.start()

    def out_rows(p):
        k, oy = p.k, p.oy
        p.hog.finish()
        lhs = [ho[k, :, f].reshape(16 * RB, 512) for f in range(2)]
        for n in range(2):
            res = mdot(lhs[0], wob[n, 0:512]) + mdot(lhs[1], wob[n, 512:1024])
            o[k, :, :, :, n * 256 : (n + 1) * 256] = res.astype(BF16).reshape(4, 2, 2 * RB, 256)
        oy[0] = send(p.base + M_Y + 0, o.at[k, yo, 0], orelay.at[k, 0], d_yr)
        oy[2] = send(p.base + M_Y + 2, o.at[k, yo, 1], orelay.at[k, 1], d_yl)
        oy[1] = send(p.base + M_Y + 1, o.at[k, yr, 1], oleft.at[k, 1], d_yr)
        oy[3] = send(p.base + M_Y + 3, o.at[k, yl, 0], oright.at[k, 0], d_yl)

    def y_relay(p, half):
        k, oy = p.k, p.oy
        to, dev, into = ((yr, d_yr, oleft), (yl, d_yl, oright))[half]
        oy[2 * half].wait_recv()
        o[k, to, half] = (o[k, to, half].astype(F32) + orelay[k, half].astype(F32)).astype(BF16)
        oy[4 + half] = send(p.base + M_Y + 4 + half, o.at[k, to, half], into.at[k, half], dev)

    def y_sum(p):
        k, oy = p.k, p.oy
        for i in (1, 3, 4, 5):
            oy[i].wait_recv()

        for z in range(2):
            ozs[k, z] = (
                o[k, y, z].astype(F32) + oleft[k, z].astype(F32) + oright[k, z].astype(F32)
            ).astype(BF16)
        p.oz = send(p.base + M_ZL, ozs.at[k], ozr.at[k], d_zl)

    def add_input(p):
        k = p.k
        p.oz.wait_recv()
        steps = pl.ds(k * TS, TS)
        for z in range(2):
            for i in range(2):
                rows = pl.ds(i * RB, RB)
                full = ozs[k, z, rows].astype(F32) + ozr[k, z, rows].astype(F32)
                hidden = xb[steps, cidx(y, z, i)].astype(F32)
                out[steps, 2 * y + z, pl.ds(16 * i, 16), :] = (
                    hidden + full.reshape(TS, 16, 512)
                ).astype(BF16)
        own = out.at[steps, pl.ds(2 * y, 2)]
        p.fo = {
            1: send(p.base + M_FO, own, own, d_yr),
            2: send(p.base + M_FO + 1, own, own, d_yl),
        }

    def pass_on(p, k):
        steps = pl.ds(p.k * TS, TS)
        p.fo[k].wait_recv()
        if k == 1:
            part = out.at[steps, 2 * yl]
            p.fo[5] = send(p.base + M_FO + 2, part, part, d_yr)
        elif k == 2:
            part = out.at[steps, 2 * yr + 1]
            p.fo[6] = send(p.base + M_FO + 3, part, part, d_yl)
        else:
            p.fo[6].wait_recv()

    def load_weights():
        for k in range(3, 8):
            loads[k].wait()
        wkvf[...] = wkvb[...].astype(F32)
        wb[4, :, 0:128] = wkvf[pl.ds(0, 512, stride=2), :].astype(BF16)
        wb[4, :, 128:256] = wkvf[pl.ds(1, 512, stride=2), :].astype(BF16)

    def sum_squares():
        lax.fori_loop(0, 16, squares, 0, unroll=4)

        def sq_send(d, carry):
            sq_msg(d).start()
            return carry

        lax.fori_loop(1, 16, sq_send, 0)

    def inverse_rms():
        def sq_wait(d, carry):
            sq_msg(d).wait_recv()
            return carry

        lax.fori_loop(1, 16, sq_wait, 0)
        sqr[c] = sqs[c]
        flat = jnp.sum(sqr[...], axis=0)[0:1, :]
        row_sq = jnp.sum(jnp.where(eye, flat, 0.0), axis=1, keepdims=True)
        return lax.rsqrt(row_sq / D + 1e-05)

    def choose_pages():
        pick = (
            lax.broadcasted_iota(jnp.int32, (16, 256), 1)
            == lax.broadcasted_iota(jnp.int32, (16, 256), 0) + 16 * c
        )
        own_pages = rdot(pick.astype(BF16), pages_ref[...].astype(BF16)).astype(jnp.int32)
        r_id = lax.broadcasted_iota(jnp.int32, (16, 256), 0)
        s_id = lax.broadcasted_iota(jnp.int32, (16, 256), 1)
        lens = jnp.zeros((16, 256), jnp.int32)
        for r in range(16):
            lens = jnp.where(r_id == r, clen_ref[c * 16 + r], lens)
        in_page = lax.rem(s_id, PAGE)
        page_id = lax.broadcasted_iota(jnp.int32, (16, 64), 1)
        named = jnp.zeros((16, 64), F32)
        for slot in range(8):
            named = jnp.where(own_pages[:, slot : slot + 1] == page_id, 1.0, named)
        present = jnp.broadcast_to(jnp.max(named, axis=0, keepdims=True), (16, 64))
        a_id = lax.broadcasted_iota(jnp.int32, (64, 64), 0)
        b_id = lax.broadcasted_iota(jnp.int32, (64, 64), 1)
        ahead = (a_id // 4 == b_id // 4) & (a_id < b_id)
        rank = mdot(present.astype(BF16), ahead.astype(BF16))
        code = jnp.where(present > 0.5, rank + 1.0, 0.0).astype(BF16)
        node_id = lax.broadcasted_iota(jnp.int32, (64, 256), 0)
        node_of = lax.broadcasted_iota(jnp.int32, (64, 256), 1) // PAGE
        to_id = lax.broadcasted_iota(jnp.int32, (128, 256), 0)
        from_id = lax.broadcasted_iota(jnp.int32, (128, 256), 1)
        same = lax.rem(to_id, PAGE) == lax.rem(from_id, PAGE)
        want = jnp.where(same, (to_id // PAGE + 1).astype(F32), -1.0)
        last = [
            (own_pages[:, slot : slot + 1], lens - slot * PAGE, s_id // PAGE)
            for slot in range(8)
        ]

        def choose(b):
            live = jnp.zeros((16, 256), F32)
            for named_page, upto, page in last:
                hit = (named_page - 4 * b == page) & (in_page < upto)
                live = jnp.where(hit, 1.0, live)
            spread = mdot(code, (node_id == node_of + 4 * b).astype(BF16))
            sel = jnp.where(spread[0:1] == want, 1.0, 0.0).astype(BF16)
            chosen[b] = sel
            return jnp.where(rdot(live.astype(BF16), sel) > 0.5, 0.0, NEG)

        def choose_two(i, carry):
            bias[i, :, 0:128] = choose(2 * i)
            bias[i, :, 128:256] = choose(2 * i + 1)
            return carry

        lax.fori_loop(0, 8, choose_two, 0, unroll=2)

    def take_pages():
        def take(b, carry):
            for f in range(2):
                rows = pl.ds(pl.multiple_of(128 * b, 128), 128)
                pool[f, rows] = mdot(chosen[b], kv[f, b]).astype(BF16)
            return carry

        lax.fori_loop(0, 16, take, 0, unroll=8)

    def list_pages():
        a_id = lax.broadcasted_iota(jnp.int32, (64, 64), 0)
        b_id = lax.broadcasted_iota(jnp.int32, (64, 64), 1)
        col_id = lax.broadcasted_iota(jnp.int32, (64, 128), 1)
        p_id = lax.broadcasted_iota(jnp.int32, (64, 128), 0)
        rows = []
        for n in range(4):
            a = 4 * c + n
            line = mask_ref[pl.ds(a, 1), :].astype(F32)
            readable = jnp.sum(jnp.where(a_id == b_id, line, 0.0), axis=1, keepdims=True)
            readable = jnp.where((readable > 0.5) & (p_id < a), 1.0, 0.0)
            before = mdot((b_id < a_id).astype(BF16), readable.astype(BF16))
            place = jnp.where(p_id == a, 0.0, before + 1.0).astype(jnp.int32)
            hit = (place == col_id) & ((readable > 0.5) | (p_id == a))
            line = jnp.sum(jnp.where(hit, p_id.astype(F32), 0.0), axis=0, keepdims=True)
            count = jnp.sum(readable, axis=0, keepdims=True) + 1.0
            rows.append(jnp.where(col_id[0:1] == 127, count, line))
        picks[...] = jnp.concatenate(rows + rows, axis=0).astype(jnp.int32)

    keep = pltpu.make_async_copy(kv, kv_out, lsem.at[10])
    rms = []

    def step(event):
        who, what = event.split(".")
        if who == "kv":
            if what == "fin":
                kvg.finish()
                keep.start()
            else:
                kvg.take(int(what[1]))
            return
        if who == "all":
            {"sq": sum_squares, "mask": choose_pages, "take": take_pages, "list": list_pages}[
                what
            ]()
            return
        p = parts[int(who[1])]
        if what == "other":
            scale_rows(p, 1 - core)
            if p.k == 0:
                load_weights()
            other_rows(p)
        elif what == "own":
            scale_rows(p, core)
            own_rows(p)
        elif what[0] == "x":
            if what == "xsum":
                x_sum(p)
            else:
                x_relay(p, int(what[2]) // 2)
        elif what == "att":
            if not rms:
                rms.append(inverse_rms())
            attend(p, rms[0])
        elif what[0] == "h":
            p.hog.take(int(what[1]))
        elif what == "out":
            if p.k == 0:
                loads[8].wait()
                loads[9].wait()
            out_rows(p)
        elif what == "ysum":
            y_sum(p)
        elif what[0] == "y":
            y_relay(p, int(what[2]) // 2)
        elif what == "add":
            add_input(p)
        else:
            pass_on(p, int(what[1]))

    for event in ORDER:
        step(event)
    keep.wait()

    for m in sent:
        m.wait_send()

    def sq_done(d, carry):
        sq_msg(d).wait_send()
        return carry

    lax.fori_loop(1, 16, sq_done, 0)


def layer_call(*args):
    hbm = pl.BlockSpec(memory_space=pl.ANY)
    vmem = pl.BlockSpec(memory_space=pltpu.VMEM)
    smem = pl.BlockSpec(memory_space=pltpu.SMEM)
    return pl.pallas_call(
        layer_kernel,
        out_shape=(
            jax.ShapeDtypeStruct((2, 16, 256, HD), BF16),
            jax.ShapeDtypeStruct((8, 128), jnp.int32),
            jax.ShapeDtypeStruct((4, 8, 32, 512), BF16),
        ),
        in_specs=[hbm, hbm, vmem, vmem, smem, hbm, vmem, hbm, hbm, hbm],
        out_specs=(hbm, vmem, vmem),
        scratch_shapes=[
            pltpu.VMEM((2, 16, 256, HD), BF16),
            pltpu.VMEM((4, 16, 16, 512), BF16),
            pltpu.VMEM((5, 512, 256), BF16),
            pltpu.VMEM((1024, 128), BF16),
            pltpu.VMEM((1024, 128), F32),
            pltpu.VMEM((2, 1024, 256), BF16),
            pltpu.VMEM((NCH, 2, 8, RB, 512), BF16),
            pltpu.VMEM((16, 8, 128), F32),
            pltpu.VMEM((16, 8, 128), F32),
            pltpu.VMEM((NCH, 10, 4, 2, RB, 128), BF16),
            pltpu.VMEM((NCH, 10, 4, 2, RB, 128), BF16),
            pltpu.VMEM((NCH, 10, 4, 2, RB, 128), BF16),
            pltpu.VMEM((NCH, 2, 5, 2, RB, 128), BF16),
            pltpu.VMEM((NCH, 2, 5, 2, RB, 128), BF16),
            pltpu.VMEM((NCH, 2, 5, 2, RB, 128), BF16),
            pltpu.VMEM((NCH, 10, RB, 128), BF16),
            pltpu.VMEM((NCH, 10, RB, 128), BF16),
            pltpu.VMEM((NCH, 10, RB, 128), F32),
            pltpu.VMEM((NCH, 10, RB, 128), BF16),
            pltpu.VMEM((64, 128), BF16),
            pltpu.VMEM((64, 128), BF16),
            pltpu.VMEM((8, 16, 256), F32),
            pltpu.VMEM((16, 128, 256), BF16),
            pltpu.VMEM((2, 2048, HD), BF16),
            pltpu.VMEM((8, 8 * RB, 256), F32),
            pltpu.VMEM((NCH, 16, 2, RB, 512), BF16),
            pltpu.VMEM((NCH, 4, 2, 2 * RB, 512), BF16),
            pltpu.VMEM((NCH, 2, 2 * RB, 512), BF16),
            pltpu.VMEM((NCH, 2, 2 * RB, 512), BF16),
            pltpu.VMEM((NCH, 2, 2 * RB, 512), BF16),
            pltpu.VMEM((NCH, 2, 2 * RB, 512), BF16),
            pltpu.VMEM((NCH, 2, 2 * RB, 512), BF16),
            pltpu.SemaphoreType.DMA((11,)),
            pltpu.SemaphoreType.DMA((NMSG,)),
            pltpu.SemaphoreType.DMA((NMSG,)),
        ],
        compiler_params=pltpu.CompilerParams(
            collective_id=0, has_side_effects=True, vmem_limit_bytes=56 * 1024 * 1024
        ),
        name="layer",
    )(*args)


def prefill_kernel(
    q_ref, kv_ref, picks, dec_ref, out, dec_out, kv, stage, mixes, peaks, totals, sem
):
    fetched = pltpu.make_async_copy(dec_ref, stage, sem.at[0])
    moved = pltpu.make_async_copy(stage, dec_out, sem.at[3])
    loads = [pltpu.make_async_copy(kv_ref.at[i], kv.at[i], sem.at[1 + i]) for i in range(2)]
    for copy in loads:
        copy.start()
    fetched.start()
    for copy in loads:
        copy.wait()
    fetched.wait()
    moved.start()

    def attend(n, start, pages, state):
        keys = jnp.concatenate([kv[0, picks[n, start + k]] for k in range(pages)], axis=0)
        values = jnp.concatenate([kv[1, picks[n, start + k]] for k in range(pages)], axis=0)
        q = jnp.concatenate([q_ref[n, :, s * HD : (s + 1) * HD] for s in range(8)], axis=0)
        i_id = lax.broadcasted_iota(jnp.int32, (512, pages * PAGE), 0)
        j_id = lax.broadcasted_iota(jnp.int32, (512, pages * PAGE), 1)
        allowed = j_id < (picks[n, 127] - start) * PAGE
        if state is None:
            allowed = allowed & ((j_id >= PAGE) | (j_id <= lax.rem(i_id, PAGE)))
        s = jnp.where(allowed, rdot(q, keys) * SCALE, NEG)
        peak = jnp.max(s, axis=1, keepdims=True)
        if state is not None:
            peak = jnp.maximum(peak, state[0])
        w = jnp.exp(s - peak)
        total = jnp.sum(w, axis=1, keepdims=True)
        mixed = mdot(w.astype(BF16), values)
        if state is not None:
            factor = jnp.exp(state[0] - peak)
            total = total + state[1] * factor
            mixed = mixed + state[2] * factor
        return peak, total, mixed

    for n in range(4):
        peak, total, mixed = attend(n, 0, 8, None)
        peaks[n] = jnp.broadcast_to(peak, (512, 128))
        totals[n] = jnp.broadcast_to(total, (512, 128))
        mixes[n] = mixed

    def deep(n, carry):
        def more(t, inner):
            state = (peaks[n][:, 0:1], totals[n][:, 0:1], mixes[n])
            peak, total, mixed = attend(n, 8 + 4 * t, 4, state)
            peaks[n] = jnp.broadcast_to(peak, (512, 128))
            totals[n] = jnp.broadcast_to(total, (512, 128))
            mixes[n] = mixed
            return inner

        return lax.fori_loop(0, jnp.maximum(picks[n, 127] - 5, 0) // 4, more, carry)

    lax.fori_loop(0, 4, deep, 0)
    for n in range(4):
        result = (mixes[n] / totals[n]).astype(BF16)
        for s in range(8):
            out[n, :, s * HD : (s + 1) * HD] = result[s * 64 : (s + 1) * 64]
    moved.wait()


def prefill_call(q, kv, picks, dec):
    hbm = pl.BlockSpec(memory_space=pl.ANY)
    vmem = pl.BlockSpec(memory_space=pltpu.VMEM)
    smem = pl.BlockSpec(memory_space=pltpu.SMEM)
    return pl.pallas_call(
        prefill_kernel,
        out_shape=(
            jax.ShapeDtypeStruct((4, PAGE, 1024), BF16),
            jax.ShapeDtypeStruct(dec.shape, BF16),
        ),
        in_specs=[vmem, hbm, smem, hbm],
        out_specs=(vmem, hbm),
        scratch_shapes=[
            pltpu.VMEM((2, 64, PAGE, HD), BF16),
            pltpu.VMEM(dec.shape, BF16),
            pltpu.VMEM((4, 512, HD), F32),
            pltpu.VMEM((4, 512, 128), F32),
            pltpu.VMEM((4, 512, 128), F32),
            pltpu.SemaphoreType.DMA((4,)),
        ],
        compiler_params=pltpu.CompilerParams(vmem_limit_bytes=62 * 1024 * 1024),
        name="prefill",
    )(q, kv, picks, dec)


def per_device(
    prefill_query, prefill_key, prefill_value, tree_mask, pages, cache_len,
    dec_in, norm_gain, w_query, w_keyval, w_out,
):
    kv, picks, dec = layer_call(
        prefill_key, prefill_value, tree_mask, pages.T, cache_len,
        dec_in.reshape(4, 16, 16, 512), norm_gain.reshape(4, 128), w_query,
        w_keyval.reshape(1024, 128), w_out,
    )
    prefill_out, dec_out = prefill_call(
        prefill_query.reshape(4, PAGE, 1024), kv.reshape(2, 64, PAGE, HD), picks, dec
    )
    return prefill_out.reshape(256, 1024), dec_out.reshape(4, 256, 512)


def solution(mesh):
    return jax.shard_map(
        per_device,
        mesh=mesh,
        in_specs=(
            P("ctx", "head"), P("ctx", "head"), P("ctx", "head"), P(), P(), P(),
            P(None, None, "ctx"), P("ctx"), P("ctx", "head"), P("ctx", None, "head"),
            P("head", "ctx"),
        ),
        out_specs=(P("ctx", "head"), P(None, None, "ctx")),
        check_vma=False,
    )
```

time: 110 us -> 84.9 us (0.77)
  the two profiles are of different devices: /device:TPU:71 before, /device:TPU:0 now
where the time goes in v2:
time: 84.9 us; the launch traced here: 84.7 us
  Pallas kernels  84.1 us (99%)
    pallas_call x1, Pallas kernels, layer_call(): pl.pallas_call(layer_kernel, out_shape=(jax.ShapeDtypeStruct((2, 16, 256,...  78.2 us
    pallas_call x1, Pallas kernels, prefill_call(): pl.pallas_call(prefill_kernel, out_shape=(jax.ShapeDtypeStruct((4, PAGE,...  5.82 us

profile of v2, /device:TPU:0, one launch (start us, length us, event | category | flops | bytes accessed | tf_op | source)
XLA Modules:
  0.0 84.7 jit_solution(13736937040579291886)
XLA Ops:
  0.6 78.2 %layer.1 = (bf16[2,16,256,128]{3,2,1,0:T(8,128)(2,1)}, s32[8,128]{1,0:T(8,128)}, bf16[4,8,32,512]{3,2,1,0:T(8,128)(2,1)}) custom-call(bf16[256,128]{1,0:T(8,128)(2,1)} %key_ref.1, bf16[256,128]{1,0:T(8,128)(2,1)} %val_ref.1, s32[64,64]{1,0:T(8,128)} %mask_ref.1, s32[8,256]{1,0:T(8,128)} %bitcast.12, s32[256]{0:T(256)} %clen_ref.1, ...), custom_call_target="tpu_custom_call" | custom-call | tf_op jit(solution)/shard_map/layer/pallas_call | solution.py:561
  78.9 5.8 %prefill.1 = (bf16[4,64,1024]{2,1,0:T(8,128)(2,1)}, bf16[4,8,32,512]{3,2,1,0:T(8,128)(2,1)}) custom-call(bf16[4,64,1024]{2,1,0:T(8,128)(2,1)} %bitcast.10, bf16[2,64,64,128]{3,2,1,0:T(8,128)(2,1)} %bitcast.8, s32[8,128]{1,0:T(8,128)} %get-tuple-element.8.picks, bf16[4,8,32,512]{3,2,1,0:T(8,128)(2,1)} %get-tuple-element.9.dec_ref), custom_call_target="tpu_custom_call" | custom-call | tf_op jit(solution)/shard_map/prefill/pallas_call | solution.py:679

commit v3 on v2

--- a/solution.py
+++ b/solution.py
@@ -15,7 +15,7 @@
 BF16 = jnp.bfloat16
 MESH = pl.DeviceIdType.MESH
 
-NCH = 2
+NCH = 4
 TS = STEPS // NCH
 RB = 16 * TS
 
@@ -28,12 +28,17 @@
 
 
 ORDER = (
-    "p0.other", "p1.other", "kv.r1", "kv.r2", "p0.own", "all.sq", "kv.r5", "kv.r0", "p0.xr0",
-    "p0.xr2", "p1.own", "all.mask", "kv.r3", "kv.r4", "p1.xr0", "p1.xr2", "p0.xsum", "all.list",
-    "kv.r7", "p1.xsum", "kv.fin", "all.take", "p0.att", "p1.att", "p0.h0", "p0.h1", "p0.h2",
-    "p1.h1", "p1.h2", "p0.h3", "p0.h4", "p1.h0", "p0.h5", "p1.h5", "p0.h7", "p1.h3", "p1.h4",
-    "p0.out", "p1.h7", "p0.yr0", "p0.yr2", "p1.out", "p0.ysum", "p1.yr0", "p1.yr2", "p0.add",
-    "p1.ysum", "p1.add", "p0.f1", "p0.f2", "p1.f1", "p1.f2", "p0.f5", "p1.f5",
+    "p0.other", "p0.own", "all.sq", "kv.r2", "kv.r1", "p0.xr0", "p0.xr2", "p1.other", "kv.r0",
+    "p2.other", "kv.r5", "p1.own", "all.mask", "kv.r3", "kv.r4", "p3.other", "p1.xr0", "p1.xr2",
+    "p0.xsum", "p2.own", "kv.r7", "p3.own", "p1.xsum", "kv.fin", "all.take", "p2.xr2", "p2.xr0",
+    "p0.att", "p3.xr2", "p2.xsum", "p3.xr0", "p1.att", "p3.xsum", "p0.h1", "p0.h2", "p0.h0",
+    "p1.h1", "p2.att", "p0.h3", "p1.h0", "p0.h4", "p0.h5", "p3.att", "p2.h0", "p1.h4", "p0.h7",
+    "p1.h3", "p2.h2", "p2.h1", "p1.h2", "p2.h3", "p2.h4", "p0.out", "p2.h5", "p1.h7", "p1.h5",
+    "p2.h7", "p3.h0", "p3.h2", "p3.h1", "p2.out", "p0.yr2", "p3.h4", "p3.h3", "p0.yr0",
+    "p1.out", "p3.h5", "p2.yr0", "p2.yr2", "p3.h7", "p0.ysum", "p1.yr0", "p1.yr2", "p3.out",
+    "p1.ysum", "p2.ysum", "p3.yr0", "p3.yr2", "p0.add", "p1.add", "p3.ysum", "p2.add", "p0.f1",
+    "all.list", "p1.f2", "p3.add", "p1.f1", "p2.f2", "p2.f1", "p0.f2", "p3.f1", "p3.f2",
+    "p2.f5", "p1.f5", "p0.f5", "p3.f5",
 )
 
 
@@ -46,10 +51,11 @@
 
 
 def layer_kernel(
-    key_ref, val_ref, mask_ref, pages_ref, clen_ref, x_ref, gain_ref, wq_ref, wkv_ref, wo_ref,
+    key_ref, val_ref, mask_hbm, pages_hbm, clen_hbm, x_ref, gain_hbm, wq_ref, wkv_ref, wo_ref,
     kv_out, picks, out,
+    mask_ref, pages_ref, clen_ref, gain_ref,
     kv, xb, wb, wkvb, wkvf, wob, xs, sqs, sqr, gs, gr, g, prelay, pleft, pright, zs, zr, rf,
-    pr, nk, nv, bias, chosen, pool, sb, ho, o, orelay, oleft, oright, ozs, ozr,
+    pr, nk, nv, bias, chosen, pool_k, pool_v, sb, ho, o, orelay, oleft, oright, ozs, ozr,
     lsem, ssem, rsem,
 ):
     c = lax.axis_index("ctx")
@@ -81,6 +87,18 @@
             src_ref=src, dst_ref=dst, send_sem=ssem.at[i], recv_sem=rsem.at[i],
             device_id=dev, device_id_type=MESH,
         )
+
+    barrier = pltpu.get_barrier_semaphore()
+
+    def greet(d, carry):
+        pl.semaphore_signal(
+            barrier, inc=1, device_id=(lax.rem(c + d, 16), h), device_id_type=MESH
+        )
+        return carry
+
+    for dev in (d_yr, d_yl, d_zl):
+        pl.semaphore_signal(barrier, inc=1, device_id=dev, device_id_type=MESH)
+    lax.fori_loop(1, 16, greet, 0)
 
     loads = [
         pltpu.make_async_copy(key_ref, kv.at[0, c], lsem.at[0]),
@@ -96,20 +114,13 @@
         loads.append(
             pltpu.make_async_copy(wo_ref.at[:, pl.ds(256 * j, 256)], wob.at[j], lsem.at[8 + j])
         )
+    for i, (src, dst) in enumerate(
+        ((gain_hbm, gain_ref), (mask_hbm, mask_ref), (pages_hbm, pages_ref), (clen_hbm, clen_ref))
+    ):
+        loads.append(pltpu.make_async_copy(src, dst, lsem.at[11 + i]))
     for copy in loads:
         copy.start()
 
-    barrier = pltpu.get_barrier_semaphore()
-
-    def greet(d, carry):
-        pl.semaphore_signal(
-            barrier, inc=1, device_id=(lax.rem(c + d, 16), h), device_id_type=MESH
-        )
-        return carry
-
-    lax.fori_loop(1, 16, greet, 0)
-    for dev in (d_yr, d_yl, d_zl):
-        pl.semaphore_signal(barrier, inc=1, device_id=dev, device_id_type=MESH)
     pl.semaphore_wait(barrier, 18)
 
     sent = []
@@ -178,6 +189,7 @@
     kvg.start()
 
     loads[2].wait()
+    loads[10].wait()
     row_id = lax.broadcasted_iota(jnp.int32, (64, 128), 0)
     lane_id = lax.broadcasted_iota(jnp.int32, (64, 128), 1)
     eye = row_id == lane_id
@@ -291,7 +303,7 @@
         for s in range(10):
             pr[k, s] = ((rf[k, s] + zr[k, s].astype(F32)) * inv).astype(BF16)
         nk[k * RB : (k + 1) * RB] = pr[k, 8]
-        nv[k * RB : (k + 1) * RB] = pr[k, 9]
+        nv[k * RB : (k + 1) * RB, 0:128] = pr[k, 9]
 
         q = pr[k, 0:8].reshape(nrow, HD)
         i_id = lax.broadcasted_iota(jnp.int32, (nrow, nnew), 0)
@@ -302,7 +314,7 @@
         s_new = jnp.where(seen, rdot(q, nk[0:nnew]) * SCALE, NEG)
         peak = None
         for b in range(8):
-            s = rdot(q, pool[0, 256 * b : 256 * b + 256]) * SCALE
+            s = rdot(q, pool_k[256 * b : 256 * b + 256]) * SCALE
             s = (s.reshape(nrow // 16, 16, 256) + bias[b][None]).reshape(nrow, 256)
             sb[b] = s
             here = jnp.maximum(s[:, :128], s[:, 128:])
@@ -312,14 +324,10 @@
         )
         w_new = jnp.exp(s_new - top)
         mixed = mdot(w_new.astype(BF16), nv[0:nnew])
-        part = None
         for b in range(8):
-            w = jnp.exp(sb[b] - top)
-            here = w[:, :128] + w[:, 128:]
-            part = here if part is None else part + here
-            mixed = mixed + mdot(w.astype(BF16), pool[1, 256 * b : 256 * b + 256])
-        total = jnp.sum(part, axis=1, keepdims=True) + jnp.sum(w_new, axis=1, keepdims=True)
-        head_out = (mixed / total).astype(BF16)
+            w = jnp.exp(sb[b] - top).astype(BF16)
+            mixed = mixed + mdot(w, pool_v[256 * b : 256 * b + 256])
+        head_out = (mixed[:, 0:128] / mixed[:, 128:256]).astype(BF16)
         for s in range(8):
             ho[k, c, s // 4, :, (s % 4) * HD : (s % 4 + 1) * HD] = head_out[s * RB : (s + 1) * RB]
         p.hog.start()
@@ -412,6 +420,8 @@
         return lax.rsqrt(row_sq / D + 1e-05)
 
     def choose_pages():
+        loads[12].wait()
+        loads[13].wait()
         pick = (
             lax.broadcasted_iota(jnp.int32, (16, 256), 1)
             == lax.broadcasted_iota(jnp.int32, (16, 256), 0) + 16 * c
@@ -462,15 +472,19 @@
         lax.fori_loop(0, 8, choose_two, 0, unroll=2)
 
     def take_pages():
+        pool_v[:, 128:256] = jnp.ones((2048, 128), BF16)
+        nv[:, 128:256] = jnp.ones((64, 128), BF16)
+
         def take(b, carry):
-            for f in range(2):
-                rows = pl.ds(pl.multiple_of(128 * b, 128), 128)
-                pool[f, rows] = mdot(chosen[b], kv[f, b]).astype(BF16)
+            rows = pl.ds(pl.multiple_of(128 * b, 128), 128)
+            pool_k[rows] = mdot(chosen[b], kv[0, b]).astype(BF16)
+            pool_v[rows, 0:128] = mdot(chosen[b], kv[1, b]).astype(BF16)
             return carry
 
         lax.fori_loop(0, 16, take, 0, unroll=8)
 
     def list_pages():
+        loads[11].wait()
         a_id = lax.broadcasted_iota(jnp.int32, (64, 64), 0)
         b_id = lax.broadcasted_iota(jnp.int32, (64, 64), 1)
         col_id = lax.broadcasted_iota(jnp.int32, (64, 128), 1)
@@ -491,6 +505,7 @@
 
     keep = pltpu.make_async_copy(kv, kv_out, lsem.at[10])
     rms = []
+    late = [loads[8], loads[9]]
 
     def step(event):
         who, what = event.split(".")
@@ -527,9 +542,8 @@
         elif what[0] == "h":
             p.hog.take(int(what[1]))
         elif what == "out":
-            if p.k == 0:
-                loads[8].wait()
-                loads[9].wait()
+            while late:
+                late.pop().wait()
             out_rows(p)
         elif what == "ysum":
             y_sum(p)
@@ -557,7 +571,6 @@
 def layer_call(*args):
     hbm = pl.BlockSpec(memory_space=pl.ANY)
     vmem = pl.BlockSpec(memory_space=pltpu.VMEM)
-    smem = pl.BlockSpec(memory_space=pltpu.SMEM)
     return pl.pallas_call(
         layer_kernel,
         out_shape=(
@@ -565,9 +578,13 @@
             jax.ShapeDtypeStruct((8, 128), jnp.int32),
             jax.ShapeDtypeStruct((4, 8, 32, 512), BF16),
         ),
-        in_specs=[hbm, hbm, vmem, vmem, smem, hbm, vmem, hbm, hbm, hbm],
+        in_specs=[hbm] * 10,
         out_specs=(hbm, vmem, vmem),
         scratch_shapes=[
+            pltpu.VMEM((64, 64), jnp.int32),
+            pltpu.VMEM((8, 256), jnp.int32),
+            pltpu.SMEM((256,), jnp.int32),
+            pltpu.VMEM((4, 128), BF16),
             pltpu.VMEM((2, 16, 256, HD), BF16),
             pltpu.VMEM((4, 16, 16, 512), BF16),
             pltpu.VMEM((5, 512, 256), BF16),
@@ -588,10 +605,11 @@
             pltpu.VMEM((NCH, 10, RB, 128), F32),
             pltpu.VMEM((NCH, 10, RB, 128), BF16),
             pltpu.VMEM((64, 128), BF16),
-            pltpu.VMEM((64, 128), BF16),
+            pltpu.VMEM((64, 256), BF16),
             pltpu.VMEM((8, 16, 256), F32),
             pltpu.VMEM((16, 128, 256), BF16),
-            pltpu.VMEM((2, 2048, HD), BF16),
+            pltpu.VMEM((2048, HD), BF16),
+            pltpu.VMEM((2048, 2 * HD), BF16),
             pltpu.VMEM((8, 8 * RB, 256), F32),
             pltpu.VMEM((NCH, 16, 2, RB, 512), BF16),
             pltpu.VMEM((NCH, 4, 2, 2 * RB, 512), BF16),
@@ -600,7 +618,7 @@
             pltpu.VMEM((NCH, 2, 2 * RB, 512), BF16),
             pltpu.VMEM((NCH, 2, 2 * RB, 512), BF16),
             pltpu.VMEM((NCH, 2, 2 * RB, 512), BF16),
-            pltpu.SemaphoreType.DMA((11,)),
+            pltpu.SemaphoreType.DMA((15,)),
             pltpu.SemaphoreType.DMA((NMSG,)),
             pltpu.SemaphoreType.DMA((NMSG,)),
         ],
@@ -612,22 +630,20 @@
 
 
 def prefill_kernel(
-    q_ref, kv_ref, picks, dec_ref, out, dec_out, kv, stage, mixes, peaks, totals, sem
+    q_hbm, kv_ref, picks, dec_ref, out_hbm, dec_out, q_ref, kv, stage, out, peaks, mixes, sem
 ):
-    fetched = pltpu.make_async_copy(dec_ref, stage, sem.at[0])
-    moved = pltpu.make_async_copy(stage, dec_out, sem.at[3])
-    loads = [pltpu.make_async_copy(kv_ref.at[i], kv.at[i], sem.at[1 + i]) for i in range(2)]
+    loads = [pltpu.make_async_copy(kv_ref.at[i], kv.at[i], sem.at[i]) for i in range(2)]
+    loads.append(pltpu.make_async_copy(q_hbm, q_ref, sem.at[2]))
+    fetched = pltpu.make_async_copy(dec_ref, stage, sem.at[3])
+    moved = pltpu.make_async_copy(stage, dec_out, sem.at[4])
     for copy in loads:
         copy.start()
     fetched.start()
-    for copy in loads:
-        copy.wait()
-    fetched.wait()
-    moved.start()
 
     def attend(n, start, pages, state):
         keys = jnp.concatenate([kv[0, picks[n, start + k]] for k in range(pages)], axis=0)
         values = jnp.concatenate([kv[1, picks[n, start + k]] for k in range(pages)], axis=0)
+        values = jnp.concatenate([values, jnp.ones((pages * PAGE, 128), BF16)], axis=1)
         q = jnp.concatenate([q_ref[n, :, s * HD : (s + 1) * HD] for s in range(8)], axis=0)
         i_id = lax.broadcasted_iota(jnp.int32, (512, pages * PAGE), 0)
         j_id = lax.broadcasted_iota(jnp.int32, (512, pages * PAGE), 1)
@@ -638,43 +654,49 @@
         peak = jnp.max(s, axis=1, keepdims=True)
         if state is not None:
             peak = jnp.maximum(peak, state[0])
-        w = jnp.exp(s - peak)
-        total = jnp.sum(w, axis=1, keepdims=True)
-        mixed = mdot(w.astype(BF16), values)
+        mixed = mdot(jnp.exp(s - peak).astype(BF16), values)
         if state is not None:
-            factor = jnp.exp(state[0] - peak)
-            total = total + state[1] * factor
-            mixed = mixed + state[2] * factor
-        return peak, total, mixed
-
-    for n in range(4):
-        peak, total, mixed = attend(n, 0, 8, None)
-        peaks[n] = jnp.broadcast_to(peak, (512, 128))
-        totals[n] = jnp.broadcast_to(total, (512, 128))
-        mixes[n] = mixed
-
-    def deep(n, carry):
-        def more(t, inner):
-            state = (peaks[n][:, 0:1], totals[n][:, 0:1], mixes[n])
-            peak, total, mixed = attend(n, 8 + 4 * t, 4, state)
-            peaks[n] = jnp.broadcast_to(peak, (512, 128))
-            totals[n] = jnp.broadcast_to(total, (512, 128))
-            mixes[n] = mixed
-            return inner
-
-        return lax.fori_loop(0, jnp.maximum(picks[n, 127] - 5, 0) // 4, more, carry)
-
-    lax.fori_loop(0, 4, deep, 0)
-    for n in range(4):
-        result = (mixes[n] / totals[n]).astype(BF16)
+            mixed = mixed + state[1] * jnp.exp(state[0] - peak)
+        return peak, mixed
+
+    def write(n, mixed):
+        result = (mixed[:, 0:128] / mixed[:, 128:256]).astype(BF16)
         for s in range(8):
             out[n, :, s * HD : (s + 1) * HD] = result[s * 64 : (s + 1) * 64]
+
+    for copy in loads:
+        copy.wait()
+    fetched.wait()
+    moved.start()
+    for n in range(4):
+        peak, mixed = attend(n, 0, 8, None)
+        peaks[n] = jnp.broadcast_to(peak, (512, 128))
+        mixes[n] = mixed
+        write(n, mixed)
+
+    def deep(n, carry):
+        @pl.when(picks[n, 127] > 8)
+        def _():
+            def more(t, inner):
+                peak, mixed = attend(n, 8 + 4 * t, 4, (peaks[n][:, 0:1], mixes[n]))
+                peaks[n] = jnp.broadcast_to(peak, (512, 128))
+                mixes[n] = mixed
+                return inner
+
+            lax.fori_loop(0, (picks[n, 127] - 5) // 4, more, 0)
+            write(n, mixes[n])
+
+        return carry
+
+    lax.fori_loop(0, 4, deep, 0)
+    done = pltpu.make_async_copy(out, out_hbm, sem.at[5])
+    done.start()
+    done.wait()
     moved.wait()
 
 
 def prefill_call(q, kv, picks, dec):
     hbm = pl.BlockSpec(memory_space=pl.ANY)
-    vmem = pl.BlockSpec(memory_space=pltpu.VMEM)
     smem = pl.BlockSpec(memory_space=pltpu.SMEM)
     return pl.pallas_call(
         prefill_kernel,
@@ -682,15 +704,16 @@
             jax.ShapeDtypeStruct((4, PAGE, 1024), BF16),
             jax.ShapeDtypeStruct(dec.shape, BF16),
         ),
-        in_specs=[vmem, hbm, smem, hbm],
-        out_specs=(vmem, hbm),
+        in_specs=[hbm, hbm, smem, hbm],
+        out_specs=(hbm, hbm),
         scratch_shapes=[
+            pltpu.VMEM((4, PAGE, 1024), BF16),
             pltpu.VMEM((2, 64, PAGE, HD), BF16),
             pltpu.VMEM(dec.shape, BF16),
-            pltpu.VMEM((4, 512, HD), F32),
+            pltpu.VMEM((4, PAGE, 1024), BF16),
             pltpu.VMEM((4, 512, 128), F32),
-            pltpu.VMEM((4, 512, 128), F32),
-            pltpu.SemaphoreType.DMA((4,)),
+            pltpu.VMEM((4, 512, 256), F32),
+            pltpu.SemaphoreType.DMA((6,)),
         ],
         compiler_params=pltpu.CompilerParams(vmem_limit_bytes=62 * 1024 * 1024),
         name="prefill",

time: 84.9 us -> 83.2 us (0.980)
  Pallas kernels: 84.1 us -> 82.5 us
    pallas_call x1, Pallas kernels: 78.2 us -> 76.9 us  [layer_call(): pl.pallas_call(layer_kernel, out_shape=(jax.ShapeDtypeStruct((2, 16, 256,...]
where the time goes in v3:
time: 83.2 us; the launch traced here: 83.1 us
  Pallas kernels  82.5 us (99%)
    pallas_call x1, Pallas kernels, layer_call(): pl.pallas_call(layer_kernel, out_shape=(jax.ShapeDtypeStruct((2, 16, 256,...  76.9 us
    pallas_call x1, Pallas kernels, prefill_call(): pl.pallas_call(prefill_kernel, out_shape=(jax.ShapeDtypeStruct((4, PAGE,...  5.54 us

profile of v3, /device:TPU:0, one launch (start us, length us, event | category | flops | bytes accessed | tf_op | source)
XLA Modules:
  0.0 83.1 jit_solution(9942583877936888400)
XLA Ops:
  0.6 76.9 %layer.1 = (bf16[2,16,256,128]{3,2,1,0:T(8,128)(2,1)}, s32[8,128]{1,0:T(8,128)}, bf16[4,8,32,512]{3,2,1,0:T(8,128)(2,1)}) custom-call(bf16[256,128]{1,0:T(8,128)(2,1)} %key_ref.1, bf16[256,128]{1,0:T(8,128)(2,1)} %val_ref.1, s32[64,64]{1,0:T(8,128)} %mask_hbm.1, s32[8,256]{1,0:T(8,128)} %bitcast.12, s32[256]{0:T(256)} %clen_hbm.1, ...), custom_call_target="tpu_custom_call" | custom-call | tf_op jit(solution)/shard_map/layer/pallas_call | solution.py:574
  77.6 5.5 %prefill.1 = (bf16[4,64,1024]{2,1,0:T(8,128)(2,1)}, bf16[4,8,32,512]{3,2,1,0:T(8,128)(2,1)}) custom-call(bf16[4,64,1024]{2,1,0:T(8,128)(2,1)} %bitcast.10, bf16[2,64,64,128]{3,2,1,0:T(8,128)(2,1)} %bitcast.8, s32[8,128]{1,0:T(8,128)} %get-tuple-element.8.picks, bf16[4,8,32,512]{3,2,1,0:T(8,128)(2,1)} %get-tuple-element.9.dec_ref), custom_call_target="tpu_custom_call" | custom-call | tf_op jit(solution)/shard_map/prefill/pallas_call | solution.py:701

commit v4 on v3

--- a/solution.py
+++ b/solution.py
@@ -20,25 +20,24 @@
 RB = 16 * TS
 
 KV0 = 0
-SQ0 = 17
-PART0 = 33
-M_CORE, M_X, M_Z, M_HO, M_Y, M_ZL, M_FO = 0, 1, 7, 8, 25, 31, 32
-PART_MSGS = 36
+SQ0 = 11
+PART0 = 16
+M_CORE, M_X, M_Z, M_HO, M_Y, M_ZL, M_FO = 0, 1, 7, 8, 17, 23, 24
+PART_MSGS = 28
 NMSG = PART0 + NCH * PART_MSGS
 
 
 ORDER = (
-    "p0.other", "p0.own", "all.sq", "kv.r2", "kv.r1", "p0.xr0", "p0.xr2", "p1.other", "kv.r0",
-    "p2.other", "kv.r5", "p1.own", "all.mask", "kv.r3", "kv.r4", "p3.other", "p1.xr0", "p1.xr2",
-    "p0.xsum", "p2.own", "kv.r7", "p3.own", "p1.xsum", "kv.fin", "all.take", "p2.xr2", "p2.xr0",
-    "p0.att", "p3.xr2", "p2.xsum", "p3.xr0", "p1.att", "p3.xsum", "p0.h1", "p0.h2", "p0.h0",
-    "p1.h1", "p2.att", "p0.h3", "p1.h0", "p0.h4", "p0.h5", "p3.att", "p2.h0", "p1.h4", "p0.h7",
-    "p1.h3", "p2.h2", "p2.h1", "p1.h2", "p2.h3", "p2.h4", "p0.out", "p2.h5", "p1.h7", "p1.h5",
-    "p2.h7", "p3.h0", "p3.h2", "p3.h1", "p2.out", "p0.yr2", "p3.h4", "p3.h3", "p0.yr0",
-    "p1.out", "p3.h5", "p2.yr0", "p2.yr2", "p3.h7", "p0.ysum", "p1.yr0", "p1.yr2", "p3.out",
-    "p1.ysum", "p2.ysum", "p3.yr0", "p3.yr2", "p0.add", "p1.add", "p3.ysum", "p2.add", "p0.f1",
-    "all.list", "p1.f2", "p3.add", "p1.f1", "p2.f2", "p2.f1", "p0.f2", "p3.f1", "p3.f2",
-    "p2.f5", "p1.f5", "p0.f5", "p3.f5",
+    "p0.other", "all.sq", "p1.other", "p0.own", "kv.z", "p1.own", "p0.xr2", "all.sq1", "p0.xr0",
+    "p2.other", "p3.other", "kv.l", "kv.r", "p1.xr0", "p2.own", "p1.xr2", "p0.xsum", "p3.own",
+    "all.mask", "kv.f", "all.sq2", "p2.xr2", "p1.xsum", "p2.xr0", "kv.fin", "all.take",
+    "p0.att", "p2.xsum", "p3.xr0", "p3.xr2", "p1.att", "p0.hz", "p2.att", "p3.xsum", "p0.hl",
+    "p0.hr", "p1.hz", "p2.hz", "p0.hf", "p3.att", "p1.hl", "p1.hr", "p2.hl", "p2.hr", "p0.out",
+    "p1.hf", "p3.hz", "all.list", "p2.hf", "p1.out", "p3.hl", "p3.hr", "p2.out", "p0.yr0",
+    "p3.hf", "p0.yr2", "p1.yr2", "p1.yr0", "p3.out", "p0.ysum", "p2.yr0", "p2.yr2", "p1.ysum",
+    "p3.yr0", "p3.yr2", "p2.ysum", "p0.add", "p3.ysum", "p1.add", "p2.add", "p3.add", "p0.f2",
+    "p1.f1", "p1.f2", "p0.f1", "p2.f1", "p2.f2", "p3.f2", "p3.f1", "p0.f5", "p1.f5", "p2.f5",
+    "p3.f5",
 )
 
 
@@ -53,8 +52,8 @@
 def layer_kernel(
     key_ref, val_ref, mask_hbm, pages_hbm, clen_hbm, x_ref, gain_hbm, wq_ref, wkv_ref, wo_ref,
     kv_out, picks, out,
-    mask_ref, pages_ref, clen_ref, gain_ref,
-    kv, xb, wb, wkvb, wkvf, wob, xs, sqs, sqr, gs, gr, g, prelay, pleft, pright, zs, zr, rf,
+    ob, mask_ref, pages_ref, clen_ref, gain_ref,
+    kv, xb, wb, wkvb, wkvf, wob, xs, sqs, sqc, sqx, sqn, sqz, sqr, gs, gr, g, prelay, pleft, pright, zs, zr, rf,
     pr, nk, nv, bias, chosen, pool_k, pool_v, sb, ho, o, orelay, oleft, oright, ozs, ozr,
     lsem, ssem, rsem,
 ):
@@ -81,6 +80,7 @@
     d_yr = (c, hidx(yr, zl))
     d_yl = (c, hidx(yl, zl))
     d_zl = (c, hidx(y, 1 - zl))
+    d_xo = (cidx(xo, zh, core), h)
 
     def msg(i, src, dst, dev):
         return pltpu.make_async_remote_copy(
@@ -90,19 +90,12 @@
 
     barrier = pltpu.get_barrier_semaphore()
 
-    def greet(d, carry):
-        pl.semaphore_signal(
-            barrier, inc=1, device_id=(lax.rem(c + d, 16), h), device_id_type=MESH
-        )
-        return carry
-
-    for dev in (d_yr, d_yl, d_zl):
+    for dev in (d_xr, d_xl, d_z, d_c, d_yr, d_yl, d_zl, d_xo):
         pl.semaphore_signal(barrier, inc=1, device_id=dev, device_id_type=MESH)
-    lax.fori_loop(1, 16, greet, 0)
 
     loads = [
-        pltpu.make_async_copy(key_ref, kv.at[0, c], lsem.at[0]),
-        pltpu.make_async_copy(val_ref, kv.at[1, c], lsem.at[1]),
+        pltpu.make_async_copy(key_ref, kv.at[x, core, zh, 0], lsem.at[0]),
+        pltpu.make_async_copy(val_ref, kv.at[x, core, zh, 1], lsem.at[1]),
         pltpu.make_async_copy(x_ref, xb, lsem.at[2]),
         pltpu.make_async_copy(wkv_ref, wkvb, lsem.at[3]),
     ]
@@ -121,7 +114,7 @@
     for copy in loads:
         copy.start()
 
-    pl.semaphore_wait(barrier, 18)
+    pl.semaphore_wait(barrier, 8)
 
     sent = []
 
@@ -131,59 +124,55 @@
         sent.append(m)
         return m
 
+    def drain(left):
+        while len(sent) > left:
+            sent.pop(0).wait_send()
+
     class Gather:
-        def __init__(self, base, blk, half):
-            self.base, self.blk, self.half = base, blk, half
+        def __init__(self, base, pair, early):
+            self.base, self.pair, self.early = base, pair, early
             self.m = {}
 
         def put(self, k, ref, dev):
             self.m[k] = send(self.base + k, ref, ref, dev)
 
-        def share(self, k, xi, zi):
-            ref = self.blk(xi, zi)
-            self.m[9 + k] = send(self.base + 9 + k, ref, ref, d_c)
-
         def start(self):
-            own = self.blk(x, zh)
+            own = self.pair(x).at[zh]
             self.put(0, own, d_z)
-            self.put(1, own, d_xr)
-            self.put(2, own, d_xl)
-            self.share(0, x, zh)
-
-        def take(self, k):
-            z2 = 1 - zh
-            self.m[k].wait_recv()
-            if k == 0:
-                other = self.blk(x, z2)
-                self.put(3, other, d_xr)
-                self.put(4, other, d_xl)
-                self.share(1, x, z2)
-            elif k == 1:
-                self.put(5, self.half(xl, zh, 0), d_xr)
-                self.share(2, xl, zh)
-            elif k == 2:
-                self.put(6, self.half(xr, zh, 1), d_xl)
-                self.share(3, xr, zh)
-            elif k == 3:
-                self.put(7, self.half(xl, z2, 0), d_xr)
-                self.share(4, xl, z2)
-            elif k == 4:
-                self.put(8, self.half(xr, z2, 1), d_xl)
-                self.share(5, xr, z2)
-            elif k == 5:
-                self.m[6].wait_recv()
-                self.share(6, xo, zh)
+            if self.early:
+                self.put(9, own, d_xr)
+                self.put(10, own, d_xl)
+
+        def take(self, which):
+            if which == "z":
+                self.m[0].wait_recv()
+                ref = self.pair(x)
+                part = ref.at[1 - zh] if self.early else ref
+                self.put(1, part, d_xr)
+                self.put(2, part, d_xl)
+                self.put(5, ref, d_c)
+            elif which == "l":
+                if self.early:
+                    self.m[9].wait_recv()
+                self.m[1].wait_recv()
+                self.put(3, self.pair(xl).at[0], d_xr)
+                self.put(6, self.pair(xl), d_c)
+            elif which == "r":
+                if self.early:
+                    self.m[10].wait_recv()
+                self.m[2].wait_recv()
+                self.put(4, self.pair(xr).at[1], d_xl)
+                self.put(7, self.pair(xr), d_c)
             else:
-                self.m[8].wait_recv()
-                self.share(7, xo, z2)
+                self.m[3].wait_recv()
+                self.m[4].wait_recv()
+                self.put(8, self.pair(xo), d_c)
 
         def finish(self):
-            for k in range(8):
-                self.m[9 + k].wait_recv()
-
-    kvg = Gather(
-        KV0, lambda a, b: kv.at[:, cidx(a, b, core)], lambda a, b, k: kv.at[k, cidx(a, b, core)]
-    )
+            for k in range(5, 9):
+                self.m[k].wait_recv()
+
+    kvg = Gather(KV0, lambda a: kv.at[a, core], True)
     loads[0].wait()
     loads[1].wait()
     kvg.start()
@@ -210,12 +199,8 @@
         raw = xb[:, d].astype(F32).reshape(64, 512)
         part = jnp.sum(raw * raw, axis=1, keepdims=True)
         flat = jnp.sum(jnp.where(eye, part, 0.0), axis=0, keepdims=True)
-        sqs[d] = jnp.broadcast_to(flat, (8, 128))
+        sqs[lax.rem(d, 2), d // 4, lax.rem(d // 2, 2)] = jnp.broadcast_to(flat, (8, 128))
         return carry
-
-    def sq_msg(d):
-        to = lax.rem(c + d, 16)
-        return msg(SQ0 + d, sqs.at[to], sqr.at[c], (to, h))
 
     first = pl.ds(0, 5)
     second = pl.ds(5, 5)
@@ -229,10 +214,7 @@
         p.k = k
         p.base = PART0 + k * PART_MSGS
         p.px, p.oy = {}, {}
-        p.hog = Gather(
-            p.base + M_HO, lambda a, b, k=k: ho.at[k, cidx(a, b, core)],
-            lambda a, b, f, k=k: ho.at[k, cidx(a, b, core), f],
-        )
+        p.hog = Gather(p.base + M_HO, lambda a, k=k: ho.at[k, a, core], False)
         parts.append(p)
 
     def other_rows(p):
@@ -256,23 +238,23 @@
                 both = res[:, 128 * i : 128 * i + 128].reshape(4, 2, RB, 128) + gr[
                     k, 2 * j + i
                 ].astype(F32)
-                g[k, 2 * j + i] = both.astype(BF16)
+                g[k, :, 2 * j + i] = both.astype(BF16)
 
         for j in range(3):
             body(j)
-        px[0] = send(p.base + M_X + 0, g.at[k, first, xo], prelay.at[k, 0], d_xr)
-        px[3] = send(p.base + M_X + 3, g.at[k, first, xl], pright.at[k, 0], d_xl)
+        px[0] = send(p.base + M_X + 0, g.at[k, xo, first], prelay.at[k, 0], d_xr)
+        px[3] = send(p.base + M_X + 3, g.at[k, xl, first], pright.at[k, 0], d_xl)
         for j in range(3, 5):
             body(j)
-        px[2] = send(p.base + M_X + 2, g.at[k, second, xo], prelay.at[k, 1], d_xl)
-        px[1] = send(p.base + M_X + 1, g.at[k, second, xr], pleft.at[k, 1], d_xr)
+        px[2] = send(p.base + M_X + 2, g.at[k, xo, second], prelay.at[k, 1], d_xl)
+        px[1] = send(p.base + M_X + 1, g.at[k, xr, second], pleft.at[k, 1], d_xr)
 
     def x_relay(p, half):
         k, px = p.k, p.px
         which, to, dev, into = ((first, xr, d_xr, pleft), (second, xl, d_xl, pright))[half]
         px[2 * half].wait_recv()
-        g[k, which, to] = (g[k, which, to].astype(F32) + prelay[k, half].astype(F32)).astype(BF16)
-        px[4 + half] = send(p.base + M_X + 4 + half, g.at[k, which, to], into.at[k, half], dev)
+        g[k, to, which] = (g[k, to, which].astype(F32) + prelay[k, half].astype(F32)).astype(BF16)
+        px[4 + half] = send(p.base + M_X + 4 + half, g.at[k, to, which], into.at[k, half], dev)
 
     def x_sum(p):
         k, px = p.k, p.px
@@ -281,7 +263,7 @@
 
         def three(half, s, z):
             return (
-                g[k, 5 * half + s, x, z].astype(F32)
+                g[k, x, 5 * half + s, z].astype(F32)
                 + pleft[k, half, s, z].astype(F32)
                 + pright[k, half, s, z].astype(F32)
             )
@@ -329,16 +311,16 @@
             mixed = mixed + mdot(w, pool_v[256 * b : 256 * b + 256])
         head_out = (mixed[:, 0:128] / mixed[:, 128:256]).astype(BF16)
         for s in range(8):
-            ho[k, c, s // 4, :, (s % 4) * HD : (s % 4 + 1) * HD] = head_out[s * RB : (s + 1) * RB]
+            ho[k, x, core, zh, s // 4, :, (s % 4) * HD : (s % 4 + 1) * HD] = head_out[s * RB : (s + 1) * RB]
         p.hog.start()
 
     def out_rows(p):
         k, oy = p.k, p.oy
         p.hog.finish()
-        lhs = [ho[k, :, f].reshape(16 * RB, 512) for f in range(2)]
+        lhs = [ho[k, :, :, :, f].reshape(16 * RB, 512) for f in range(2)]
         for n in range(2):
             res = mdot(lhs[0], wob[n, 0:512]) + mdot(lhs[1], wob[n, 512:1024])
-            o[k, :, :, :, n * 256 : (n + 1) * 256] = res.astype(BF16).reshape(4, 2, 2 * RB, 256)
+            o[k, :, :, :, :, n * 256 : (n + 1) * 256] = res.astype(BF16).reshape(4, 2, 2, RB, 256)
         oy[0] = send(p.base + M_Y + 0, o.at[k, yo, 0], orelay.at[k, 0], d_yr)
         oy[2] = send(p.base + M_Y + 2, o.at[k, yo, 1], orelay.at[k, 1], d_yl)
         oy[1] = send(p.base + M_Y + 1, o.at[k, yr, 1], oleft.at[k, 1], d_yr)
@@ -356,9 +338,9 @@
         for i in (1, 3, 4, 5):
             oy[i].wait_recv()
 
-        for z in range(2):
-            ozs[k, z] = (
-                o[k, y, z].astype(F32) + oleft[k, z].astype(F32) + oright[k, z].astype(F32)
+        for i in range(2):
+            ozs[k, i] = (
+                o[k, y, i].astype(F32) + oleft[k, i].astype(F32) + oright[k, i].astype(F32)
             ).astype(BF16)
         p.oz = send(p.base + M_ZL, ozs.at[k], ozr.at[k], d_zl)
 
@@ -368,13 +350,12 @@
         steps = pl.ds(k * TS, TS)
         for z in range(2):
             for i in range(2):
-                rows = pl.ds(i * RB, RB)
-                full = ozs[k, z, rows].astype(F32) + ozr[k, z, rows].astype(F32)
+                full = ozs[k, i, z].astype(F32) + ozr[k, i, z].astype(F32)
                 hidden = xb[steps, cidx(y, z, i)].astype(F32)
-                out[steps, 2 * y + z, pl.ds(16 * i, 16), :] = (
+                ob[steps, 2 * y + z, pl.ds(16 * i, 16), :] = (
                     hidden + full.reshape(TS, 16, 512)
                 ).astype(BF16)
-        own = out.at[steps, pl.ds(2 * y, 2)]
+        own = ob.at[steps, pl.ds(2 * y, 2)]
         p.fo = {
             1: send(p.base + M_FO, own, own, d_yr),
             2: send(p.base + M_FO + 1, own, own, d_yl),
@@ -382,15 +363,19 @@
 
     def pass_on(p, k):
         steps = pl.ds(p.k * TS, TS)
-        p.fo[k].wait_recv()
         if k == 1:
-            part = out.at[steps, 2 * yl]
+            p.fo[1].wait_recv()
+            part = ob.at[steps, 2 * yl]
             p.fo[5] = send(p.base + M_FO + 2, part, part, d_yr)
         elif k == 2:
-            part = out.at[steps, 2 * yr + 1]
+            p.fo[2].wait_recv()
+            part = ob.at[steps, 2 * yr + 1]
             p.fo[6] = send(p.base + M_FO + 3, part, part, d_yl)
         else:
+            p.fo[5].wait_recv()
             p.fo[6].wait_recv()
+            p.done = pltpu.make_async_copy(ob.at[steps], out.at[steps], lsem.at[15 + p.k])
+            p.done.start()
 
     def load_weights():
         for k in range(3, 8):
@@ -401,21 +386,26 @@
 
     def sum_squares():
         lax.fori_loop(0, 16, squares, 0, unroll=4)
-
-        def sq_send(d, carry):
-            sq_msg(d).start()
-            return carry
-
-        lax.fori_loop(1, 16, sq_send, 0)
-
-    def inverse_rms():
-        def sq_wait(d, carry):
-            sq_msg(d).wait_recv()
-            return carry
-
-        lax.fori_loop(1, 16, sq_wait, 0)
-        sqr[c] = sqs[c]
-        flat = jnp.sum(sqr[...], axis=0)[0:1, :]
+        return [send(SQ0, sqs.at[1 - core], sqc, d_c)]
+
+    def sum_squares_x(before):
+        before[0].wait_recv()
+        sqx[...] = sqs[core] + sqc[...]
+        return [
+            send(SQ0 + 1, sqx.at[xr], sqn.at[0], d_xr),
+            send(SQ0 + 2, sqx.at[xl], sqn.at[1], d_xl),
+            send(SQ0 + 3, sqx.at[xo], sqn.at[2], d_xo),
+        ]
+
+    def sum_squares_z(before):
+        for m in before:
+            m.wait_recv()
+        sqz[...] = sqx[x] + sqn[0] + sqn[1] + sqn[2]
+        return [send(SQ0 + 4, sqz.at[1 - zh], sqr, d_z)]
+
+    def inverse_rms(before):
+        before[0].wait_recv()
+        flat = (sqz[zh] + sqr[...])[0:1, :]
         row_sq = jnp.sum(jnp.where(eye, flat, 0.0), axis=1, keepdims=True)
         return lax.rsqrt(row_sq / D + 1e-05)
 
@@ -477,8 +467,9 @@
 
         def take(b, carry):
             rows = pl.ds(pl.multiple_of(128 * b, 128), 128)
-            pool_k[rows] = mdot(chosen[b], kv[0, b]).astype(BF16)
-            pool_v[rows, 0:128] = mdot(chosen[b], kv[1, b]).astype(BF16)
+            block = (b // 4, lax.rem(b, 2), lax.rem(b // 2, 2))
+            pool_k[rows] = mdot(chosen[b], kv[block + (0,)]).astype(BF16)
+            pool_v[rows, 0:128] = mdot(chosen[b], kv[block + (1,)]).astype(BF16)
             return carry
 
         lax.fori_loop(0, 16, take, 0, unroll=8)
@@ -489,6 +480,8 @@
         b_id = lax.broadcasted_iota(jnp.int32, (64, 64), 1)
         col_id = lax.broadcasted_iota(jnp.int32, (64, 128), 1)
         p_id = lax.broadcasted_iota(jnp.int32, (64, 128), 0)
+        spot = (p_id // 16) * 16 + lax.rem(p_id // 4, 2) * 8 + lax.rem(p_id // 8, 2) * 4
+        spot = (spot + lax.rem(p_id, 4)).astype(F32)
         rows = []
         for n in range(4):
             a = 4 * c + n
@@ -498,13 +491,13 @@
             before = mdot((b_id < a_id).astype(BF16), readable.astype(BF16))
             place = jnp.where(p_id == a, 0.0, before + 1.0).astype(jnp.int32)
             hit = (place == col_id) & ((readable > 0.5) | (p_id == a))
-            line = jnp.sum(jnp.where(hit, p_id.astype(F32), 0.0), axis=0, keepdims=True)
+            line = jnp.sum(jnp.where(hit, spot, 0.0), axis=0, keepdims=True)
             count = jnp.sum(readable, axis=0, keepdims=True) + 1.0
             rows.append(jnp.where(col_id[0:1] == 127, count, line))
         picks[...] = jnp.concatenate(rows + rows, axis=0).astype(jnp.int32)
 
     keep = pltpu.make_async_copy(kv, kv_out, lsem.at[10])
-    rms = []
+    rms, squared = [], []
     late = [loads[8], loads[9]]
 
     def step(event):
@@ -514,12 +507,14 @@
                 kvg.finish()
                 keep.start()
             else:
-                kvg.take(int(what[1]))
+                kvg.take(what)
             return
         if who == "all":
-            {"sq": sum_squares, "mask": choose_pages, "take": take_pages, "list": list_pages}[
-                what
-            ]()
+            if what[:2] == "sq":
+                stage = {"sq": sum_squares, "sq1": sum_squares_x, "sq2": sum_squares_z}[what]
+                squared[:] = stage(squared) if squared else stage()
+            else:
+                {"mask": choose_pages, "take": take_pages, "list": list_pages}[what]()
             return
         p = parts[int(who[1])]
         if what == "other":
@@ -537,35 +532,31 @@
                 x_relay(p, int(what[2]) // 2)
         elif what == "att":
             if not rms:
-                rms.append(inverse_rms())
+                rms.append(inverse_rms(squared))
             attend(p, rms[0])
         elif what[0] == "h":
-            p.hog.take(int(what[1]))
+            p.hog.take(what[1])
         elif what == "out":
             while late:
                 late.pop().wait()
             out_rows(p)
         elif what == "ysum":
+            drain(10)
             y_sum(p)
         elif what[0] == "y":
             y_relay(p, int(what[2]) // 2)
         elif what == "add":
             add_input(p)
         else:
+            drain(6)
             pass_on(p, int(what[1]))
 
     for event in ORDER:
         step(event)
     keep.wait()
-
-    for m in sent:
-        m.wait_send()
-
-    def sq_done(d, carry):
-        sq_msg(d).wait_send()
-        return carry
-
-    lax.fori_loop(1, 16, sq_done, 0)
+    drain(0)
+    for p in parts:
+        p.done.wait()
 
 
 def layer_call(*args):
@@ -574,29 +565,34 @@
     return pl.pallas_call(
         layer_kernel,
         out_shape=(
-            jax.ShapeDtypeStruct((2, 16, 256, HD), BF16),
+            jax.ShapeDtypeStruct((4, 2, 2, 2, 256, HD), BF16),
             jax.ShapeDtypeStruct((8, 128), jnp.int32),
             jax.ShapeDtypeStruct((4, 8, 32, 512), BF16),
         ),
         in_specs=[hbm] * 10,
-        out_specs=(hbm, vmem, vmem),
+        out_specs=(hbm, vmem, hbm),
         scratch_shapes=[
+            pltpu.VMEM((4, 8, 32, 512), BF16),
             pltpu.VMEM((64, 64), jnp.int32),
             pltpu.VMEM((8, 256), jnp.int32),
             pltpu.SMEM((256,), jnp.int32),
             pltpu.VMEM((4, 128), BF16),
-            pltpu.VMEM((2, 16, 256, HD), BF16),
+            pltpu.VMEM((4, 2, 2, 2, 256, HD), BF16),
             pltpu.VMEM((4, 16, 16, 512), BF16),
             pltpu.VMEM((5, 512, 256), BF16),
             pltpu.VMEM((1024, 128), BF16),
             pltpu.VMEM((1024, 128), F32),
             pltpu.VMEM((2, 1024, 256), BF16),
             pltpu.VMEM((NCH, 2, 8, RB, 512), BF16),
-            pltpu.VMEM((16, 8, 128), F32),
-            pltpu.VMEM((16, 8, 128), F32),
+            pltpu.VMEM((2, 4, 2, 8, 128), F32),
+            pltpu.VMEM((4, 2, 8, 128), F32),
+            pltpu.VMEM((4, 2, 8, 128), F32),
+            pltpu.VMEM((3, 2, 8, 128), F32),
+            pltpu.VMEM((2, 8, 128), F32),
+            pltpu.VMEM((8, 128), F32),
             pltpu.VMEM((NCH, 10, 4, 2, RB, 128), BF16),
             pltpu.VMEM((NCH, 10, 4, 2, RB, 128), BF16),
-            pltpu.VMEM((NCH, 10, 4, 2, RB, 128), BF16),
+            pltpu.VMEM((NCH, 4, 10, 2, RB, 128), BF16),
             pltpu.VMEM((NCH, 2, 5, 2, RB, 128), BF16),
             pltpu.VMEM((NCH, 2, 5, 2, RB, 128), BF16),
             pltpu.VMEM((NCH, 2, 5, 2, RB, 128), BF16),
@@ -611,14 +607,14 @@
             pltpu.VMEM((2048, HD), BF16),
             pltpu.VMEM((2048, 2 * HD), BF16),
             pltpu.VMEM((8, 8 * RB, 256), F32),
-            pltpu.VMEM((NCH, 16, 2, RB, 512), BF16),
-            pltpu.VMEM((NCH, 4, 2, 2 * RB, 512), BF16),
-            pltpu.VMEM((NCH, 2, 2 * RB, 512), BF16),
-            pltpu.VMEM((NCH, 2, 2 * RB, 512), BF16),
-            pltpu.VMEM((NCH, 2, 2 * RB, 512), BF16),
-            pltpu.VMEM((NCH, 2, 2 * RB, 512), BF16),
-            pltpu.VMEM((NCH, 2, 2 * RB, 512), BF16),
-            pltpu.SemaphoreType.DMA((15,)),
+            pltpu.VMEM((NCH, 4, 2, 2, 2, RB, 512), BF16),
+            pltpu.VMEM((NCH, 4, 2, 2, RB, 512), BF16),
+            pltpu.VMEM((NCH, 2, 2, RB, 512), BF16),
+            pltpu.VMEM((NCH, 2, 2, RB, 512), BF16),
+            pltpu.VMEM((NCH, 2, 2, RB, 512), BF16),
+            pltpu.VMEM((NCH, 2, 2, RB, 512), BF16),
+            pltpu.VMEM((NCH, 2, 2, RB, 512), BF16),
+            pltpu.SemaphoreType.DMA((15 + NCH,)),
             pltpu.SemaphoreType.DMA((NMSG,)),
             pltpu.SemaphoreType.DMA((NMSG,)),
         ],
@@ -632,7 +628,7 @@
 def prefill_kernel(
     q_hbm, kv_ref, picks, dec_ref, out_hbm, dec_out, q_ref, kv, stage, out, peaks, mixes, sem
 ):
-    loads = [pltpu.make_async_copy(kv_ref.at[i], kv.at[i], sem.at[i]) for i in range(2)]
+    loads = [pltpu.make_async_copy(kv_ref, kv, sem.at[0])]
     loads.append(pltpu.make_async_copy(q_hbm, q_ref, sem.at[2]))
     fetched = pltpu.make_async_copy(dec_ref, stage, sem.at[3])
     moved = pltpu.make_async_copy(stage, dec_out, sem.at[4])
@@ -641,8 +637,9 @@
     fetched.start()
 
     def attend(n, start, pages, state):
-        keys = jnp.concatenate([kv[0, picks[n, start + k]] for k in range(pages)], axis=0)
-        values = jnp.concatenate([kv[1, picks[n, start + k]] for k in range(pages)], axis=0)
+        spots = [picks[n, start + k] for k in range(pages)]
+        keys = jnp.concatenate([kv[p // 4, 0, lax.rem(p, 4)] for p in spots], axis=0)
+        values = jnp.concatenate([kv[p // 4, 1, lax.rem(p, 4)] for p in spots], axis=0)
         values = jnp.concatenate([values, jnp.ones((pages * PAGE, 128), BF16)], axis=1)
         q = jnp.concatenate([q_ref[n, :, s * HD : (s + 1) * HD] for s in range(8)], axis=0)
         i_id = lax.broadcasted_iota(jnp.int32, (512, pages * PAGE), 0)
@@ -708,7 +705,7 @@
         out_specs=(hbm, hbm),
         scratch_shapes=[
             pltpu.VMEM((4, PAGE, 1024), BF16),
-            pltpu.VMEM((2, 64, PAGE, HD), BF16),
+            pltpu.VMEM((16, 2, 4, PAGE, HD), BF16),
             pltpu.VMEM(dec.shape, BF16),
             pltpu.VMEM((4, PAGE, 1024), BF16),
             pltpu.VMEM((4, 512, 128), F32),
@@ -730,7 +727,7 @@
         w_keyval.reshape(1024, 128), w_out,
     )
     prefill_out, dec_out = prefill_call(
-        prefill_query.reshape(4, PAGE, 1024), kv.reshape(2, 64, PAGE, HD), picks, dec
+        prefill_query.reshape(4, PAGE, 1024), kv.reshape(16, 2, 4, PAGE, HD), picks, dec
     )
     return prefill_out.reshape(256, 1024), dec_out.reshape(4, 256, 512)
 

time: 83.2 us -> 82.8 us (level)
  the two profiles are of different devices: /device:TPU:0 before, /device:TPU:6 now
where the time goes in v4:
time: 82.8 us; the launch traced here: 82.7 us
  Pallas kernels  82.1 us (99%)
    pallas_call x1, Pallas kernels, layer_call(): pl.pallas_call(layer_kernel, out_shape=(jax.ShapeDtypeStruct((4, 2, 2, 2,...  73.6 us
    pallas_call x1, Pallas kernels, prefill_call(): pl.pallas_call(prefill_kernel, out_shape=(jax.ShapeDtypeStruct((4, PAGE,...  8.45 us

profile of v4, /device:TPU:6, one launch (start us, length us, event | category | flops | bytes accessed | tf_op | source)
XLA Modules:
  0.0 82.7 jit_solution(6530901290080217022)
XLA Ops:
  0.6 73.6 %layer.1 = (bf16[4,2,2,2,256,128]{5,4,3,2,1,0:T(8,128)(2,1)}, s32[8,128]{1,0:T(8,128)}, bf16[4,8,32,512]{3,2,1,0:T(8,128)(2,1)}) custom-call(bf16[256,128]{1,0:T(8,128)(2,1)} %key_ref.1, bf16[256,128]{1,0:T(8,128)(2,1)} %val_ref.1, s32[64,64]{1,0:T(8,128)} %mask_hbm.1, s32[8,256]{1,0:T(8,128)} %bitcast.12, s32[256]{0:T(256)} %clen_hbm.1, ...), custom_call_target="tpu_custom_call" | custom-call | tf_op jit(solution)/shard_map/layer/pallas_call | solution.py:565
  74.2 8.5 %prefill.1 = (bf16[4,64,1024]{2,1,0:T(8,128)(2,1)}, bf16[4,8,32,512]{3,2,1,0:T(8,128)(2,1)}) custom-call(bf16[4,64,1024]{2,1,0:T(8,128)(2,1)} %bitcast.10, bf16[16,2,4,64,128]{4,3,2,1,0:T(8,128)(2,1)} %bitcast.8, s32[8,128]{1,0:T(8,128)} %get-tuple-element.8.picks, bf16[4,8,32,512]{3,2,1,0:T(8,128)(2,1)} %get-tuple-element.9.dec_ref), custom_call_target="tpu_custom_call" | custom-call | tf_op jit(solution)/shard_map/prefill/pallas_call | solution.py:698

commit v5 on v4

--- a/solution.py
+++ b/solution.py
@@ -20,24 +20,24 @@
 RB = 16 * TS
 
 KV0 = 0
-SQ0 = 11
-PART0 = 16
-M_CORE, M_X, M_Z, M_HO, M_Y, M_ZL, M_FO = 0, 1, 7, 8, 17, 23, 24
-PART_MSGS = 28
+SQ0 = 12
+PART0 = 17
+M_CORE, M_X, M_Z, M_HO, M_Y, M_ZL, M_FO = 0, 1, 5, 6, 15, 19, 20
+PART_MSGS = 24
 NMSG = PART0 + NCH * PART_MSGS
 
 
 ORDER = (
-    "p0.other", "all.sq", "p1.other", "p0.own", "kv.z", "p1.own", "p0.xr2", "all.sq1", "p0.xr0",
-    "p2.other", "p3.other", "kv.l", "kv.r", "p1.xr0", "p2.own", "p1.xr2", "p0.xsum", "p3.own",
-    "all.mask", "kv.f", "all.sq2", "p2.xr2", "p1.xsum", "p2.xr0", "kv.fin", "all.take",
-    "p0.att", "p2.xsum", "p3.xr0", "p3.xr2", "p1.att", "p0.hz", "p2.att", "p3.xsum", "p0.hl",
-    "p0.hr", "p1.hz", "p2.hz", "p0.hf", "p3.att", "p1.hl", "p1.hr", "p2.hl", "p2.hr", "p0.out",
-    "p1.hf", "p3.hz", "all.list", "p2.hf", "p1.out", "p3.hl", "p3.hr", "p2.out", "p0.yr0",
-    "p3.hf", "p0.yr2", "p1.yr2", "p1.yr0", "p3.out", "p0.ysum", "p2.yr0", "p2.yr2", "p1.ysum",
-    "p3.yr0", "p3.yr2", "p2.ysum", "p0.add", "p3.ysum", "p1.add", "p2.add", "p3.add", "p0.f2",
-    "p1.f1", "p1.f2", "p0.f1", "p2.f1", "p2.f2", "p3.f2", "p3.f1", "p0.f5", "p1.f5", "p2.f5",
-    "p3.f5",
+    "p0.other", "p1.other", "all.sq", "p0.own", "kv.r", "p2.other", "kv.l", "p3.other",
+    "p0.xr0", "p0.xr2", "p1.own", "kv.f", "p2.own", "p3.own", "kv.s", "all.sq1", "p1.xr0",
+    "kv.z", "p0.xsum", "kv.m", "p1.xr2", "all.sq2", "p3.xr0", "p3.xr2", "p2.xr2", "p2.xr0",
+    "kv.o", "all.mask", "kv.fin", "p1.xsum", "all.take", "p0.att", "p2.xsum", "p3.xsum",
+    "p1.att", "p0.hz", "p2.att", "p1.hz", "p0.hl", "p0.hr", "p3.att", "p2.hz", "p0.hf", "p1.hr",
+    "p1.hl", "p0.out", "p3.hz", "p1.hf", "p2.hr", "p2.hl", "p1.out", "p3.hl", "p2.hf", "p3.hr",
+    "p0.yr2", "p0.yr0", "p2.out", "p3.hf", "p1.yr2", "p1.yr0", "p3.out", "p0.ysum", "p2.yr2",
+    "p2.yr0", "p1.ysum", "p3.yr0", "p3.yr2", "p0.add", "p2.ysum", "p1.add", "p3.ysum", "p0.f1",
+    "p0.f2", "p2.add", "p3.add", "p1.f1", "p1.f2", "p2.f1", "p2.f2", "p3.f1", "p3.f2", "p1.f5",
+    "p2.f5", "all.list", "p0.f5", "p3.f5",
 )
 
 
@@ -128,38 +128,58 @@
         while len(sent) > left:
             sent.pop(0).wait_send()
 
+    def pass_to(msgs, base, k, ref, dev):
+        msgs[k] = send(base + k, ref, ref, dev)
+
+    kvm = {}
+
+    def kv_start():
+        own = kv.at[x, core, zh]
+        pass_to(kvm, KV0, 1, own, d_xr)
+        pass_to(kvm, KV0, 2, own, d_xl)
+        pass_to(kvm, KV0, 0, own, d_z)
+
+    def kv_pass(what):
+        if what == "l":
+            kvm[1].wait_recv()
+            pass_to(kvm, KV0, 3, kv.at[xl, core, zh, 0], d_xr)
+            pass_to(kvm, KV0, 5, kv.at[xl, core, zh], d_z)
+        elif what == "r":
+            kvm[2].wait_recv()
+            pass_to(kvm, KV0, 4, kv.at[xr, core, zh, 1], d_xl)
+            pass_to(kvm, KV0, 6, kv.at[xr, core, zh], d_z)
+        elif what == "f":
+            kvm[3].wait_recv()
+            kvm[4].wait_recv()
+            pass_to(kvm, KV0, 7, kv.at[xo, core, zh], d_z)
+        else:
+            waited, given, place = {"z": (0, 8, x), "m": (5, 9, xl), "s": (6, 10, xr), "o": (7, 11, xo)}[
+                what
+            ]
+            kvm[waited].wait_recv()
+            pass_to(kvm, KV0, given, kv.at[place, core], d_c)
+
     class Gather:
-        def __init__(self, base, pair, early):
-            self.base, self.pair, self.early = base, pair, early
-            self.m = {}
+        def __init__(self, base, pair):
+            self.base, self.pair, self.m = base, pair, {}
 
         def put(self, k, ref, dev):
-            self.m[k] = send(self.base + k, ref, ref, dev)
+            pass_to(self.m, self.base, k, ref, dev)
 
         def start(self):
-            own = self.pair(x).at[zh]
-            self.put(0, own, d_z)
-            if self.early:
-                self.put(9, own, d_xr)
-                self.put(10, own, d_xl)
+            self.put(0, self.pair(x).at[zh], d_z)
 
         def take(self, which):
             if which == "z":
                 self.m[0].wait_recv()
-                ref = self.pair(x)
-                part = ref.at[1 - zh] if self.early else ref
-                self.put(1, part, d_xr)
-                self.put(2, part, d_xl)
-                self.put(5, ref, d_c)
+                self.put(1, self.pair(x), d_xr)
+                self.put(2, self.pair(x), d_xl)
+                self.put(5, self.pair(x), d_c)
             elif which == "l":
-                if self.early:
-                    self.m[9].wait_recv()
                 self.m[1].wait_recv()
                 self.put(3, self.pair(xl).at[0], d_xr)
                 self.put(6, self.pair(xl), d_c)
             elif which == "r":
-                if self.early:
-                    self.m[10].wait_recv()
                 self.m[2].wait_recv()
                 self.put(4, self.pair(xr).at[1], d_xl)
                 self.put(7, self.pair(xr), d_c)
@@ -172,10 +192,9 @@
             for k in range(5, 9):
                 self.m[k].wait_recv()
 
-    kvg = Gather(KV0, lambda a: kv.at[a, core], True)
     loads[0].wait()
     loads[1].wait()
-    kvg.start()
+    kv_start()
 
     loads[2].wait()
     loads[10].wait()
@@ -214,7 +233,7 @@
         p.k = k
         p.base = PART0 + k * PART_MSGS
         p.px, p.oy = {}, {}
-        p.hog = Gather(p.base + M_HO, lambda a, k=k: ho.at[k, a, core], False)
+        p.hog = Gather(p.base + M_HO, lambda a, k=k: ho.at[k, a, core])
         parts.append(p)
 
     def other_rows(p):
@@ -242,38 +261,36 @@
 
         for j in range(3):
             body(j)
-        px[0] = send(p.base + M_X + 0, g.at[k, xo, first], prelay.at[k, 0], d_xr)
-        px[3] = send(p.base + M_X + 3, g.at[k, xl, first], pright.at[k, 0], d_xl)
+        px[0] = send(p.base + M_X, g.at[k, xo, first], prelay.at[k, 0], d_xr)
         for j in range(3, 5):
             body(j)
-        px[2] = send(p.base + M_X + 2, g.at[k, xo, second], prelay.at[k, 1], d_xl)
-        px[1] = send(p.base + M_X + 1, g.at[k, xr, second], pleft.at[k, 1], d_xr)
-
-    def x_relay(p, half):
+        px[1] = send(p.base + M_X + 1, g.at[k, xo, second], prelay.at[k, 1], d_xl)
+
+    def x_relay(p, side):
         k, px = p.k, p.px
-        which, to, dev, into = ((first, xr, d_xr, pleft), (second, xl, d_xl, pright))[half]
-        px[2 * half].wait_recv()
-        g[k, to, which] = (g[k, to, which].astype(F32) + prelay[k, half].astype(F32)).astype(BF16)
-        px[4 + half] = send(p.base + M_X + 4 + half, g.at[k, to, which], into.at[k, half], dev)
+        which, to, dev, into = ((first, xr, d_xr, pleft), (second, xl, d_xl, pright))[side]
+        px[side].wait_recv()
+        g[k, to, which] = (g[k, to, which].astype(F32) + prelay[k, side].astype(F32)).astype(BF16)
+        px[2 + side] = send(p.base + M_X + 2 + side, g.at[k, to], into.at[k], dev)
 
     def x_sum(p):
         k, px = p.k, p.px
-        for i in (1, 3, 4, 5):
-            px[i].wait_recv()
-
-        def three(half, s, z):
+        px[2].wait_recv()
+        px[3].wait_recv()
+
+        def three(s, z):
             return (
-                g[k, x, 5 * half + s, z].astype(F32)
-                + pleft[k, half, s, z].astype(F32)
-                + pright[k, half, s, z].astype(F32)
+                g[k, x, s, z].astype(F32)
+                + pleft[k, s, z].astype(F32)
+                + pright[k, s, z].astype(F32)
             )
 
         for s in range(10):
-            zs[k, s] = three(s // 5, s % 5, 1 - zh).astype(BF16)
+            zs[k, s] = three(s, 1 - zh).astype(BF16)
         p.zp = send(p.base + M_Z, zs.at[k], zr.at[k], d_z)
 
         for s in range(10):
-            rf[k, s] = three(s // 5, s % 5, zh)
+            rf[k, s] = three(s, zh)
 
     def attend(p, inverse):
         k = p.k
@@ -321,22 +338,20 @@
         for n in range(2):
             res = mdot(lhs[0], wob[n, 0:512]) + mdot(lhs[1], wob[n, 512:1024])
             o[k, :, :, :, :, n * 256 : (n + 1) * 256] = res.astype(BF16).reshape(4, 2, 2, RB, 256)
-        oy[0] = send(p.base + M_Y + 0, o.at[k, yo, 0], orelay.at[k, 0], d_yr)
-        oy[2] = send(p.base + M_Y + 2, o.at[k, yo, 1], orelay.at[k, 1], d_yl)
-        oy[1] = send(p.base + M_Y + 1, o.at[k, yr, 1], oleft.at[k, 1], d_yr)
-        oy[3] = send(p.base + M_Y + 3, o.at[k, yl, 0], oright.at[k, 0], d_yl)
-
-    def y_relay(p, half):
+        oy[0] = send(p.base + M_Y, o.at[k, yo, 0], orelay.at[k, 0], d_yr)
+        oy[1] = send(p.base + M_Y + 1, o.at[k, yo, 1], orelay.at[k, 1], d_yl)
+
+    def y_relay(p, side):
         k, oy = p.k, p.oy
-        to, dev, into = ((yr, d_yr, oleft), (yl, d_yl, oright))[half]
-        oy[2 * half].wait_recv()
-        o[k, to, half] = (o[k, to, half].astype(F32) + orelay[k, half].astype(F32)).astype(BF16)
-        oy[4 + half] = send(p.base + M_Y + 4 + half, o.at[k, to, half], into.at[k, half], dev)
+        to, dev, into = ((yr, d_yr, oleft), (yl, d_yl, oright))[side]
+        oy[side].wait_recv()
+        o[k, to, side] = (o[k, to, side].astype(F32) + orelay[k, side].astype(F32)).astype(BF16)
+        oy[2 + side] = send(p.base + M_Y + 2 + side, o.at[k, to], into.at[k], dev)
 
     def y_sum(p):
         k, oy = p.k, p.oy
-        for i in (1, 3, 4, 5):
-            oy[i].wait_recv()
+        oy[2].wait_recv()
+        oy[3].wait_recv()
 
         for i in range(2):
             ozs[k, i] = (
@@ -504,10 +519,11 @@
         who, what = event.split(".")
         if who == "kv":
             if what == "fin":
-                kvg.finish()
+                for k in range(8, 12):
+                    kvm[k].wait_recv()
                 keep.start()
             else:
-                kvg.take(what)
+                kv_pass(what)
             return
         if who == "all":
             if what[:2] == "sq":
@@ -594,8 +610,8 @@
             pltpu.VMEM((NCH, 10, 4, 2, RB, 128), BF16),
             pltpu.VMEM((NCH, 4, 10, 2, RB, 128), BF16),
             pltpu.VMEM((NCH, 2, 5, 2, RB, 128), BF16),
-            pltpu.VMEM((NCH, 2, 5, 2, RB, 128), BF16),
-            pltpu.VMEM((NCH, 2, 5, 2, RB, 128), BF16),
+            pltpu.VMEM((NCH, 10, 2, RB, 128), BF16),
+            pltpu.VMEM((NCH, 10, 2, RB, 128), BF16),
             pltpu.VMEM((NCH, 10, RB, 128), BF16),
             pltpu.VMEM((NCH, 10, RB, 128), BF16),
             pltpu.VMEM((NCH, 10, RB, 128), F32),
@@ -642,12 +658,14 @@
         values = jnp.concatenate([kv[p // 4, 1, lax.rem(p, 4)] for p in spots], axis=0)
         values = jnp.concatenate([values, jnp.ones((pages * PAGE, 128), BF16)], axis=1)
         q = jnp.concatenate([q_ref[n, :, s * HD : (s + 1) * HD] for s in range(8)], axis=0)
-        i_id = lax.broadcasted_iota(jnp.int32, (512, pages * PAGE), 0)
-        j_id = lax.broadcasted_iota(jnp.int32, (512, pages * PAGE), 1)
-        allowed = j_id < (picks[n, 127] - start) * PAGE
+        j_id = lax.broadcasted_iota(jnp.int32, (1, pages * PAGE), 1)
+        hidden = jnp.where(j_id < (picks[n, 127] - start) * PAGE, 0.0, NEG)
+        s = rdot(q, keys) * SCALE + hidden
         if state is None:
-            allowed = allowed & ((j_id >= PAGE) | (j_id <= lax.rem(i_id, PAGE)))
-        s = jnp.where(allowed, rdot(q, keys) * SCALE, NEG)
+            i_id = lax.broadcasted_iota(jnp.int32, (512, 128), 0)
+            j_id = lax.broadcasted_iota(jnp.int32, (512, 128), 1)
+            seen = (j_id >= PAGE) | (j_id <= lax.rem(i_id, PAGE))
+            s = jnp.concatenate([jnp.where(seen, s[:, :128], NEG), s[:, 128:]], axis=1)
         peak = jnp.max(s, axis=1, keepdims=True)
         if state is not None:
             peak = jnp.maximum(peak, state[0])
@@ -661,15 +679,20 @@
         for s in range(8):
             out[n, :, s * HD : (s + 1) * HD] = result[s * 64 : (s + 1) * 64]
 
+    def leave(n):
+        return pltpu.make_async_copy(out.at[n], out_hbm.at[n], sem.at[5 + n])
+
     for copy in loads:
         copy.wait()
-    fetched.wait()
-    moved.start()
     for n in range(4):
         peak, mixed = attend(n, 0, 8, None)
         peaks[n] = jnp.broadcast_to(peak, (512, 128))
         mixes[n] = mixed
         write(n, mixed)
+        leave(n).start()
+        if n == 0:
+            fetched.wait()
+            moved.start()
 
     def deep(n, carry):
         @pl.when(picks[n, 127] > 8)
@@ -681,14 +704,15 @@
                 return inner
 
             lax.fori_loop(0, (picks[n, 127] - 5) // 4, more, 0)
+            leave(n).wait()
             write(n, mixes[n])
+            leave(n).start()
 
         return carry
 
     lax.fori_loop(0, 4, deep, 0)
-    done = pltpu.make_async_copy(out, out_hbm, sem.at[5])
-    done.start()
-    done.wait()
+    for n in range(4):
+        leave(n).wait()
     moved.wait()
 
 
@@ -710,7 +734,7 @@
             pltpu.VMEM((4, PAGE, 1024), BF16),
             pltpu.VMEM((4, 512, 128), F32),
             pltpu.VMEM((4, 512, 256), F32),
-            pltpu.SemaphoreType.DMA((6,)),
+            pltpu.SemaphoreType.DMA((9,)),
         ],
         compiler_params=pltpu.CompilerParams(vmem_limit_bytes=62 * 1024 * 1024),
         name="prefill",

time: 82.8 us -> 75.7 us (0.914)
  the two profiles are of different devices: /device:TPU:6 before, /device:TPU:0 now
where the time goes in v5:
time: 75.7 us; the launch traced here: 74.3 us
  Pallas kernels  73.7 us (97%)
    pallas_call x1, Pallas kernels, layer_call(): pl.pallas_call(layer_kernel, out_shape=(jax.ShapeDtypeStruct((4, 2, 2, 2,...  68.3 us
    pallas_call x1, Pallas kernels, prefill_call(): pl.pallas_call(prefill_kernel, out_shape=(jax.ShapeDtypeStruct((4, PAGE,...  5.4 us

profile of v5, /device:TPU:0, one launch (start us, length us, event | category | flops | bytes accessed | tf_op | source)
XLA Modules:
  0.0 74.3 jit_solution(3519636338669853659)
XLA Ops:
  0.6 68.3 %layer.1 = (bf16[4,2,2,2,256,128]{5,4,3,2,1,0:T(8,128)(2,1)}, s32[8,128]{1,0:T(8,128)}, bf16[4,8,32,512]{3,2,1,0:T(8,128)(2,1)}) custom-call(bf16[256,128]{1,0:T(8,128)(2,1)} %key_ref.1, bf16[256,128]{1,0:T(8,128)(2,1)} %val_ref.1, s32[64,64]{1,0:T(8,128)} %mask_hbm.1, s32[8,256]{1,0:T(8,128)} %bitcast.12, s32[256]{0:T(256)} %clen_hbm.1, ...), custom_call_target="tpu_custom_call" | custom-call | tf_op jit(solution)/shard_map/layer/pallas_call | solution.py:581
  68.9 5.4 %prefill.1 = (bf16[4,64,1024]{2,1,0:T(8,128)(2,1)}, bf16[4,8,32,512]{3,2,1,0:T(8,128)(2,1)}) custom-call(bf16[4,64,1024]{2,1,0:T(8,128)(2,1)} %bitcast.10, bf16[16,2,4,64,128]{4,3,2,1,0:T(8,128)(2,1)} %bitcast.8, s32[8,128]{1,0:T(8,128)} %get-tuple-element.8.picks, bf16[4,8,32,512]{3,2,1,0:T(8,128)(2,1)} %get-tuple-element.9.dec_ref), custom_call_target="tpu_custom_call" | custom-call | tf_op jit(solution)/shard_map/prefill/pallas_call | solution.py:722

commit v6 on v5

--- a/solution.py
+++ b/solution.py
@@ -642,21 +642,27 @@
 
 
 def prefill_kernel(
-    q_hbm, kv_ref, picks, dec_ref, out_hbm, dec_out, q_ref, kv, stage, out, peaks, mixes, sem
+    q_hbm, kv_ref, picks, dec_ref, out_hbm, dec_out, q_ref, kv, extra, stage, out, peaks, mixes, sem
 ):
-    loads = [pltpu.make_async_copy(kv_ref, kv, sem.at[0])]
-    loads.append(pltpu.make_async_copy(q_hbm, q_ref, sem.at[2]))
-    fetched = pltpu.make_async_copy(dec_ref, stage, sem.at[3])
-    moved = pltpu.make_async_copy(stage, dec_out, sem.at[4])
-    for copy in loads:
-        copy.start()
+    def page(n, k):
+        spot = picks[n, k]
+        return kv_ref.at[spot // 4, :, lax.rem(spot, 4)]
+
+    get_q = pltpu.make_async_copy(q_hbm, q_ref, sem.at[0])
+    fetched = pltpu.make_async_copy(dec_ref, stage, sem.at[1])
+    moved = pltpu.make_async_copy(stage, dec_out, sem.at[2])
+    get_q.start()
+    for n in range(4):
+        for k in range(8):
+            pltpu.make_async_copy(page(n, k), kv.at[n, k], sem.at[7 + n]).start()
     fetched.start()
 
     def attend(n, start, pages, state):
-        spots = [picks[n, start + k] for k in range(pages)]
-        keys = jnp.concatenate([kv[p // 4, 0, lax.rem(p, 4)] for p in spots], axis=0)
-        values = jnp.concatenate([kv[p // 4, 1, lax.rem(p, 4)] for p in spots], axis=0)
-        values = jnp.concatenate([values, jnp.ones((pages * PAGE, 128), BF16)], axis=1)
+        block = kv[n] if state is None else extra[...]
+        keys = block[:, 0].reshape(pages * PAGE, HD)
+        values = jnp.concatenate(
+            [block[:, 1].reshape(pages * PAGE, HD), jnp.ones((pages * PAGE, 128), BF16)], axis=1
+        )
         q = jnp.concatenate([q_ref[n, :, s * HD : (s + 1) * HD] for s in range(8)], axis=0)
         j_id = lax.broadcasted_iota(jnp.int32, (1, pages * PAGE), 1)
         hidden = jnp.where(j_id < (picks[n, 127] - start) * PAGE, 0.0, NEG)
@@ -680,17 +686,17 @@
             out[n, :, s * HD : (s + 1) * HD] = result[s * 64 : (s + 1) * 64]
 
     def leave(n):
-        return pltpu.make_async_copy(out.at[n], out_hbm.at[n], sem.at[5 + n])
-
-    for copy in loads:
-        copy.wait()
+        return pltpu.make_async_copy(out.at[n], out_hbm.at[n], sem.at[3 + n])
+
+    get_q.wait()
     for n in range(4):
+        pltpu.make_async_copy(kv.at[n], kv.at[n], sem.at[7 + n]).wait()
         peak, mixed = attend(n, 0, 8, None)
         peaks[n] = jnp.broadcast_to(peak, (512, 128))
         mixes[n] = mixed
         write(n, mixed)
         leave(n).start()
-        if n == 0:
+        if n == 1:
             fetched.wait()
             moved.start()
 
@@ -698,6 +704,9 @@
         @pl.when(picks[n, 127] > 8)
         def _():
             def more(t, inner):
+                for k in range(4):
+                    pltpu.make_async_copy(page(n, 8 + 4 * t + k), extra.at[k], sem.at[11]).start()
+                pltpu.make_async_copy(extra, extra, sem.at[11]).wait()
                 peak, mixed = attend(n, 8 + 4 * t, 4, (peaks[n][:, 0:1], mixes[n]))
                 peaks[n] = jnp.broadcast_to(peak, (512, 128))
                 mixes[n] = mixed
@@ -729,12 +738,13 @@
         out_specs=(hbm, hbm),
         scratch_shapes=[
             pltpu.VMEM((4, PAGE, 1024), BF16),
-            pltpu.VMEM((16, 2, 4, PAGE, HD), BF16),
+            pltpu.VMEM((4, 8, 2, PAGE, HD), BF16),
+            pltpu.VMEM((4, 2, PAGE, HD), BF16),
             pltpu.VMEM(dec.shape, BF16),
             pltpu.VMEM((4, PAGE, 1024), BF16),
             pltpu.VMEM((4, 512, 128), F32),
             pltpu.VMEM((4, 512, 256), F32),
-            pltpu.SemaphoreType.DMA((9,)),
+            pltpu.SemaphoreType.DMA((12,)),
         ],
         compiler_params=pltpu.CompilerParams(vmem_limit_bytes=62 * 1024 * 1024),
         name="prefill",

time: 75.7 us -> 76.1 us (level)
  no operation moved by 1% of the time
where the time goes in v6:
time: 76.1 us; the launch traced here: 75.1 us
  Pallas kernels  74.4 us (98%)
    pallas_call x1, Pallas kernels, layer_call(): pl.pallas_call(layer_kernel, out_shape=(jax.ShapeDtypeStruct((4, 2, 2, 2,...  68.3 us
    pallas_call x1, Pallas kernels, prefill_call(): pl.pallas_call(prefill_kernel, out_shape=(jax.ShapeDtypeStruct((4, PAGE,...  6.12 us

profile of v6, /device:TPU:0, one launch (start us, length us, event | category | flops | bytes accessed | tf_op | source)
XLA Modules:
  0.0 75.1 jit_solution(943604615593527022)
XLA Ops:
  0.6 68.3 %layer.1 = (bf16[4,2,2,2,256,128]{5,4,3,2,1,0:T(8,128)(2,1)}, s32[8,128]{1,0:T(8,128)}, bf16[4,8,32,512]{3,2,1,0:T(8,128)(2,1)}) custom-call(bf16[256,128]{1,0:T(8,128)(2,1)} %key_ref.1, bf16[256,128]{1,0:T(8,128)(2,1)} %val_ref.1, s32[64,64]{1,0:T(8,128)} %mask_hbm.1, s32[8,256]{1,0:T(8,128)} %bitcast.12, s32[256]{0:T(256)} %clen_hbm.1, ...), custom_call_target="tpu_custom_call" | custom-call | tf_op jit(solution)/shard_map/layer/pallas_call | solution.py:581
  68.9 6.1 %prefill.1 = (bf16[4,64,1024]{2,1,0:T(8,128)(2,1)}, bf16[4,8,32,512]{3,2,1,0:T(8,128)(2,1)}) custom-call(bf16[4,64,1024]{2,1,0:T(8,128)(2,1)} %bitcast.10, bf16[16,2,4,64,128]{4,3,2,1,0:T(8,128)(2,1)} %bitcast.8, s32[8,128]{1,0:T(8,128)} %get-tuple-element.8.picks, bf16[4,8,32,512]{3,2,1,0:T(8,128)(2,1)} %get-tuple-element.9.dec_ref), custom_call_target="tpu_custom_call" | custom-call | tf_op jit(solution)/shard_map/prefill/pallas_call | solution.py:731

commit v7 on v5

--- a/solution.py
+++ b/solution.py
@@ -28,16 +28,16 @@
 
 
 ORDER = (
-    "p0.other", "p1.other", "all.sq", "p0.own", "kv.r", "p2.other", "kv.l", "p3.other",
-    "p0.xr0", "p0.xr2", "p1.own", "kv.f", "p2.own", "p3.own", "kv.s", "all.sq1", "p1.xr0",
-    "kv.z", "p0.xsum", "kv.m", "p1.xr2", "all.sq2", "p3.xr0", "p3.xr2", "p2.xr2", "p2.xr0",
-    "kv.o", "all.mask", "kv.fin", "p1.xsum", "all.take", "p0.att", "p2.xsum", "p3.xsum",
-    "p1.att", "p0.hz", "p2.att", "p1.hz", "p0.hl", "p0.hr", "p3.att", "p2.hz", "p0.hf", "p1.hr",
-    "p1.hl", "p0.out", "p3.hz", "p1.hf", "p2.hr", "p2.hl", "p1.out", "p3.hl", "p2.hf", "p3.hr",
-    "p0.yr2", "p0.yr0", "p2.out", "p3.hf", "p1.yr2", "p1.yr0", "p3.out", "p0.ysum", "p2.yr2",
-    "p2.yr0", "p1.ysum", "p3.yr0", "p3.yr2", "p0.add", "p2.ysum", "p1.add", "p3.ysum", "p0.f1",
-    "p0.f2", "p2.add", "p3.add", "p1.f1", "p1.f2", "p2.f1", "p2.f2", "p3.f1", "p3.f2", "p1.f5",
-    "p2.f5", "all.list", "p0.f5", "p3.f5",
+    "p0.other", "p1.other", "all.sq", "p0.own", "kv.r", "p2.other", "kv.l", "p1.own", "p0.xr2",
+    "p3.other", "p0.xr0", "kv.f", "p2.own", "p3.own", "all.sq1", "p1.xr2", "p1.xr0", "p2.xr2",
+    "kv.m", "kv.z", "p0.xsum", "kv.s", "p2.xr0", "all.mask", "p3.xr0", "kv.o", "all.sq2",
+    "p3.xr2", "p1.xsum", "p2.xsum", "kv.fin", "all.take", "p0.att", "p3.xsum", "p1.att",
+    "p2.att", "p0.hz", "p1.hz", "p3.att", "p2.hz", "p1.hl", "p1.hr", "p0.hl", "p0.hr", "p3.hz",
+    "p2.hl", "p1.hf", "p2.hr", "p0.hf", "p1.out", "p3.hr", "p3.hl", "p2.hf", "p0.out", "p1.yr0",
+    "p1.yr2", "p3.hf", "p2.out", "p0.yr0", "p0.yr2", "p3.out", "p1.ysum", "p2.yr0", "p2.yr2",
+    "p0.ysum", "p3.yr0", "p3.yr2", "all.list", "p1.add", "p2.ysum", "p0.add", "p3.ysum",
+    "p1.f1", "p1.f2", "p2.add", "all.pf0", "p3.add", "p0.f1", "p0.f2", "p1.f5", "p2.f1",
+    "p2.f2", "all.pf1", "p3.f1", "p3.f2", "all.pf2", "p2.f5", "all.pf3", "p0.f5", "p3.f5",
 )
 
 
@@ -49,10 +49,29 @@
     return lax.dot_general(a, b, (((1,), (0,)), ((), ())), preferred_element_type=F32)
 
 
+def first_pages(q_node, keys, values, count):
+    q = jnp.concatenate([q_node[:, s * HD : (s + 1) * HD] for s in range(8)], axis=0)
+    values = jnp.concatenate([values, jnp.ones((8 * PAGE, 128), BF16)], axis=1)
+    j_id = lax.broadcasted_iota(jnp.int32, (1, 8 * PAGE), 1)
+    s = rdot(q, keys) * SCALE + jnp.where(j_id < count * PAGE, 0.0, NEG)
+    i_id = lax.broadcasted_iota(jnp.int32, (512, 128), 0)
+    j_id = lax.broadcasted_iota(jnp.int32, (512, 128), 1)
+    seen = (j_id >= PAGE) | (j_id <= lax.rem(i_id, PAGE))
+    s = jnp.concatenate([jnp.where(seen, s[:, :128], NEG), s[:, 128:]], axis=1)
+    peak = jnp.max(s, axis=1, keepdims=True)
+    return peak, mdot(jnp.exp(s - peak).astype(BF16), values)
+
+
+def write_heads(out, n, mixed):
+    result = (mixed[:, 0:128] / mixed[:, 128:256]).astype(BF16)
+    for s in range(8):
+        out[n, :, s * HD : (s + 1) * HD] = result[s * 64 : (s + 1) * 64]
+
+
 def layer_kernel(
-    key_ref, val_ref, mask_hbm, pages_hbm, clen_hbm, x_ref, gain_hbm, wq_ref, wkv_ref, wo_ref,
-    kv_out, picks, out,
-    ob, mask_ref, pages_ref, clen_ref, gain_ref,
+    q_hbm, key_ref, val_ref, mask_hbm, pages_hbm, clen_hbm, x_ref, gain_hbm, wq_ref, wkv_ref, wo_ref,
+    kv_out, picks, pout, out,
+    qb, spots, pb, ob, mask_ref, pages_ref, clen_ref, gain_ref,
     kv, xb, wb, wkvb, wkvf, wob, xs, sqs, sqc, sqx, sqn, sqz, sqr, gs, gr, g, prelay, pleft, pright, zs, zr, rf,
     pr, nk, nv, bias, chosen, pool_k, pool_v, sb, ho, o, orelay, oleft, oright, ozs, ozr,
     lsem, ssem, rsem,
@@ -111,6 +130,7 @@
         ((gain_hbm, gain_ref), (mask_hbm, mask_ref), (pages_hbm, pages_ref), (clen_hbm, clen_ref))
     ):
         loads.append(pltpu.make_async_copy(src, dst, lsem.at[11 + i]))
+    loads.append(pltpu.make_async_copy(q_hbm, qb, lsem.at[15 + NCH]))
     for copy in loads:
         copy.start()
 
@@ -483,8 +503,8 @@
         def take(b, carry):
             rows = pl.ds(pl.multiple_of(128 * b, 128), 128)
             block = (b // 4, lax.rem(b, 2), lax.rem(b // 2, 2))
-            pool_k[rows] = mdot(chosen[b], kv[block + (0,)]).astype(BF16)
-            pool_v[rows, 0:128] = mdot(chosen[b], kv[block + (1,)]).astype(BF16)
+            pool_k[rows] = mdot(chosen[b], kv[block + (0,)].reshape(256, HD)).astype(BF16)
+            pool_v[rows, 0:128] = mdot(chosen[b], kv[block + (1,)].reshape(256, HD)).astype(BF16)
             return carry
 
         lax.fori_loop(0, 16, take, 0, unroll=8)
@@ -510,6 +530,28 @@
             count = jnp.sum(readable, axis=0, keepdims=True) + 1.0
             rows.append(jnp.where(col_id[0:1] == 127, count, line))
         picks[...] = jnp.concatenate(rows + rows, axis=0).astype(jnp.int32)
+        listed.start()
+
+    def prefill_node(n):
+        if n == 0:
+            listed.wait()
+            loads[14].wait()
+        pages = []
+        for i in range(8):
+            spot = jnp.minimum(jnp.maximum(spots[n, i], 0), 63)
+            pages.append(
+                (spot // 16, lax.rem(spot // 8, 2), lax.rem(spot // 4, 2), lax.rem(spot, 4))
+            )
+        keys = jnp.concatenate([kv[a, b, d, 0, i] for a, b, d, i in pages], axis=0)
+        values = jnp.concatenate([kv[a, b, d, 1, i] for a, b, d, i in pages], axis=0)
+        mixed = first_pages(qb[n], keys, values, spots[n, 127])[1]
+        write_heads(pb, n, mixed)
+        prefilled[n].start()
+
+    listed = pltpu.make_async_copy(picks, spots, lsem.at[16 + NCH])
+    prefilled = [
+        pltpu.make_async_copy(pb.at[n], pout.at[n], lsem.at[17 + NCH + n]) for n in range(4)
+    ]
 
     keep = pltpu.make_async_copy(kv, kv_out, lsem.at[10])
     rms, squared = [], []
@@ -530,7 +572,10 @@
                 stage = {"sq": sum_squares, "sq1": sum_squares_x, "sq2": sum_squares_z}[what]
                 squared[:] = stage(squared) if squared else stage()
             else:
-                {"mask": choose_pages, "take": take_pages, "list": list_pages}[what]()
+                if what[:2] == "pf":
+                    prefill_node(int(what[2]))
+                else:
+                    {"mask": choose_pages, "take": take_pages, "list": list_pages}[what]()
             return
         p = parts[int(who[1])]
         if what == "other":
@@ -570,6 +615,8 @@
     for event in ORDER:
         step(event)
     keep.wait()
+    for copy in prefilled:
+        copy.wait()
     drain(0)
     for p in parts:
         p.done.wait()
@@ -581,19 +628,23 @@
     return pl.pallas_call(
         layer_kernel,
         out_shape=(
-            jax.ShapeDtypeStruct((4, 2, 2, 2, 256, HD), BF16),
+            jax.ShapeDtypeStruct((4, 2, 2, 2, 4, PAGE, HD), BF16),
             jax.ShapeDtypeStruct((8, 128), jnp.int32),
+            jax.ShapeDtypeStruct((4, PAGE, 1024), BF16),
             jax.ShapeDtypeStruct((4, 8, 32, 512), BF16),
         ),
-        in_specs=[hbm] * 10,
-        out_specs=(hbm, vmem, hbm),
+        in_specs=[hbm] * 11,
+        out_specs=(hbm, vmem, hbm, hbm),
         scratch_shapes=[
+            pltpu.VMEM((4, PAGE, 1024), BF16),
+            pltpu.SMEM((8, 128), jnp.int32),
+            pltpu.VMEM((4, PAGE, 1024), BF16),
             pltpu.VMEM((4, 8, 32, 512), BF16),
             pltpu.VMEM((64, 64), jnp.int32),
             pltpu.VMEM((8, 256), jnp.int32),
             pltpu.SMEM((256,), jnp.int32),
             pltpu.VMEM((4, 128), BF16),
-            pltpu.VMEM((4, 2, 2, 2, 256, HD), BF16),
+            pltpu.VMEM((4, 2, 2, 2, 4, PAGE, HD), BF16),
             pltpu.VMEM((4, 16, 16, 512), BF16),
             pltpu.VMEM((5, 512, 256), BF16),
             pltpu.VMEM((1024, 128), BF16),
@@ -630,7 +681,7 @@
             pltpu.VMEM((NCH, 2, 2, RB, 512), BF16),
             pltpu.VMEM((NCH, 2, 2, RB, 512), BF16),
             pltpu.VMEM((NCH, 2, 2, RB, 512), BF16),
-            pltpu.SemaphoreType.DMA((15 + NCH,)),
+            pltpu.SemaphoreType.DMA((21 + NCH,)),
             pltpu.SemaphoreType.DMA((NMSG,)),
             pltpu.SemaphoreType.DMA((NMSG,)),
         ],
@@ -641,117 +692,109 @@
     )(*args)
 
 
-def prefill_kernel(
-    q_hbm, kv_ref, picks, dec_ref, out_hbm, dec_out, q_ref, kv, stage, out, peaks, mixes, sem
+def finish_kernel(
+    q_hbm, kv_ref, picks, pre_ref, dec_ref, out_hbm, dec_out, q, kv, extra, stage, out, peak, mix, sem
 ):
-    loads = [pltpu.make_async_copy(kv_ref, kv, sem.at[0])]
-    loads.append(pltpu.make_async_copy(q_hbm, q_ref, sem.at[2]))
-    fetched = pltpu.make_async_copy(dec_ref, stage, sem.at[3])
-    moved = pltpu.make_async_copy(stage, dec_out, sem.at[4])
-    for copy in loads:
+    get_dec = [pltpu.make_async_copy(dec_ref.at[t], stage.at[t], sem.at[t]) for t in range(4)]
+    put_dec = [pltpu.make_async_copy(stage.at[t], dec_out.at[t], sem.at[4 + t]) for t in range(4)]
+    get_pre = pltpu.make_async_copy(pre_ref, out, sem.at[8])
+    put_pre = pltpu.make_async_copy(out, out_hbm, sem.at[9])
+    get_pre.start()
+    for copy in get_dec:
         copy.start()
-    fetched.start()
-
-    def attend(n, start, pages, state):
-        spots = [picks[n, start + k] for k in range(pages)]
-        keys = jnp.concatenate([kv[p // 4, 0, lax.rem(p, 4)] for p in spots], axis=0)
-        values = jnp.concatenate([kv[p // 4, 1, lax.rem(p, 4)] for p in spots], axis=0)
-        values = jnp.concatenate([values, jnp.ones((pages * PAGE, 128), BF16)], axis=1)
-        q = jnp.concatenate([q_ref[n, :, s * HD : (s + 1) * HD] for s in range(8)], axis=0)
-        j_id = lax.broadcasted_iota(jnp.int32, (1, pages * PAGE), 1)
-        hidden = jnp.where(j_id < (picks[n, 127] - start) * PAGE, 0.0, NEG)
-        s = rdot(q, keys) * SCALE + hidden
-        if state is None:
-            i_id = lax.broadcasted_iota(jnp.int32, (512, 128), 0)
-            j_id = lax.broadcasted_iota(jnp.int32, (512, 128), 1)
-            seen = (j_id >= PAGE) | (j_id <= lax.rem(i_id, PAGE))
-            s = jnp.concatenate([jnp.where(seen, s[:, :128], NEG), s[:, 128:]], axis=1)
-        peak = jnp.max(s, axis=1, keepdims=True)
-        if state is not None:
-            peak = jnp.maximum(peak, state[0])
-        mixed = mdot(jnp.exp(s - peak).astype(BF16), values)
-        if state is not None:
-            mixed = mixed + state[1] * jnp.exp(state[0] - peak)
-        return peak, mixed
-
-    def write(n, mixed):
-        result = (mixed[:, 0:128] / mixed[:, 128:256]).astype(BF16)
-        for s in range(8):
-            out[n, :, s * HD : (s + 1) * HD] = result[s * 64 : (s + 1) * 64]
-
-    def leave(n):
-        return pltpu.make_async_copy(out.at[n], out_hbm.at[n], sem.at[5 + n])
-
-    for copy in loads:
-        copy.wait()
-    for n in range(4):
-        peak, mixed = attend(n, 0, 8, None)
-        peaks[n] = jnp.broadcast_to(peak, (512, 128))
-        mixes[n] = mixed
-        write(n, mixed)
-        leave(n).start()
-        if n == 0:
-            fetched.wait()
-            moved.start()
+
+    def page(n, k):
+        spot = picks[n, k]
+        return kv_ref.at[spot // 4, :, lax.rem(spot, 4)]
+
+    get_pre.wait()
 
     def deep(n, carry):
         @pl.when(picks[n, 127] > 8)
         def _():
+            pltpu.make_async_copy(q_hbm.at[n], q, sem.at[10]).start()
+            for k in range(8):
+                pltpu.make_async_copy(page(n, k), kv.at[k], sem.at[11]).start()
+            pltpu.make_async_copy(q, q, sem.at[10]).wait()
+            pltpu.make_async_copy(kv, kv, sem.at[11]).wait()
+            top, mixed = first_pages(
+                q[...], kv[:, 0].reshape(512, HD), kv[:, 1].reshape(512, HD), picks[n, 127]
+            )
+            peak[...] = jnp.broadcast_to(top, (512, 128))
+            mix[...] = mixed
+
             def more(t, inner):
-                peak, mixed = attend(n, 8 + 4 * t, 4, (peaks[n][:, 0:1], mixes[n]))
-                peaks[n] = jnp.broadcast_to(peak, (512, 128))
-                mixes[n] = mixed
+                for k in range(4):
+                    pltpu.make_async_copy(page(n, 8 + 4 * t + k), extra.at[k], sem.at[12]).start()
+                pltpu.make_async_copy(extra, extra, sem.at[12]).wait()
+                rows = jnp.concatenate([q[:, s * HD : (s + 1) * HD] for s in range(8)], axis=0)
+                j_id = lax.broadcasted_iota(jnp.int32, (1, 4 * PAGE), 1)
+                hidden = jnp.where(j_id < (picks[n, 127] - 8 - 4 * t) * PAGE, 0.0, NEG)
+                s = rdot(rows, extra[:, 0].reshape(4 * PAGE, HD)) * SCALE + hidden
+                before = peak[:, 0:1]
+                top = jnp.maximum(jnp.max(s, axis=1, keepdims=True), before)
+                values = jnp.concatenate(
+                    [extra[:, 1].reshape(4 * PAGE, HD), jnp.ones((4 * PAGE, 128), BF16)], axis=1
+                )
+                mix[...] = mix[...] * jnp.exp(before - top) + mdot(
+                    jnp.exp(s - top).astype(BF16), values
+                )
+                peak[...] = jnp.broadcast_to(top, (512, 128))
                 return inner
 
             lax.fori_loop(0, (picks[n, 127] - 5) // 4, more, 0)
-            leave(n).wait()
-            write(n, mixes[n])
-            leave(n).start()
+            write_heads(out, n, mix[...])
 
         return carry
 
     lax.fori_loop(0, 4, deep, 0)
-    for n in range(4):
-        leave(n).wait()
-    moved.wait()
-
-
-def prefill_call(q, kv, picks, dec):
+    put_pre.start()
+    for t in range(4):
+        get_dec[t].wait()
+        put_dec[t].start()
+    put_pre.wait()
+    for t in range(4):
+        put_dec[t].wait()
+
+
+def finish_call(q, kv, picks, pre, dec):
     hbm = pl.BlockSpec(memory_space=pl.ANY)
     smem = pl.BlockSpec(memory_space=pltpu.SMEM)
     return pl.pallas_call(
-        prefill_kernel,
+        finish_kernel,
         out_shape=(
             jax.ShapeDtypeStruct((4, PAGE, 1024), BF16),
             jax.ShapeDtypeStruct(dec.shape, BF16),
         ),
-        in_specs=[hbm, hbm, smem, hbm],
+        in_specs=[hbm, hbm, smem, hbm, hbm],
         out_specs=(hbm, hbm),
         scratch_shapes=[
-            pltpu.VMEM((4, PAGE, 1024), BF16),
-            pltpu.VMEM((16, 2, 4, PAGE, HD), BF16),
+            pltpu.VMEM((PAGE, 1024), BF16),
+            pltpu.VMEM((8, 2, PAGE, HD), BF16),
+            pltpu.VMEM((4, 2, PAGE, HD), BF16),
             pltpu.VMEM(dec.shape, BF16),
             pltpu.VMEM((4, PAGE, 1024), BF16),
-            pltpu.VMEM((4, 512, 128), F32),
-            pltpu.VMEM((4, 512, 256), F32),
-            pltpu.SemaphoreType.DMA((9,)),
+            pltpu.VMEM((512, 128), F32),
+            pltpu.VMEM((512, 256), F32),
+            pltpu.SemaphoreType.DMA((13,)),
         ],
         compiler_params=pltpu.CompilerParams(vmem_limit_bytes=62 * 1024 * 1024),
-        name="prefill",
-    )(q, kv, picks, dec)
+        name="finish",
+    )(q, kv, picks, pre, dec)
 
 
 def per_device(
     prefill_query, prefill_key, prefill_value, tree_mask, pages, cache_len,
     dec_in, norm_gain, w_query, w_keyval, w_out,
 ):
-    kv, picks, dec = layer_call(
-        prefill_key, prefill_value, tree_mask, pages.T, cache_len,
-        dec_in.reshape(4, 16, 16, 512), norm_gain.reshape(4, 128), w_query,
+    query = prefill_query.reshape(4, PAGE, 1024)
+    kv, picks, pre, dec = layer_call(
+        query, prefill_key.reshape(4, PAGE, HD), prefill_value.reshape(4, PAGE, HD), tree_mask,
+        pages.T, cache_len, dec_in.reshape(4, 16, 16, 512), norm_gain.reshape(4, 128), w_query,
         w_keyval.reshape(1024, 128), w_out,
     )
-    prefill_out, dec_out = prefill_call(
-        prefill_query.reshape(4, PAGE, 1024), kv.reshape(16, 2, 4, PAGE, HD), picks, dec
+    prefill_out, dec_out = finish_call(
+        query, kv.reshape(16, 2, 4, PAGE, HD), picks, pre, dec
     )
     return prefill_out.reshape(256, 1024), dec_out.reshape(4, 256, 512)
 

time: 75.7 us -> 73 us (0.964); the launches traced: 74.3 us -> 72.8 us
  Pallas kernels: 73.7 us -> 72.2 us
    pallas_call x1, Pallas kernels: 5.4 us -> 3.01 us  [finish_call(): pl.pallas_call(finish_kernel, out_shape=(jax.ShapeDtypeStruct((4, PAGE, 1...]
    pallas_call x1, Pallas kernels: 68.3 us -> 69.2 us  [layer_call(): pl.pallas_call(layer_kernel, out_shape=(jax.ShapeDtypeStruct((4, 2, 2, 2,...]
where the time goes in v7:
time: 73 us; the launch traced here: 72.8 us
  Pallas kernels  72.2 us (99%)
    pallas_call x1, Pallas kernels, layer_call(): pl.pallas_call(layer_kernel, out_shape=(jax.ShapeDtypeStruct((4, 2, 2, 2,...  69.2 us
    pallas_call x1, Pallas kernels, finish_call(): pl.pallas_call(finish_kernel, out_shape=(jax.ShapeDtypeStruct((4, PAGE, 1...  3.01 us

profile of v7, /device:TPU:0, one launch (start us, length us, event | category | flops | bytes accessed | tf_op | source)
XLA Modules:
  0.0 72.8 jit_solution(1759547318752658343)
XLA Ops:
  0.6 69.2 %layer.1 = (bf16[4,2,2,2,4,64,128]{6,5,4,3,2,1,0:T(8,128)(2,1)}, s32[8,128]{1,0:T(8,128)}, bf16[4,64,1024]{2,1,0:T(8,128)(2,1)}, bf16[4,8,32,512]{3,2,1,0:T(8,128)(2,1)}) custom-call(bf16[4,64,1024]{2,1,0:T(8,128)(2,1)} %bitcast.10, bf16[4,64,128]{2,1,0:T(8,128)(2,1)} %bitcast.15, bf16[4,64,128]{2,1,0:T(8,128)(2,1)} %bitcast.16, s32[64,64]{1,0:T(8,128)} %mask_hbm.1, ...), custom_call_target="tpu_custom_call" | custom-call | tf_op jit(solution)/shard_map/layer/pallas_call | solution.py:628
  69.8 3.0 %finish.1 = (bf16[4,64,1024]{2,1,0:T(8,128)(2,1)}, bf16[4,8,32,512]{3,2,1,0:T(8,128)(2,1)}) custom-call(bf16[4,64,1024]{2,1,0:T(8,128)(2,1)} %bitcast.11, bf16[16,2,4,64,128]{4,3,2,1,0:T(8,128)(2,1)} %bitcast.12, s32[8,128]{1,0:T(8,128)} %get-tuple-element.9.picks, bf16[4,64,1024]{2,1,0:T(8,128)(2,1)} %get-tuple-element.10.pre_ref, ...), custom_call_target="tpu_custom_call" | custom-call | tf_op jit(solution)/shard_map/finish/pallas_call | solution.py:763

commit v8 on v7

--- a/solution.py
+++ b/solution.py
@@ -28,16 +28,16 @@
 
 
 ORDER = (
-    "p0.other", "p1.other", "all.sq", "p0.own", "kv.r", "p2.other", "kv.l", "p1.own", "p0.xr2",
-    "p3.other", "p0.xr0", "kv.f", "p2.own", "p3.own", "all.sq1", "p1.xr2", "p1.xr0", "p2.xr2",
-    "kv.m", "kv.z", "p0.xsum", "kv.s", "p2.xr0", "all.mask", "p3.xr0", "kv.o", "all.sq2",
-    "p3.xr2", "p1.xsum", "p2.xsum", "kv.fin", "all.take", "p0.att", "p3.xsum", "p1.att",
-    "p2.att", "p0.hz", "p1.hz", "p3.att", "p2.hz", "p1.hl", "p1.hr", "p0.hl", "p0.hr", "p3.hz",
-    "p2.hl", "p1.hf", "p2.hr", "p0.hf", "p1.out", "p3.hr", "p3.hl", "p2.hf", "p0.out", "p1.yr0",
-    "p1.yr2", "p3.hf", "p2.out", "p0.yr0", "p0.yr2", "p3.out", "p1.ysum", "p2.yr0", "p2.yr2",
-    "p0.ysum", "p3.yr0", "p3.yr2", "all.list", "p1.add", "p2.ysum", "p0.add", "p3.ysum",
-    "p1.f1", "p1.f2", "p2.add", "all.pf0", "p3.add", "p0.f1", "p0.f2", "p1.f5", "p2.f1",
-    "p2.f2", "all.pf1", "p3.f1", "p3.f2", "all.pf2", "p2.f5", "all.pf3", "p0.f5", "p3.f5",
+    "p0.other", "p1.other", "p2.other", "p0.own", "all.pick", "kv.r", "kv.l", "kv.z", "p1.own",
+    "all.sq", "p0.xr2", "p0.xr0", "p2.own", "p3.other", "kv.f", "p1.xr0", "p1.xr2", "all.sq1",
+    "p3.own", "p2.xr0", "kv.s", "p2.xr2", "kv.m", "p0.xsum", "all.sq2", "kv.o", "all.mask",
+    "p3.xr2", "p1.xsum", "kv.fin", "p3.xr0", "p2.xsum", "p0.att", "p1.att", "p3.xsum", "p2.att",
+    "p0.hz", "p1.hz", "p3.att", "p0.hl", "p0.hr", "p2.hz", "p1.hl", "all.list", "p3.hz",
+    "p0.hf", "p1.hr", "p2.hl", "p2.hr", "p0.out", "p3.hr", "p3.hl", "p1.hf", "all.pf0", "p2.hf",
+    "p0.yr0", "p0.yr2", "p3.hf", "p1.out", "p3.out", "p2.out", "p1.yr2", "p1.yr0", "p0.ysum",
+    "p3.yr2", "p3.yr0", "p2.yr0", "p2.yr2", "all.pf1", "p1.ysum", "all.pf2", "p3.ysum",
+    "p0.add", "p2.ysum", "p1.add", "p3.add", "p2.add", "p0.f2", "all.pf3", "p0.f1", "p1.f1",
+    "p1.f2", "p3.f1", "p3.f2", "p2.f1", "p2.f2", "p1.f5", "p0.f5", "p3.f5", "p2.f5",
 )
 
 
@@ -73,7 +73,7 @@
     kv_out, picks, pout, out,
     qb, spots, pb, ob, mask_ref, pages_ref, clen_ref, gain_ref,
     kv, xb, wb, wkvb, wkvf, wob, xs, sqs, sqc, sqx, sqn, sqz, sqr, gs, gr, g, prelay, pleft, pright, zs, zr, rf,
-    pr, nk, nv, bias, chosen, pool_k, pool_v, sb, ho, o, orelay, oleft, oright, ozs, ozr,
+    pr, nk, nv, bias, two, two_s, sb, ho, o, orelay, oleft, oright, ozs, ozr,
     lsem, ssem, rsem,
 ):
     c = lax.axis_index("ctx")
@@ -90,8 +90,9 @@
     def hidx(yi, zi):
         return zi * 4 + yi
 
-    xr, xl, xo = lax.rem(x + 1, 4), lax.rem(x + 3, 4), lax.rem(x + 2, 4)
-    yr, yl, yo = lax.rem(y + 1, 4), lax.rem(y + 3, 4), lax.rem(y + 2, 4)
+    up, down = 1 + 2 * core, 3 - 2 * core
+    xr, xl, xo = lax.rem(x + up, 4), lax.rem(x + down, 4), lax.rem(x + 2, 4)
+    yr, yl, yo = lax.rem(y + up, 4), lax.rem(y + down, 4), lax.rem(y + 2, 4)
     d_xr = (cidx(xr, zh, core), h)
     d_xl = (cidx(xl, zh, core), h)
     d_z = (cidx(x, 1 - zh, core), h)
@@ -322,7 +323,7 @@
         for s in range(10):
             pr[k, s] = ((rf[k, s] + zr[k, s].astype(F32)) * inv).astype(BF16)
         nk[k * RB : (k + 1) * RB] = pr[k, 8]
-        nv[k * RB : (k + 1) * RB, 0:128] = pr[k, 9]
+        nv[k * RB : (k + 1) * RB] = pr[k, 9]
 
         q = pr[k, 0:8].reshape(nrow, HD)
         i_id = lax.broadcasted_iota(jnp.int32, (nrow, nnew), 0)
@@ -333,7 +334,7 @@
         s_new = jnp.where(seen, rdot(q, nk[0:nnew]) * SCALE, NEG)
         peak = None
         for b in range(8):
-            s = rdot(q, pool_k[256 * b : 256 * b + 256]) * SCALE
+            s = rdot(q, pool(b, 0)) * SCALE
             s = (s.reshape(nrow // 16, 16, 256) + bias[b][None]).reshape(nrow, 256)
             sb[b] = s
             here = jnp.maximum(s[:, :128], s[:, 128:])
@@ -342,10 +343,13 @@
             jnp.max(peak, axis=1, keepdims=True), jnp.max(s_new, axis=1, keepdims=True)
         )
         w_new = jnp.exp(s_new - top)
-        mixed = mdot(w_new.astype(BF16), nv[0:nnew])
+        ones = jnp.ones((256, HD), BF16)
+        mixed = mdot(
+            w_new.astype(BF16), jnp.concatenate([nv[0:nnew], ones[0:nnew]], axis=1)
+        )
         for b in range(8):
             w = jnp.exp(sb[b] - top).astype(BF16)
-            mixed = mixed + mdot(w, pool_v[256 * b : 256 * b + 256])
+            mixed = mixed + mdot(w, jnp.concatenate([pool(b, 1), ones], axis=1))
         head_out = (mixed[:, 0:128] / mixed[:, 128:256]).astype(BF16)
         for s in range(8):
             ho[k, x, core, zh, s // 4, :, (s % 4) * HD : (s % 4 + 1) * HD] = head_out[s * RB : (s + 1) * RB]
@@ -444,70 +448,60 @@
         row_sq = jnp.sum(jnp.where(eye, flat, 0.0), axis=1, keepdims=True)
         return lax.rsqrt(row_sq / D + 1e-05)
 
-    def choose_pages():
-        loads[12].wait()
-        loads[13].wait()
+    def own_rows_pages():
         pick = (
             lax.broadcasted_iota(jnp.int32, (16, 256), 1)
             == lax.broadcasted_iota(jnp.int32, (16, 256), 0) + 16 * c
         )
-        own_pages = rdot(pick.astype(BF16), pages_ref[...].astype(BF16)).astype(jnp.int32)
-        r_id = lax.broadcasted_iota(jnp.int32, (16, 256), 0)
-        s_id = lax.broadcasted_iota(jnp.int32, (16, 256), 1)
-        lens = jnp.zeros((16, 256), jnp.int32)
+        return rdot(pick.astype(BF16), pages_ref[...].astype(BF16))
+
+    def pick_pages():
+        loads[12].wait()
+        loads[13].wait()
+        own_pages = own_rows_pages()
+        page_id = lax.broadcasted_iota(jnp.int32, (16, 64), 1)
+        block_id = lax.broadcasted_iota(jnp.int32, (16, 64), 0)
+        named = jnp.zeros((16, 64), F32)
+        for slot in range(8):
+            named = jnp.where(own_pages[:, slot : slot + 1] == page_id.astype(F32), 1.0, named)
+        present = jnp.max(named, axis=0, keepdims=True) > 0.5
+        here = present & (page_id // 4 == block_id)
+        place = lax.rem(page_id, 4).astype(F32)
+        low = jnp.min(jnp.where(here, place, 9.0), axis=1, keepdims=True)
+        high = jnp.max(jnp.where(here, place, -1.0), axis=1, keepdims=True)
+        column = lax.broadcasted_iota(jnp.int32, (16, 128), 1)
+        two[...] = jnp.where(column == 0, low, high).astype(jnp.int32)
+        paired.start()
+
+    paired = pltpu.make_async_copy(two, two_s, lsem.at[21 + NCH])
+
+    def chosen(b, i):
+        return jnp.minimum(jnp.maximum(two_s[b, i], 0), 3)
+
+    def mask_pages():
+        paired.wait()
+        own_pages = own_rows_pages().astype(jnp.int32)
+        r_id = lax.broadcasted_iota(jnp.int32, (16, 128), 0)
+        s_id = lax.broadcasted_iota(jnp.int32, (16, 128), 1)
+        lens = jnp.zeros((16, 128), jnp.int32)
         for r in range(16):
             lens = jnp.where(r_id == r, clen_ref[c * 16 + r], lens)
+        named = [jnp.broadcast_to(own_pages[:, slot : slot + 1], (16, 128)) for slot in range(8)]
+        upto = [lens - slot * PAGE for slot in range(8)]
         in_page = lax.rem(s_id, PAGE)
-        page_id = lax.broadcasted_iota(jnp.int32, (16, 64), 1)
-        named = jnp.zeros((16, 64), F32)
-        for slot in range(8):
-            named = jnp.where(own_pages[:, slot : slot + 1] == page_id, 1.0, named)
-        present = jnp.broadcast_to(jnp.max(named, axis=0, keepdims=True), (16, 64))
-        a_id = lax.broadcasted_iota(jnp.int32, (64, 64), 0)
-        b_id = lax.broadcasted_iota(jnp.int32, (64, 64), 1)
-        ahead = (a_id // 4 == b_id // 4) & (a_id < b_id)
-        rank = mdot(present.astype(BF16), ahead.astype(BF16))
-        code = jnp.where(present > 0.5, rank + 1.0, 0.0).astype(BF16)
-        node_id = lax.broadcasted_iota(jnp.int32, (64, 256), 0)
-        node_of = lax.broadcasted_iota(jnp.int32, (64, 256), 1) // PAGE
-        to_id = lax.broadcasted_iota(jnp.int32, (128, 256), 0)
-        from_id = lax.broadcasted_iota(jnp.int32, (128, 256), 1)
-        same = lax.rem(to_id, PAGE) == lax.rem(from_id, PAGE)
-        want = jnp.where(same, (to_id // PAGE + 1).astype(F32), -1.0)
-        last = [
-            (own_pages[:, slot : slot + 1], lens - slot * PAGE, s_id // PAGE)
-            for slot in range(8)
-        ]
-
-        def choose(b):
-            live = jnp.zeros((16, 256), F32)
-            for named_page, upto, page in last:
-                hit = (named_page - 4 * b == page) & (in_page < upto)
-                live = jnp.where(hit, 1.0, live)
-            spread = mdot(code, (node_id == node_of + 4 * b).astype(BF16))
-            sel = jnp.where(spread[0:1] == want, 1.0, 0.0).astype(BF16)
-            chosen[b] = sel
-            return jnp.where(rdot(live.astype(BF16), sel) > 0.5, 0.0, NEG)
-
-        def choose_two(i, carry):
-            bias[i, :, 0:128] = choose(2 * i)
-            bias[i, :, 128:256] = choose(2 * i + 1)
-            return carry
-
-        lax.fori_loop(0, 8, choose_two, 0, unroll=2)
-
-    def take_pages():
-        pool_v[:, 128:256] = jnp.ones((2048, 128), BF16)
-        nv[:, 128:256] = jnp.ones((64, 128), BF16)
-
-        def take(b, carry):
-            rows = pl.ds(pl.multiple_of(128 * b, 128), 128)
-            block = (b // 4, lax.rem(b, 2), lax.rem(b // 2, 2))
-            pool_k[rows] = mdot(chosen[b], kv[block + (0,)].reshape(256, HD)).astype(BF16)
-            pool_v[rows, 0:128] = mdot(chosen[b], kv[block + (1,)].reshape(256, HD)).astype(BF16)
-            return carry
-
-        lax.fori_loop(0, 16, take, 0, unroll=8)
+        for b in range(16):
+            page = 4 * b + jnp.where(s_id < PAGE, chosen(b, 0), chosen(b, 1))
+            end = jnp.zeros((16, 128), jnp.int32)
+            for slot in range(8):
+                end = jnp.where(named[slot] == page, upto[slot], end)
+            bias[b // 2, :, 128 * (b % 2) : 128 * (b % 2) + 128] = jnp.where(in_page < end, 0.0, NEG)
+
+    def pool(t, f):
+        pages = []
+        for b in (2 * t, 2 * t + 1):
+            for i in range(2):
+                pages.append(kv[b // 4, b % 2, (b // 2) % 2, f, chosen(b, i)])
+        return jnp.concatenate(pages, axis=0)
 
     def list_pages():
         loads[11].wait()
@@ -575,7 +569,7 @@
                 if what[:2] == "pf":
                     prefill_node(int(what[2]))
                 else:
-                    {"mask": choose_pages, "take": take_pages, "list": list_pages}[what]()
+                    {"pick": pick_pages, "mask": mask_pages, "list": list_pages}[what]()
             return
         p = parts[int(who[1])]
         if what == "other":
@@ -668,11 +662,10 @@
             pltpu.VMEM((NCH, 10, RB, 128), F32),
             pltpu.VMEM((NCH, 10, RB, 128), BF16),
             pltpu.VMEM((64, 128), BF16),
-            pltpu.VMEM((64, 256), BF16),
+            pltpu.VMEM((64, 128), BF16),
             pltpu.VMEM((8, 16, 256), F32),
-            pltpu.VMEM((16, 128, 256), BF16),
-            pltpu.VMEM((2048, HD), BF16),
-            pltpu.VMEM((2048, 2 * HD), BF16),
+            pltpu.VMEM((16, 128), jnp.int32),
+            pltpu.SMEM((16, 128), jnp.int32),
             pltpu.VMEM((8, 8 * RB, 256), F32),
             pltpu.VMEM((NCH, 4, 2, 2, 2, RB, 512), BF16),
             pltpu.VMEM((NCH, 4, 2, 2, RB, 512), BF16),
@@ -681,7 +674,7 @@
             pltpu.VMEM((NCH, 2, 2, RB, 512), BF16),
             pltpu.VMEM((NCH, 2, 2, RB, 512), BF16),
             pltpu.VMEM((NCH, 2, 2, RB, 512), BF16),
-            pltpu.SemaphoreType.DMA((21 + NCH,)),
+            pltpu.SemaphoreType.DMA((22 + NCH,)),
             pltpu.SemaphoreType.DMA((NMSG,)),
             pltpu.SemaphoreType.DMA((NMSG,)),
         ],

time: 73 us -> 72 us (0.986)
  Pallas kernels: 72.2 us -> 71.1 us
    pallas_call x1, Pallas kernels: 69.2 us -> 68.1 us  [layer_call(): pl.pallas_call(layer_kernel, out_shape=(jax.ShapeDtypeStruct((4, 2, 2, 2,...]
where the time goes in v8:
time: 72 us; the launch traced here: 71.8 us
  Pallas kernels  71.1 us (99%)
    pallas_call x1, Pallas kernels, layer_call(): pl.pallas_call(layer_kernel, out_shape=(jax.ShapeDtypeStruct((4, 2, 2, 2,...  68.1 us
    pallas_call x1, Pallas kernels, finish_call(): pl.pallas_call(finish_kernel, out_shape=(jax.ShapeDtypeStruct((4, PAGE, 1...  3.01 us

profile of v8, /device:TPU:0, one launch (start us, length us, event | category | flops | bytes accessed | tf_op | source)
XLA Modules:
  0.0 71.8 jit_solution(15208484457784646881)
XLA Ops:
  0.6 68.1 %layer.1 = (bf16[4,2,2,2,4,64,128]{6,5,4,3,2,1,0:T(8,128)(2,1)}, s32[8,128]{1,0:T(8,128)}, bf16[4,64,1024]{2,1,0:T(8,128)(2,1)}, bf16[4,8,32,512]{3,2,1,0:T(8,128)(2,1)}) custom-call(bf16[4,64,1024]{2,1,0:T(8,128)(2,1)} %bitcast.10, bf16[4,64,128]{2,1,0:T(8,128)(2,1)} %bitcast.15, bf16[4,64,128]{2,1,0:T(8,128)(2,1)} %bitcast.16, s32[64,64]{1,0:T(8,128)} %mask_hbm.1, ...), custom_call_target="tpu_custom_call" | custom-call | tf_op jit(solution)/shard_map/layer/pallas_call | solution.py:622
  68.8 3.0 %finish.1 = (bf16[4,64,1024]{2,1,0:T(8,128)(2,1)}, bf16[4,8,32,512]{3,2,1,0:T(8,128)(2,1)}) custom-call(bf16[4,64,1024]{2,1,0:T(8,128)(2,1)} %bitcast.11, bf16[16,2,4,64,128]{4,3,2,1,0:T(8,128)(2,1)} %bitcast.12, s32[8,128]{1,0:T(8,128)} %get-tuple-element.9.picks, bf16[4,64,1024]{2,1,0:T(8,128)(2,1)} %get-tuple-element.10.pre_ref, ...), custom_call_target="tpu_custom_call" | custom-call | tf_op jit(solution)/shard_map/finish/pallas_call | solution.py:756

commit v9 on v8

--- a/solution.py
+++ b/solution.py
@@ -18,6 +18,7 @@
 NCH = 4
 TS = STEPS // NCH
 RB = 16 * TS
+NEAR = 12
 
 KV0 = 0
 SQ0 = 12
@@ -51,8 +52,8 @@
 
 def first_pages(q_node, keys, values, count):
     q = jnp.concatenate([q_node[:, s * HD : (s + 1) * HD] for s in range(8)], axis=0)
-    values = jnp.concatenate([values, jnp.ones((8 * PAGE, 128), BF16)], axis=1)
-    j_id = lax.broadcasted_iota(jnp.int32, (1, 8 * PAGE), 1)
+    values = jnp.concatenate([values, jnp.ones((NEAR * PAGE, 128), BF16)], axis=1)
+    j_id = lax.broadcasted_iota(jnp.int32, (1, NEAR * PAGE), 1)
     s = rdot(q, keys) * SCALE + jnp.where(j_id < count * PAGE, 0.0, NEG)
     i_id = lax.broadcasted_iota(jnp.int32, (512, 128), 0)
     j_id = lax.broadcasted_iota(jnp.int32, (512, 128), 1)
@@ -70,8 +71,8 @@
 
 def layer_kernel(
     q_hbm, key_ref, val_ref, mask_hbm, pages_hbm, clen_hbm, x_ref, gain_hbm, wq_ref, wkv_ref, wo_ref,
-    kv_out, picks, pout, out,
-    qb, spots, pb, ob, mask_ref, pages_ref, clen_ref, gain_ref,
+    kv_out, picks_out, pout, out,
+    picks, qb, spots, pb, ob, mask_ref, pages_ref, clen_ref, gain_ref,
     kv, xb, wb, wkvb, wkvf, wob, xs, sqs, sqc, sqx, sqn, sqz, sqr, gs, gr, g, prelay, pleft, pright, zs, zr, rf,
     pr, nk, nv, bias, two, two_s, sb, ho, o, orelay, oleft, oright, ozs, ozr,
     lsem, ssem, rsem,
@@ -343,14 +344,15 @@
             jnp.max(peak, axis=1, keepdims=True), jnp.max(s_new, axis=1, keepdims=True)
         )
         w_new = jnp.exp(s_new - top)
-        ones = jnp.ones((256, HD), BF16)
-        mixed = mdot(
-            w_new.astype(BF16), jnp.concatenate([nv[0:nnew], ones[0:nnew]], axis=1)
-        )
+        mixed = mdot(w_new.astype(BF16), nv[0:nnew])
+        part = None
         for b in range(8):
-            w = jnp.exp(sb[b] - top).astype(BF16)
-            mixed = mixed + mdot(w, jnp.concatenate([pool(b, 1), ones], axis=1))
-        head_out = (mixed[:, 0:128] / mixed[:, 128:256]).astype(BF16)
+            w = jnp.exp(sb[b] - top)
+            here = w[:, :128] + w[:, 128:]
+            part = here if part is None else part + here
+            mixed = mixed + mdot(w.astype(BF16), pool(b, 1))
+        total = jnp.sum(part, axis=1, keepdims=True) + jnp.sum(w_new, axis=1, keepdims=True)
+        head_out = (mixed / total).astype(BF16)
         for s in range(8):
             ho[k, x, core, zh, s // 4, :, (s % 4) * HD : (s % 4 + 1) * HD] = head_out[s * RB : (s + 1) * RB]
         p.hog.start()
@@ -525,13 +527,14 @@
             rows.append(jnp.where(col_id[0:1] == 127, count, line))
         picks[...] = jnp.concatenate(rows + rows, axis=0).astype(jnp.int32)
         listed.start()
+        told.start()
 
     def prefill_node(n):
         if n == 0:
             listed.wait()
             loads[14].wait()
         pages = []
-        for i in range(8):
+        for i in range(NEAR):
             spot = jnp.minimum(jnp.maximum(spots[n, i], 0), 63)
             pages.append(
                 (spot // 16, lax.rem(spot // 8, 2), lax.rem(spot // 4, 2), lax.rem(spot, 4))
@@ -543,6 +546,7 @@
         prefilled[n].start()
 
     listed = pltpu.make_async_copy(picks, spots, lsem.at[16 + NCH])
+    told = pltpu.make_async_copy(picks, picks_out, lsem.at[22 + NCH])
     prefilled = [
         pltpu.make_async_copy(pb.at[n], pout.at[n], lsem.at[17 + NCH + n]) for n in range(4)
     ]
@@ -609,6 +613,7 @@
     for event in ORDER:
         step(event)
     keep.wait()
+    told.wait()
     for copy in prefilled:
         copy.wait()
     drain(0)
@@ -618,7 +623,6 @@
 
 def layer_call(*args):
     hbm = pl.BlockSpec(memory_space=pl.ANY)
-    vmem = pl.BlockSpec(memory_space=pltpu.VMEM)
     return pl.pallas_call(
         layer_kernel,
         out_shape=(
@@ -628,8 +632,9 @@
             jax.ShapeDtypeStruct((4, 8, 32, 512), BF16),
         ),
         in_specs=[hbm] * 11,
-        out_specs=(hbm, vmem, hbm, hbm),
+        out_specs=(hbm, hbm, hbm, hbm),
         scratch_shapes=[
+            pltpu.VMEM((8, 128), jnp.int32),
             pltpu.VMEM((4, PAGE, 1024), BF16),
             pltpu.SMEM((8, 128), jnp.int32),
             pltpu.VMEM((4, PAGE, 1024), BF16),
@@ -674,7 +679,7 @@
             pltpu.VMEM((NCH, 2, 2, RB, 512), BF16),
             pltpu.VMEM((NCH, 2, 2, RB, 512), BF16),
             pltpu.VMEM((NCH, 2, 2, RB, 512), BF16),
-            pltpu.SemaphoreType.DMA((22 + NCH,)),
+            pltpu.SemaphoreType.DMA((23 + NCH,)),
             pltpu.SemaphoreType.DMA((NMSG,)),
             pltpu.SemaphoreType.DMA((NMSG,)),
         ],
@@ -686,12 +691,15 @@
 
 
 def finish_kernel(
-    q_hbm, kv_ref, picks, pre_ref, dec_ref, out_hbm, dec_out, q, kv, extra, stage, out, peak, mix, sem
+    q_hbm, kv_ref, picks_hbm, pre_ref, dec_ref, out_hbm, dec_out,
+    picks, q, kv, extra, stage, out, peak, mix, sem,
 ):
     get_dec = [pltpu.make_async_copy(dec_ref.at[t], stage.at[t], sem.at[t]) for t in range(4)]
     put_dec = [pltpu.make_async_copy(stage.at[t], dec_out.at[t], sem.at[4 + t]) for t in range(4)]
     get_pre = pltpu.make_async_copy(pre_ref, out, sem.at[8])
     put_pre = pltpu.make_async_copy(out, out_hbm, sem.at[9])
+    get_picks = pltpu.make_async_copy(picks_hbm, picks, sem.at[13])
+    get_picks.start()
     get_pre.start()
     for copy in get_dec:
         copy.start()
@@ -700,29 +708,38 @@
         spot = picks[n, k]
         return kv_ref.at[spot // 4, :, lax.rem(spot, 4)]
 
+    get_picks.wait()
     get_pre.wait()
+    for t in range(4):
+        get_dec[t].wait()
+        put_dec[t].start()
 
     def deep(n, carry):
-        @pl.when(picks[n, 127] > 8)
+        @pl.when(picks[n, 127] > NEAR)
         def _():
             pltpu.make_async_copy(q_hbm.at[n], q, sem.at[10]).start()
-            for k in range(8):
+            for k in range(NEAR):
                 pltpu.make_async_copy(page(n, k), kv.at[k], sem.at[11]).start()
             pltpu.make_async_copy(q, q, sem.at[10]).wait()
             pltpu.make_async_copy(kv, kv, sem.at[11]).wait()
             top, mixed = first_pages(
-                q[...], kv[:, 0].reshape(512, HD), kv[:, 1].reshape(512, HD), picks[n, 127]
+                q[...],
+                kv[:, 0].reshape(NEAR * PAGE, HD),
+                kv[:, 1].reshape(NEAR * PAGE, HD),
+                picks[n, 127],
             )
             peak[...] = jnp.broadcast_to(top, (512, 128))
             mix[...] = mixed
 
             def more(t, inner):
                 for k in range(4):
-                    pltpu.make_async_copy(page(n, 8 + 4 * t + k), extra.at[k], sem.at[12]).start()
+                    pltpu.make_async_copy(
+                        page(n, NEAR + 4 * t + k), extra.at[k], sem.at[12]
+                    ).start()
                 pltpu.make_async_copy(extra, extra, sem.at[12]).wait()
                 rows = jnp.concatenate([q[:, s * HD : (s + 1) * HD] for s in range(8)], axis=0)
                 j_id = lax.broadcasted_iota(jnp.int32, (1, 4 * PAGE), 1)
-                hidden = jnp.where(j_id < (picks[n, 127] - 8 - 4 * t) * PAGE, 0.0, NEG)
+                hidden = jnp.where(j_id < (picks[n, 127] - NEAR - 4 * t) * PAGE, 0.0, NEG)
                 s = rdot(rows, extra[:, 0].reshape(4 * PAGE, HD)) * SCALE + hidden
                 before = peak[:, 0:1]
                 top = jnp.maximum(jnp.max(s, axis=1, keepdims=True), before)
@@ -735,16 +752,13 @@
                 peak[...] = jnp.broadcast_to(top, (512, 128))
                 return inner
 
-            lax.fori_loop(0, (picks[n, 127] - 5) // 4, more, 0)
+            lax.fori_loop(0, (picks[n, 127] - NEAR + 3) // 4, more, 0)
             write_heads(out, n, mix[...])
 
         return carry
 
     lax.fori_loop(0, 4, deep, 0)
     put_pre.start()
-    for t in range(4):
-        get_dec[t].wait()
-        put_dec[t].start()
     put_pre.wait()
     for t in range(4):
         put_dec[t].wait()
@@ -752,24 +766,24 @@
 
 def finish_call(q, kv, picks, pre, dec):
     hbm = pl.BlockSpec(memory_space=pl.ANY)
-    smem = pl.BlockSpec(memory_space=pltpu.SMEM)
     return pl.pallas_call(
         finish_kernel,
         out_shape=(
             jax.ShapeDtypeStruct((4, PAGE, 1024), BF16),
             jax.ShapeDtypeStruct(dec.shape, BF16),
         ),
-        in_specs=[hbm, hbm, smem, hbm, hbm],
+        in_specs=[hbm] * 5,
         out_specs=(hbm, hbm),
         scratch_shapes=[
+            pltpu.SMEM((8, 128), jnp.int32),
             pltpu.VMEM((PAGE, 1024), BF16),
-            pltpu.VMEM((8, 2, PAGE, HD), BF16),
+            pltpu.VMEM((NEAR, 2, PAGE, HD), BF16),
             pltpu.VMEM((4, 2, PAGE, HD), BF16),
             pltpu.VMEM(dec.shape, BF16),
             pltpu.VMEM((4, PAGE, 1024), BF16),
             pltpu.VMEM((512, 128), F32),
             pltpu.VMEM((512, 256), F32),
-            pltpu.SemaphoreType.DMA((13,)),
+            pltpu.SemaphoreType.DMA((14,)),
         ],
         compiler_params=pltpu.CompilerParams(vmem_limit_bytes=62 * 1024 * 1024),
         name="finish",

time: 72 us -> 70.7 us (0.982)
  Pallas kernels: 71.1 us -> 69.9 us
where the time goes in v9:
time: 70.7 us; the launch traced here: 70.6 us
  Pallas kernels  69.9 us (99%)
    pallas_call x1, Pallas kernels, layer_call(): pl.pallas_call(layer_kernel, out_shape=(jax.ShapeDtypeStruct((4, 2, 2, 2,...  67.5 us
    pallas_call x1, Pallas kernels, finish_call(): pl.pallas_call(finish_kernel, out_shape=(jax.ShapeDtypeStruct((4, PAGE, 1...  2.38 us

profile of v9, /device:TPU:0, one launch (start us, length us, event | category | flops | bytes accessed | tf_op | source)
XLA Modules:
  0.0 70.6 jit_solution(10393618542866869609)
XLA Ops:
  0.6 67.5 %layer.1 = (bf16[4,2,2,2,4,64,128]{6,5,4,3,2,1,0:T(8,128)(2,1)}, s32[8,128]{1,0:T(8,128)}, bf16[4,64,1024]{2,1,0:T(8,128)(2,1)}, bf16[4,8,32,512]{3,2,1,0:T(8,128)(2,1)}) custom-call(bf16[4,64,1024]{2,1,0:T(8,128)(2,1)} %bitcast.10, bf16[4,64,128]{2,1,0:T(8,128)(2,1)} %bitcast.15, bf16[4,64,128]{2,1,0:T(8,128)(2,1)} %bitcast.16, s32[64,64]{1,0:T(8,128)} %mask_hbm.1, ...), custom_call_target="tpu_custom_call" | custom-call | tf_op jit(solution)/shard_map/layer/pallas_call | solution.py:626
  68.2 2.4 %finish.1 = (bf16[4,64,1024]{2,1,0:T(8,128)(2,1)}, bf16[4,8,32,512]{3,2,1,0:T(8,128)(2,1)}) custom-call(bf16[4,64,1024]{2,1,0:T(8,128)(2,1)} %bitcast.11, bf16[16,2,4,64,128]{4,3,2,1,0:T(8,128)(2,1)} %bitcast.12, s32[8,128]{1,0:T(8,128)} %get-tuple-element.9.picks_hbm, bf16[4,64,1024]{2,1,0:T(8,128)(2,1)} %get-tuple-element.10.pre_ref, ...), custom_call_target="tpu_custom_call" | custom-call | tf_op jit(solution)/shard_map/finish/pallas_call | solution.py:769

commit v10 on v9

--- a/solution.py
+++ b/solution.py
@@ -29,16 +29,17 @@
 
 
 ORDER = (
-    "p0.other", "p1.other", "p2.other", "p0.own", "all.pick", "kv.r", "kv.l", "kv.z", "p1.own",
-    "all.sq", "p0.xr2", "p0.xr0", "p2.own", "p3.other", "kv.f", "p1.xr0", "p1.xr2", "all.sq1",
-    "p3.own", "p2.xr0", "kv.s", "p2.xr2", "kv.m", "p0.xsum", "all.sq2", "kv.o", "all.mask",
-    "p3.xr2", "p1.xsum", "kv.fin", "p3.xr0", "p2.xsum", "p0.att", "p1.att", "p3.xsum", "p2.att",
-    "p0.hz", "p1.hz", "p3.att", "p0.hl", "p0.hr", "p2.hz", "p1.hl", "all.list", "p3.hz",
-    "p0.hf", "p1.hr", "p2.hl", "p2.hr", "p0.out", "p3.hr", "p3.hl", "p1.hf", "all.pf0", "p2.hf",
-    "p0.yr0", "p0.yr2", "p3.hf", "p1.out", "p3.out", "p2.out", "p1.yr2", "p1.yr0", "p0.ysum",
-    "p3.yr2", "p3.yr0", "p2.yr0", "p2.yr2", "all.pf1", "p1.ysum", "all.pf2", "p3.ysum",
-    "p0.add", "p2.ysum", "p1.add", "p3.add", "p2.add", "p0.f2", "all.pf3", "p0.f1", "p1.f1",
-    "p1.f2", "p3.f1", "p3.f2", "p2.f1", "p2.f2", "p1.f5", "p0.f5", "p3.f5", "p2.f5",
+    "p0.other", "p1.other", "p2.other", "all.sq", "kv.r", "p0.own", "all.pick", "p3.other",
+    "kv.l", "p1.own", "p0.xr2", "p0.xr0", "all.sq1", "kv.f", "p2.own", "p3.own", "p1.xr0",
+    "all.sq2", "p1.xr2", "p0.xsum", "kv.m", "all.mask", "p2.xr2", "kv.z", "p2.xr0", "kv.o",
+    "p3.xr2", "kv.s", "p3.xr0", "p1.xsum", "all.list", "kv.fin", "p0.att", "p2.xsum", "p1.att",
+    "p3.xsum", "p0.hz", "p2.att", "p1.hz", "p0.hl", "p0.hr", "p3.att", "p2.hz", "p1.hl",
+    "p1.hr", "all.pf0", "p0.hf", "p3.hz", "p2.hr", "p2.hl", "p1.hf", "p0.out", "p1.out",
+    "p2.hf", "p3.hl", "p3.hr", "p0.yr2", "p0.yr0", "p2.out", "p3.hf", "p1.yr0", "p1.yr2",
+    "p3.out", "p0.ysum", "p2.yr0", "p2.yr2", "p1.ysum", "p3.yr0", "p3.yr2", "p0.add", "p2.ysum",
+    "p1.add", "p3.ysum", "all.pf1", "p0.f2", "p2.add", "p3.add", "p0.f1", "p1.f2", "p1.f1",
+    "all.pf2", "p2.f2", "p2.f1", "p3.f1", "p3.f2", "all.pf3", "p1.f5", "p0.f5", "p2.f5",
+    "p3.f5",
 )
 
 
@@ -114,27 +115,36 @@
     for dev in (d_xr, d_xl, d_z, d_c, d_yr, d_yl, d_zl, d_xo):
         pl.semaphore_signal(barrier, inc=1, device_id=dev, device_id_type=MESH)
 
-    loads = [
-        pltpu.make_async_copy(key_ref, kv.at[x, core, zh, 0], lsem.at[0]),
-        pltpu.make_async_copy(val_ref, kv.at[x, core, zh, 1], lsem.at[1]),
-        pltpu.make_async_copy(x_ref, xb, lsem.at[2]),
-        pltpu.make_async_copy(wkv_ref, wkvb, lsem.at[3]),
-    ]
+    loads = {}
+
+    def load(name, src, dst):
+        loads[name] = pltpu.make_async_copy(src, dst, lsem.at[len(loads)])
+        loads[name].start()
+
+    waited = set()
+
+    def need(name):
+        if name not in waited:
+            waited.add(name)
+            loads[name].wait()
+
+    load("key", key_ref, kv.at[x, core, zh, 0])
+    load("value", val_ref, kv.at[x, core, zh, 1])
+    load("gain", gain_hbm, gain_ref)
+    load("x0", x_ref.at[0], xb.at[0])
+    load("wkv", wkv_ref, wkvb)
     for j in range(4):
-        loads.append(
-            pltpu.make_async_copy(wq_ref.at[:, pl.ds(256 * j, 256)], wb.at[j], lsem.at[4 + j])
-        )
-    for j in range(2):
-        loads.append(
-            pltpu.make_async_copy(wo_ref.at[:, pl.ds(256 * j, 256)], wob.at[j], lsem.at[8 + j])
-        )
-    for i, (src, dst) in enumerate(
-        ((gain_hbm, gain_ref), (mask_hbm, mask_ref), (pages_hbm, pages_ref), (clen_hbm, clen_ref))
-    ):
-        loads.append(pltpu.make_async_copy(src, dst, lsem.at[11 + i]))
-    loads.append(pltpu.make_async_copy(q_hbm, qb, lsem.at[15 + NCH]))
-    for copy in loads:
-        copy.start()
+        load(f"wq{j}", wq_ref.at[:, pl.ds(256 * j, 256)], wb.at[j])
+    for t in range(1, 4):
+        load(f"x{t}", x_ref.at[t], xb.at[t])
+
+    def load_rest():
+        load("pages", pages_hbm, pages_ref)
+        load("lens", clen_hbm, clen_ref)
+        load("mask", mask_hbm, mask_ref)
+        for j in range(2):
+            load(f"wo{j}", wo_ref.at[:, pl.ds(256 * j, 256)], wob.at[j])
+        load("query", q_hbm, qb)
 
     pl.semaphore_wait(barrier, 8)
 
@@ -157,9 +167,9 @@
 
     def kv_start():
         own = kv.at[x, core, zh]
+        pass_to(kvm, KV0, 0, own, d_z)
         pass_to(kvm, KV0, 1, own, d_xr)
         pass_to(kvm, KV0, 2, own, d_xl)
-        pass_to(kvm, KV0, 0, own, d_z)
 
     def kv_pass(what):
         if what == "l":
@@ -214,12 +224,11 @@
             for k in range(5, 9):
                 self.m[k].wait_recv()
 
-    loads[0].wait()
-    loads[1].wait()
+    need("key")
+    need("value")
     kv_start()
 
-    loads[2].wait()
-    loads[10].wait()
+    need("gain")
     row_id = lax.broadcasted_iota(jnp.int32, (64, 128), 0)
     lane_id = lax.broadcasted_iota(jnp.int32, (64, 128), 1)
     eye = row_id == lane_id
@@ -228,6 +237,8 @@
 
     def scale_rows(p, side):
         steps = pl.ds(p.k * TS, TS)
+        for t in range(p.k * TS, p.k * TS + TS):
+            need(f"x{t}")
 
         def body(i, carry):
             raw = xb[steps, 2 * i + side].astype(F32).reshape(RB, 512)
@@ -263,7 +274,7 @@
 
         rows = xs[k, 1 - core].reshape(8 * RB, 512)
         for j in range(5):
-            res = mdot(rows, wb[j]).astype(BF16)
+            res = mdot(rows, weights(j)).astype(BF16)
             gs[k, 2 * j] = res[:, :128].reshape(4, 2, RB, 128)
             gs[k, 2 * j + 1] = res[:, 128:].reshape(4, 2, RB, 128)
         p.core = send(p.base + M_CORE, gs.at[k], gr.at[k], d_c)
@@ -415,17 +426,22 @@
         else:
             p.fo[5].wait_recv()
             p.fo[6].wait_recv()
-            p.done = pltpu.make_async_copy(ob.at[steps], out.at[steps], lsem.at[15 + p.k])
+            p.done = pltpu.make_async_copy(ob.at[steps], out.at[steps], lsem.at[19 + p.k])
             p.done.start()
 
-    def load_weights():
-        for k in range(3, 8):
-            loads[k].wait()
-        wkvf[...] = wkvb[...].astype(F32)
-        wb[4, :, 0:128] = wkvf[pl.ds(0, 512, stride=2), :].astype(BF16)
-        wb[4, :, 128:256] = wkvf[pl.ds(1, 512, stride=2), :].astype(BF16)
+    def weights(j):
+        if j < 4:
+            need(f"wq{j}")
+        elif "wkv" not in waited:
+            need("wkv")
+            wkvf[...] = wkvb[...].astype(F32)
+            wb[4, :, 0:128] = wkvf[pl.ds(0, 512, stride=2), :].astype(BF16)
+            wb[4, :, 128:256] = wkvf[pl.ds(1, 512, stride=2), :].astype(BF16)
+        return wb[j]
 
     def sum_squares():
+        for t in range(4):
+            need(f"x{t}")
         lax.fori_loop(0, 16, squares, 0, unroll=4)
         return [send(SQ0, sqs.at[1 - core], sqc, d_c)]
 
@@ -458,8 +474,8 @@
         return rdot(pick.astype(BF16), pages_ref[...].astype(BF16))
 
     def pick_pages():
-        loads[12].wait()
-        loads[13].wait()
+        need("pages")
+        need("lens")
         own_pages = own_rows_pages()
         page_id = lax.broadcasted_iota(jnp.int32, (16, 64), 1)
         block_id = lax.broadcasted_iota(jnp.int32, (16, 64), 0)
@@ -475,7 +491,7 @@
         two[...] = jnp.where(column == 0, low, high).astype(jnp.int32)
         paired.start()
 
-    paired = pltpu.make_async_copy(two, two_s, lsem.at[21 + NCH])
+    paired = pltpu.make_async_copy(two, two_s, lsem.at[24 + NCH])
 
     def chosen(b, i):
         return jnp.minimum(jnp.maximum(two_s[b, i], 0), 3)
@@ -506,7 +522,7 @@
         return jnp.concatenate(pages, axis=0)
 
     def list_pages():
-        loads[11].wait()
+        need("mask")
         a_id = lax.broadcasted_iota(jnp.int32, (64, 64), 0)
         b_id = lax.broadcasted_iota(jnp.int32, (64, 64), 1)
         col_id = lax.broadcasted_iota(jnp.int32, (64, 128), 1)
@@ -532,7 +548,7 @@
     def prefill_node(n):
         if n == 0:
             listed.wait()
-            loads[14].wait()
+            need("query")
         pages = []
         for i in range(NEAR):
             spot = jnp.minimum(jnp.maximum(spots[n, i], 0), 63)
@@ -545,15 +561,14 @@
         write_heads(pb, n, mixed)
         prefilled[n].start()
 
-    listed = pltpu.make_async_copy(picks, spots, lsem.at[16 + NCH])
-    told = pltpu.make_async_copy(picks, picks_out, lsem.at[22 + NCH])
+    listed = pltpu.make_async_copy(picks, spots, lsem.at[19 + NCH])
+    told = pltpu.make_async_copy(picks, picks_out, lsem.at[25 + NCH])
     prefilled = [
-        pltpu.make_async_copy(pb.at[n], pout.at[n], lsem.at[17 + NCH + n]) for n in range(4)
+        pltpu.make_async_copy(pb.at[n], pout.at[n], lsem.at[20 + NCH + n]) for n in range(4)
     ]
 
-    keep = pltpu.make_async_copy(kv, kv_out, lsem.at[10])
+    keep = pltpu.make_async_copy(kv, kv_out, lsem.at[18])
     rms, squared = [], []
-    late = [loads[8], loads[9]]
 
     def step(event):
         who, what = event.split(".")
@@ -578,9 +593,9 @@
         p = parts[int(who[1])]
         if what == "other":
             scale_rows(p, 1 - core)
+            other_rows(p)
             if p.k == 0:
-                load_weights()
-            other_rows(p)
+                load_rest()
         elif what == "own":
             scale_rows(p, core)
             own_rows(p)
@@ -596,8 +611,8 @@
         elif what[0] == "h":
             p.hog.take(what[1])
         elif what == "out":
-            while late:
-                late.pop().wait()
+            need("wo0")
+            need("wo1")
             out_rows(p)
         elif what == "ysum":
             drain(10)
@@ -679,7 +694,7 @@
             pltpu.VMEM((NCH, 2, 2, RB, 512), BF16),
             pltpu.VMEM((NCH, 2, 2, RB, 512), BF16),
             pltpu.VMEM((NCH, 2, 2, RB, 512), BF16),
-            pltpu.SemaphoreType.DMA((23 + NCH,)),
+            pltpu.SemaphoreType.DMA((26 + NCH,)),
             pltpu.SemaphoreType.DMA((NMSG,)),
             pltpu.SemaphoreType.DMA((NMSG,)),
         ],

time: 70.7 us -> 70.9 us (level)
  no operation moved by 1% of the time
where the time goes in v10:
time: 70.9 us; the launch traced here: 70.8 us
  Pallas kernels  70.1 us (99%)
    pallas_call x1, Pallas kernels, layer_call(): pl.pallas_call(layer_kernel, out_shape=(jax.ShapeDtypeStruct((4, 2, 2, 2,...  67.7 us
    pallas_call x1, Pallas kernels, finish_call(): pl.pallas_call(finish_kernel, out_shape=(jax.ShapeDtypeStruct((4, PAGE, 1...  2.38 us

profile of v10, /device:TPU:0, one launch (start us, length us, event | category | flops | bytes accessed | tf_op | source)
XLA Modules:
  0.0 70.8 jit_solution(14476782737150972774)
XLA Ops:
  0.6 67.7 %layer.1 = (bf16[4,2,2,2,4,64,128]{6,5,4,3,2,1,0:T(8,128)(2,1)}, s32[8,128]{1,0:T(8,128)}, bf16[4,64,1024]{2,1,0:T(8,128)(2,1)}, bf16[4,8,32,512]{3,2,1,0:T(8,128)(2,1)}) custom-call(bf16[4,64,1024]{2,1,0:T(8,128)(2,1)} %bitcast.10, bf16[4,64,128]{2,1,0:T(8,128)(2,1)} %bitcast.15, bf16[4,64,128]{2,1,0:T(8,128)(2,1)} %bitcast.16, s32[64,64]{1,0:T(8,128)} %mask_hbm.1, ...), custom_call_target="tpu_custom_call" | custom-call | tf_op jit(solution)/shard_map/layer/pallas_call | solution.py:641
  68.4 2.4 %finish.1 = (bf16[4,64,1024]{2,1,0:T(8,128)(2,1)}, bf16[4,8,32,512]{3,2,1,0:T(8,128)(2,1)}) custom-call(bf16[4,64,1024]{2,1,0:T(8,128)(2,1)} %bitcast.11, bf16[16,2,4,64,128]{4,3,2,1,0:T(8,128)(2,1)} %bitcast.12, s32[8,128]{1,0:T(8,128)} %get-tuple-element.9.picks_hbm, bf16[4,64,1024]{2,1,0:T(8,128)(2,1)} %get-tuple-element.10.pre_ref, ...), custom_call_target="tpu_custom_call" | custom-call | tf_op jit(solution)/shard_map/finish/pallas_call | solution.py:784

commit v11 on v10

--- a/solution.py
+++ b/solution.py
@@ -29,17 +29,16 @@
 
 
 ORDER = (
-    "p0.other", "p1.other", "p2.other", "all.sq", "kv.r", "p0.own", "all.pick", "p3.other",
-    "kv.l", "p1.own", "p0.xr2", "p0.xr0", "all.sq1", "kv.f", "p2.own", "p3.own", "p1.xr0",
-    "all.sq2", "p1.xr2", "p0.xsum", "kv.m", "all.mask", "p2.xr2", "kv.z", "p2.xr0", "kv.o",
-    "p3.xr2", "kv.s", "p3.xr0", "p1.xsum", "all.list", "kv.fin", "p0.att", "p2.xsum", "p1.att",
-    "p3.xsum", "p0.hz", "p2.att", "p1.hz", "p0.hl", "p0.hr", "p3.att", "p2.hz", "p1.hl",
-    "p1.hr", "all.pf0", "p0.hf", "p3.hz", "p2.hr", "p2.hl", "p1.hf", "p0.out", "p1.out",
-    "p2.hf", "p3.hl", "p3.hr", "p0.yr2", "p0.yr0", "p2.out", "p3.hf", "p1.yr0", "p1.yr2",
-    "p3.out", "p0.ysum", "p2.yr0", "p2.yr2", "p1.ysum", "p3.yr0", "p3.yr2", "p0.add", "p2.ysum",
-    "p1.add", "p3.ysum", "all.pf1", "p0.f2", "p2.add", "p3.add", "p0.f1", "p1.f2", "p1.f1",
-    "all.pf2", "p2.f2", "p2.f1", "p3.f1", "p3.f2", "all.pf3", "p1.f5", "p0.f5", "p2.f5",
-    "p3.f5",
+    "p0.other", "p1.other", "p2.other", "p0.own", "all.pick", "kv.r", "kv.l", "kv.z", "p1.own",
+    "all.sq", "p0.xr2", "p0.xr0", "p2.own", "p3.other", "kv.f", "p1.xr0", "p1.xr2", "all.sq1",
+    "p3.own", "p2.xr0", "kv.s", "p2.xr2", "kv.m", "p0.xsum", "all.sq2", "kv.o", "all.mask",
+    "p3.xr2", "p1.xsum", "kv.fin", "p3.xr0", "p2.xsum", "p0.att", "p1.att", "p3.xsum", "p2.att",
+    "p0.hz", "p1.hz", "p3.att", "p0.hl", "p0.hr", "p2.hz", "p1.hl", "all.list", "p3.hz",
+    "p0.hf", "p1.hr", "p2.hl", "p2.hr", "p0.out", "p3.hr", "p3.hl", "p1.hf", "all.pf0", "p2.hf",
+    "p0.yr0", "p0.yr2", "p3.hf", "p1.out", "p3.out", "p2.out", "p1.yr2", "p1.yr0", "p0.ysum",
+    "p3.yr2", "p3.yr0", "p2.yr0", "p2.yr2", "all.pf1", "p1.ysum", "all.pf2", "p3.ysum",
+    "p0.add", "p2.ysum", "p1.add", "p3.add", "p2.add", "p0.f2", "all.pf3", "p0.f1", "p1.f1",
+    "p1.f2", "p3.f1", "p3.f2", "p2.f1", "p2.f2", "p1.f5", "p0.f5", "p3.f5", "p2.f5",
 )
 
 

time: 70.9 us -> 70.7 us (level)
  no operation moved by 1% of the time
where the time goes in v11:
time: 70.7 us; the launch traced here: 70.5 us
  Pallas kernels  69.9 us (99%)
    pallas_call x1, Pallas kernels, layer_call(): pl.pallas_call(layer_kernel, out_shape=(jax.ShapeDtypeStruct((4, 2, 2, 2,...  67.5 us
    pallas_call x1, Pallas kernels, finish_call(): pl.pallas_call(finish_kernel, out_shape=(jax.ShapeDtypeStruct((4, PAGE, 1...  2.38 us

profile of v11, /device:TPU:0, one launch (start us, length us, event | category | flops | bytes accessed | tf_op | source)
XLA Modules:
  0.0 70.5 jit_solution(21224547650018666)
XLA Ops:
  0.6 67.5 %layer.1 = (bf16[4,2,2,2,4,64,128]{6,5,4,3,2,1,0:T(8,128)(2,1)}, s32[8,128]{1,0:T(8,128)}, bf16[4,64,1024]{2,1,0:T(8,128)(2,1)}, bf16[4,8,32,512]{3,2,1,0:T(8,128)(2,1)}) custom-call(bf16[4,64,1024]{2,1,0:T(8,128)(2,1)} %bitcast.10, bf16[4,64,128]{2,1,0:T(8,128)(2,1)} %bitcast.15, bf16[4,64,128]{2,1,0:T(8,128)(2,1)} %bitcast.16, s32[64,64]{1,0:T(8,128)} %mask_hbm.1, ...), custom_call_target="tpu_custom_call" | custom-call | tf_op jit(solution)/shard_map/layer/pallas_call | solution.py:640
  68.1 2.4 %finish.1 = (bf16[4,64,1024]{2,1,0:T(8,128)(2,1)}, bf16[4,8,32,512]{3,2,1,0:T(8,128)(2,1)}) custom-call(bf16[4,64,1024]{2,1,0:T(8,128)(2,1)} %bitcast.11, bf16[16,2,4,64,128]{4,3,2,1,0:T(8,128)(2,1)} %bitcast.12, s32[8,128]{1,0:T(8,128)} %get-tuple-element.9.picks_hbm, bf16[4,64,1024]{2,1,0:T(8,128)(2,1)} %get-tuple-element.10.pre_ref, ...), custom_call_target="tpu_custom_call" | custom-call | tf_op jit(solution)/shard_map/finish/pallas_call | solution.py:783

commit v12 on v11

--- a/solution.py
+++ b/solution.py
@@ -614,14 +614,14 @@
             need("wo1")
             out_rows(p)
         elif what == "ysum":
-            drain(10)
+            drain(30)
             y_sum(p)
         elif what[0] == "y":
             y_relay(p, int(what[2]) // 2)
         elif what == "add":
             add_input(p)
         else:
-            drain(6)
+            drain(16)
             pass_on(p, int(what[1]))
 
     for event in ORDER:

time: 70.7 us -> 70.7 us (level)
  no operation moved by 1% of the time
where the time goes in v12:
time: 70.7 us; the launch traced here: 70.5 us
  Pallas kernels  69.9 us (99%)
    pallas_call x1, Pallas kernels, layer_call(): pl.pallas_call(layer_kernel, out_shape=(jax.ShapeDtypeStruct((4, 2, 2, 2,...  67.5 us
    pallas_call x1, Pallas kernels, finish_call(): pl.pallas_call(finish_kernel, out_shape=(jax.ShapeDtypeStruct((4, PAGE, 1...  2.38 us

profile of v12, /device:TPU:0, one launch (start us, length us, event | category | flops | bytes accessed | tf_op | source)
XLA Modules:
  0.0 70.5 jit_solution(4444702359216705062)
XLA Ops:
  0.6 67.5 %layer.1 = (bf16[4,2,2,2,4,64,128]{6,5,4,3,2,1,0:T(8,128)(2,1)}, s32[8,128]{1,0:T(8,128)}, bf16[4,64,1024]{2,1,0:T(8,128)(2,1)}, bf16[4,8,32,512]{3,2,1,0:T(8,128)(2,1)}) custom-call(bf16[4,64,1024]{2,1,0:T(8,128)(2,1)} %bitcast.10, bf16[4,64,128]{2,1,0:T(8,128)(2,1)} %bitcast.15, bf16[4,64,128]{2,1,0:T(8,128)(2,1)} %bitcast.16, s32[64,64]{1,0:T(8,128)} %mask_hbm.1, ...), custom_call_target="tpu_custom_call" | custom-call | tf_op jit(solution)/shard_map/layer/pallas_call | solution.py:640
  68.2 2.4 %finish.1 = (bf16[4,64,1024]{2,1,0:T(8,128)(2,1)}, bf16[4,8,32,512]{3,2,1,0:T(8,128)(2,1)}) custom-call(bf16[4,64,1024]{2,1,0:T(8,128)(2,1)} %bitcast.11, bf16[16,2,4,64,128]{4,3,2,1,0:T(8,128)(2,1)} %bitcast.12, s32[8,128]{1,0:T(8,128)} %get-tuple-element.9.picks_hbm, bf16[4,64,1024]{2,1,0:T(8,128)(2,1)} %get-tuple-element.10.pre_ref, ...), custom_call_target="tpu_custom_call" | custom-call | tf_op jit(solution)/shard_map/finish/pallas_call | solution.py:783
